TPU v7x, 32 devices: a whole 2x2x4 slice. The times are simulated.
32 devices in a mesh: seq: 4 (over y, x), chan: 8 (over z, core).
Axes of the slice: x: 2, y: 2, z: 4, core: 2. Of those that a mesh axis runs over, the one named last changes fastest.
Arguments:
- post_gate: bfloat16 [512, 4096], P('chan', 'seq'), may hold values from -6 to 6
- pre_gate: bfloat16 [512, 4096], P('chan', 'seq'), may hold values from -6 to 6
- signal: bfloat16 [512, 4096], P('chan', 'seq'), may hold values from -6 to 6
- cotangent: bfloat16 [512, 4096], P('chan', 'seq'), may hold values from -6 to 6
- filter_taps: float32 [512, 4096], P('chan', 'seq'), may hold values from -0.09375 to 0.09375
- skip_gain: float32 [512], P('chan'), may hold values from -4 to 4
Outputs:
- output: bfloat16 [512, 4096], P('chan', 'seq')
- d_post: bfloat16 [512, 4096], P('chan', 'seq')
- d_pre: bfloat16 [512, 4096], P('chan', 'seq')
- d_signal: bfloat16 [512, 4096], P('chan', 'seq')
- d_skip: float32 [512], P('chan')
- d_filter: float32 [512, 4096], P('chan', 'seq')
All inputs are finite; a program needn't handle non-finite values.
Results may differ from a plain program's by a relative error of at most 0.004.
Values sent between devices are 32-bit elements; how exact they have to be, the bound alone decides.
No kernel may reach another device: no remote copies, remote signals or barrier semaphores. Data moves between devices by JAX's collectives and lax.ppermute only.
A program may use at most 64 MiB of HBM per device.

v0:
```python
import functools
import math

import jax
import jax.numpy as jnp
import ml_dtypes
import numpy as np
from jax import lax
from jax.experimental import pallas as pl
from jax.experimental.pallas import tpu as pltpu
from jax.sharding import PartitionSpec as P

LANES = 128
SUBLANES = 8
BF16 = jnp.bfloat16
F32 = jnp.float32


def halves(table):
    high = table.astype(np.float32).astype(ml_dtypes.bfloat16)
    low = (table - high.astype(np.float64)).astype(np.float32).astype(ml_dtypes.bfloat16)
    return high, low


def tables(shards_of, total_len):
    blocks = total_len // LANES
    per_shard = blocks // shards_of
    k = np.arange(blocks)[:, None]
    a = np.arange(blocks)[None, :]
    angle = np.pi * (2 * k + 1) * a / (2 * blocks)
    outer = np.concatenate([np.cos(angle), -np.sin(angle)], axis=0)
    inverse = np.concatenate([np.cos(angle).T, -np.sin(angle).T], axis=1) / total_len
    filter_inverse = inverse / math.sqrt(total_len)
    order = [
        np.concatenate(
            [np.arange(per_shard) + (me ^ d) * per_shard for d in range(shards_of)]
        )
        for me in range(shards_of)
    ]

    def wide(table):
        high, low = halves(table)
        return np.concatenate([high, high, low], axis=1)

    outer_w = np.stack([wide(outer[:, o]) for o in order])
    inverse_w = np.stack([wide(inverse[o]) for o in order])
    filter_w = np.stack([wide(filter_inverse[o]) for o in order])
    b = np.arange(LANES)[None, :]
    turn = np.pi * (2 * k + 1) * b / (2 * total_len)
    twiddle = np.stack([np.cos(turn), np.sin(turn)]).astype(np.float32)
    q = np.arange(LANES)
    inner = 2 * np.pi * (q[:, None] * q[None, :] % LANES) / LANES
    dft = np.block([[np.cos(inner), -np.sin(inner)], [np.sin(inner), np.cos(inner)]])
    dft_high, dft_low = halves(dft)
    return outer_w, inverse_w, filter_w, twiddle, np.stack([dft_high, dft_low])


def split(x):
    high = x.astype(BF16)
    low = (x - high.astype(F32)).astype(BF16)
    return high, low


def outer_mix(table, x):
    high, low = split(x)
    return jnp.dot(table, jnp.concatenate([high, low, high], axis=0), preferred_element_type=F32)


def inner_mix(x, dft_ref):
    high, low = split(x)
    return (
        jnp.dot(high, dft_ref[0], preferred_element_type=F32)
        + jnp.dot(low, dft_ref[0], preferred_element_type=F32)
        + jnp.dot(high, dft_ref[1], preferred_element_type=F32)
    )


def pack_kernel(shards_of, post, pre, signal, cotangent, taps, *outs):
    me = lax.axis_index("seq")
    channels, length = post.shape
    group = channels // shards_of
    per = length // LANES
    field_rows = group * per
    for d in range(shards_of):
        rows = pl.ds(pl.multiple_of((me ^ d) * group, group), group)
        gated = pre[rows, :].astype(F32) * signal[rows, :].astype(F32)
        d_conved = cotangent[rows, :].astype(F32) * post[rows, :].astype(F32)
        for f, x in enumerate((taps[rows, :], gated, d_conved)):
            for cb in range(group // SUBLANES):
                for a in range(per):
                    start = f * field_rows + cb * SUBLANES * per + a
                    outs[d][pl.ds(start, SUBLANES, stride=per), :] = x[
                        cb * SUBLANES : (cb + 1) * SUBLANES, a * LANES : (a + 1) * LANES
                    ]
    parts = []
    for cb in range(0, channels, 16):
        prod = (pre[cb : cb + 16, :].astype(F32) * signal[cb : cb + 16, :].astype(F32)) * (
            cotangent[cb : cb + 16, :].astype(F32) * post[cb : cb + 16, :].astype(F32)
        )
        parts.append(sum(prod[:, a * LANES : (a + 1) * LANES] for a in range(per)))
    folded = jnp.concatenate(parts + [jnp.zeros((LANES - channels, LANES), F32)], axis=0)
    skip = jnp.sum(folded.T, axis=0, keepdims=True)
    for d in range(shards_of):
        outs[d][3 * field_rows :, :] = jnp.broadcast_to(skip, (SUBLANES, LANES))


def spectral_kernel(shards_of, group, per, *refs):
    skip_gain, outer_w, inverse_w, filter_w, twiddle, dft = refs[:6]
    pieces = refs[6 : 6 + shards_of]
    outs = refs[6 + shards_of : 6 + 2 * shards_of]
    d_skip = refs[6 + 2 * shards_of]
    spectra = refs[7 + 2 * shards_of :]
    me = lax.axis_index("seq")
    blocks = shards_of * per
    field_rows = group * per
    cos_t = twiddle[0]
    sin_t = twiddle[1]
    forward = outer_w[me]
    first = (lax.broadcasted_iota(jnp.int32, (per, LANES), 0) == 0) & (
        lax.broadcasted_iota(jnp.int32, (per, LANES), 1) == 0
    )
    total_len = blocks * LANES
    skips = sum(pieces[d][3 * field_rows : 3 * field_rows + 1, :] for d in range(shards_of))
    d_skip[...] = skips[:, : d_skip.shape[1]] * (1.0 / math.sqrt(total_len))

    for f in range(3):
        for c in range(0, group, 2):
            cols = []
            for ch in (c, c + 1):
                start = f * field_rows + ch * per
                cols.append(
                    jnp.concatenate([pieces[d][start : start + per, :] for d in range(shards_of)], axis=0)
                )
            mixed = outer_mix(forward, jnp.concatenate(cols, axis=1))
            for i in range(2):
                real = mixed[:blocks, i * LANES : (i + 1) * LANES]
                imag = mixed[blocks:, i * LANES : (i + 1) * LANES]
                row = jnp.concatenate(
                    [real * cos_t + imag * sin_t, imag * cos_t - real * sin_t], axis=1
                )
                spectra[f][pl.ds((c + i) * blocks, blocks), :] = inner_mix(row, dft)
    back = inverse_w[me]
    filter_back = filter_w[me]
    for c in range(0, group, 2):
        pairs = [[], [], []]
        for ch in (c, c + 1):
            rows = pl.ds(ch * blocks, blocks)
            tr, ti = spectra[0][rows, :LANES], spectra[0][rows, LANES:]
            gr, gi = spectra[1][rows, :LANES], spectra[1][rows, LANES:]
            dr, di = spectra[2][rows, :LANES], spectra[2][rows, LANES:]
            tr = tr + skip_gain[me * group + ch]
            products = (
                (gr * tr - gi * ti, gr * ti + gi * tr),
                (tr * dr + ti * di, tr * di - ti * dr),
                (gr * dr + gi * di, gr * di - gi * dr),
            )
            for f in range(3):
                real, imag = products[f]
                swapped = inner_mix(jnp.concatenate([imag, real], axis=1), dft)
                imag, real = swapped[:, :LANES], swapped[:, LANES:]
                pairs[f].append(
                    jnp.concatenate(
                        [real * cos_t - imag * sin_t, imag * cos_t + real * sin_t], axis=0
                    )
                )
        for f in range(3):
            y = outer_mix(filter_back if f == 2 else back, jnp.concatenate(pairs[f], axis=1))
            for i in range(2):
                start = f * field_rows + (c + i) * per
                for d in range(shards_of):
                    outs[d][start : start + per, :] = y[
                        d * per : (d + 1) * per, i * LANES : (i + 1) * LANES
                    ]


def gate_kernel(shards_of, *refs):
    post, pre, signal, cotangent = refs[:4]
    pieces = refs[4 : 4 + shards_of]
    output, d_post, d_pre, d_signal, d_filter = refs[4 + shards_of :]
    me = lax.axis_index("seq")
    channels, length = post.shape
    group = channels // shards_of
    per = length // LANES
    field_rows = group * per
    for d in range(shards_of):
        rows = pl.ds(pl.multiple_of((me ^ d) * group, group), group)
        for a in range(per):
            cols = slice(a * LANES, (a + 1) * LANES)

            def field(f):
                return jnp.concatenate(
                    [
                        pieces[d][pl.ds(f * field_rows + cb * per + a, SUBLANES, stride=per), :]
                        for cb in range(0, group, SUBLANES)
                    ],
                    axis=0,
                )

            conved, d_gated = field(0), field(1)
            output[rows, cols] = (post[rows, cols].astype(F32) * conved).astype(BF16)
            d_post[rows, cols] = (cotangent[rows, cols].astype(F32) * conved).astype(BF16)
            d_pre[rows, cols] = (signal[rows, cols].astype(F32) * d_gated).astype(BF16)
            d_signal[rows, cols] = (pre[rows, cols].astype(F32) * d_gated).astype(BF16)
            d_filter[rows, cols] = field(2)


def shards(post_gate, pre_gate, signal, cotangent, filter_taps, skip_gain):
    shards_of = lax.axis_size("seq")
    channels, length = post_gate.shape
    group = channels // shards_of
    per = length // LANES
    field_rows = group * per
    total_len = shards_of * length
    vmem = pl.BlockSpec(memory_space=pltpu.VMEM)
    params = pltpu.CompilerParams(vmem_limit_bytes=48 * 2**20)

    def swap(pieces):
        return [pieces[0]] + [
            lax.ppermute(pieces[d], "seq", [(i, i ^ d) for i in range(shards_of)])
            for d in range(1, shards_of)
        ]

    packed = pl.pallas_call(
        functools.partial(pack_kernel, shards_of),
        out_shape=[jax.ShapeDtypeStruct((3 * field_rows + SUBLANES, LANES), F32)] * shards_of,
        in_specs=[vmem] * 5,
        out_specs=[vmem] * shards_of,
        compiler_params=params,
    )(post_gate, pre_gate, signal, cotangent, filter_taps)
    packed = swap(packed)
    consts = [jnp.asarray(t) for t in tables(shards_of, total_len)]
    *mixed, d_skip = pl.pallas_call(
        functools.partial(spectral_kernel, shards_of, group, per),
        out_shape=[jax.ShapeDtypeStruct((3 * field_rows, LANES), F32)] * shards_of
        + [jax.ShapeDtypeStruct((1, channels), F32)],
        in_specs=[pl.BlockSpec(memory_space=pltpu.SMEM)] + [vmem] * (5 + shards_of),
        out_specs=[vmem] * (shards_of + 1),
        scratch_shapes=[pltpu.VMEM((group * shards_of * per, 2 * LANES), F32)] * 3,
        compiler_params=params,
    )(skip_gain, *consts, *packed)
    mixed = swap(mixed)
    wide = jax.ShapeDtypeStruct((channels, length), BF16)
    output, d_post, d_pre, d_signal, d_filter = pl.pallas_call(
        functools.partial(gate_kernel, shards_of),
        out_shape=[wide] * 4 + [jax.ShapeDtypeStruct((channels, length), F32)],
        in_specs=[vmem] * (4 + shards_of),
        out_specs=[vmem] * 5,
        compiler_params=params,
    )(post_gate, pre_gate, signal, cotangent, *mixed)
    return (output, d_post, d_pre, d_signal, d_skip.reshape(channels), d_filter)


def solution(mesh):
    both = P("chan", "seq")
    return jax.shard_map(
        shards,
        mesh=mesh,
        in_specs=(both,) * 5 + (P("chan"),),
        out_specs=(both,) * 4 + (P("chan"), both),
        check_vma=False,
    )
```

profile of v0, /device:TPU:0, one launch (start us, length us, event | category | flops | bytes accessed | tf_op | source)
XLA Modules:
  0.0 42.6 jit_solution(1418733284346125335)
XLA Ops:
  0.6 0.0 copy-start
  0.6 0.9 %copy-done = bf16[64,1024]{1,0:T(8,128)(2,1)S(1)} copy-done((bf16[64,1024]{1,0:T(8,128)(2,1)S(1)}, bf16[64,1024]{1,0:T(8,128)(2,1)}, u32[]{:S(2)}) %copy-start) | copy-done | bytes 131096
  1.5 0.0 copy-start.2
  1.5 0.9 %copy-done.2 = bf16[64,1024]{1,0:T(8,128)(2,1)S(1)} copy-done((bf16[64,1024]{1,0:T(8,128)(2,1)S(1)}, bf16[64,1024]{1,0:T(8,128)(2,1)}, u32[]{:S(2)}) %copy-start.2) | copy-done | bytes 131096
  2.4 0.0 copy-start.4
  2.4 0.9 %copy-done.4 = bf16[64,1024]{1,0:T(8,128)(2,1)S(1)} copy-done((bf16[64,1024]{1,0:T(8,128)(2,1)S(1)}, bf16[64,1024]{1,0:T(8,128)(2,1)}, u32[]{:S(2)}) %copy-start.4) | copy-done | bytes 131096
  3.3 0.0 copy-start.6
  3.4 0.9 %copy-done.6 = bf16[64,1024]{1,0:T(8,128)(2,1)S(1)} copy-done((bf16[64,1024]{1,0:T(8,128)(2,1)S(1)}, bf16[64,1024]{1,0:T(8,128)(2,1)}, u32[]{:S(2)}) %copy-start.6) | copy-done | bytes 131096
  4.3 0.0 copy-start.8
  4.3 0.9 %copy-done.8 = f32[64,1024]{1,0:T(8,128)S(1)} copy-done((f32[64,1024]{1,0:T(8,128)S(1)}, f32[64,1024]{1,0:T(8,128)}, u32[]{:S(2)}) %copy-start.8) | copy-done | bytes 262168
  5.2 0.0 copy-start.9
  5.2 0.0 copy-start.10
  5.2 0.0 copy-start.11
  5.2 0.0 copy-start.12
  5.2 0.0 copy-start.13
  5.2 0.2 shard_map.154
  5.4 3.0 %collective-permute-start = (f32[392,128]{1,0:T(8,128)S(1)}, f32[392,128]{1,0:T(8,128)S(1)}, u32[]{:S(2)}, u32[]{:S(2)}) collective-permute-start(f32[392,128]{1,0:T(8,128)S(1)} %get-tuple-element.21), channel_id=1, source_target_pairs={{0,8},{8,0},{16,24},{24,16},{1,9},{9,1},{17,25},{25,17},{2,10},{10... | collective-permute-start | bytes 602120 | tf_op jit(solution)/shard_map/ppermute | solution.py:219
  8.4 1.5 %collective-permute-start.1 = (f32[392,128]{1,0:T(8,128)S(1)}, f32[392,128]{1,0:T(8,128)S(1)}, u32[]{:S(2)}, u32[]{:S(2)}) collective-permute-start(f32[392,128]{1,0:T(8,128)S(1)} %get-tuple-element.22), channel_id=1, source_target_pairs={{0,16},{8,24},{16,0},{24,8},{1,17},{9,25},{17,1},{25,9},{2,18},{10... | collective-permute-start | bytes 602120 | tf_op jit(solution)/shard_map/ppermute | solution.py:219
  10.0 0.0 copy-start.14
  10.0 0.0 collective-permute-start.2
  10.0 4.3 %collective-permute-done.refs_7_ = f32[392,128]{1,0:T(8,128)S(1)} collective-permute-done((f32[392,128]{1,0:T(8,128)S(1)}, f32[392,128]{1,0:T(8,128)S(1)}, u32[]{:S(2)}, u32[]{:S(2)}) %collective-permute-start) | collective-permute-done | bytes 200736 | tf_op jit(solution)/shard_map/ppermute | solution.py:219
  14.3 4.9 %collective-permute-done.1.refs_8_ = f32[392,128]{1,0:T(8,128)S(1)} collective-permute-done((f32[392,128]{1,0:T(8,128)S(1)}, f32[392,128]{1,0:T(8,128)S(1)}, u32[]{:S(2)}, u32[]{:S(2)}) %collective-permute-start.1) | collective-permute-done | bytes 200736 | tf_op jit(solution)/shard_map/ppermute | solution.py:219
  19.2 0.0 collective-permute-done.2.refs_9_
  19.2 0.0 copy-done.9
  19.2 0.0 copy-done.10
  19.2 0.0 copy-done.11
  19.2 0.0 copy-done.12
  19.2 0.0 copy-done.13
  19.2 0.0 copy-done.14
  19.2 0.0 copy-start.1
  19.3 0.0 copy-start.3
  19.3 0.0 copy-start.5
  19.3 0.0 copy-start.7
  19.3 11.3 %shard_map.155 = (f32[384,128]{1,0:T(8,128)S(1)}, f32[384,128]{1,0:T(8,128)S(1)}, f32[384,128]{1,0:T(8,128)S(1)}, f32[384,128]{1,0:T(8,128)S(1)}, f32[1,64]{1,0:T(1,128)}) custom-call(f32[64]{0:T(128)S(1)} %copy-done.14, bf16[4,64,96]{2,1,0:T(8,128)(2,1)S(1)} %copy-done.12, bf16[4,32,192]{2,1,0:T(8,128)(2,1)S(1)} %copy-done.11, ...), custom_call_target="tpu_custom_call" | custom-call | tf_op jit(solution)/shard_map/pallas_call | solution.py:232
  30.6 1.2 %collective-permute-start.3 = (f32[384,128]{1,0:T(8,128)S(1)}, f32[384,128]{1,0:T(8,128)S(1)}, u32[]{:S(2)}, u32[]{:S(2)}) collective-permute-start(f32[384,128]{1,0:T(8,128)S(1)} %get-tuple-element.25), channel_id=1, source_target_pairs={{0,8},{8,0},{16,24},{24,16},{1,9},{9,1},{17,25},{25,17},{2,10},{10... | collective-permute-start | bytes 589832 | tf_op jit(solution)/shard_map/ppermute | solution.py:219
  31.8 0.8 %collective-permute-start.4 = (f32[384,128]{1,0:T(8,128)S(1)}, f32[384,128]{1,0:T(8,128)S(1)}, u32[]{:S(2)}, u32[]{:S(2)}) collective-permute-start(f32[384,128]{1,0:T(8,128)S(1)} %get-tuple-element.26), channel_id=1, source_target_pairs={{0,16},{8,24},{16,0},{24,8},{1,17},{9,25},{17,1},{25,9},{2,18},{10... | collective-permute-start | bytes 589832 | tf_op jit(solution)/shard_map/ppermute | solution.py:219
  32.7 1.4 %collective-permute-start.5 = (f32[384,128]{1,0:T(8,128)S(1)}, f32[384,128]{1,0:T(8,128)S(1)}, u32[]{:S(2)}, u32[]{:S(2)}) collective-permute-start(f32[384,128]{1,0:T(8,128)S(1)} %get-tuple-element.27), channel_id=1, source_target_pairs={{0,24},{8,16},{16,8},{24,0},{1,25},{9,17},{17,9},{25,1},{2,26},{10... | collective-permute-start | bytes 589832 | tf_op jit(solution)/shard_map/ppermute | solution.py:219
  34.1 4.2 %collective-permute-done.3.refs_5_ = f32[384,128]{1,0:T(8,128)S(1)} collective-permute-done((f32[384,128]{1,0:T(8,128)S(1)}, f32[384,128]{1,0:T(8,128)S(1)}, u32[]{:S(2)}, u32[]{:S(2)}) %collective-permute-start.3) | collective-permute-done | bytes 196640 | tf_op jit(solution)/shard_map/ppermute | solution.py:219
  38.3 3.3 %collective-permute-done.4.refs_6_ = f32[384,128]{1,0:T(8,128)S(1)} collective-permute-done((f32[384,128]{1,0:T(8,128)S(1)}, f32[384,128]{1,0:T(8,128)S(1)}, u32[]{:S(2)}, u32[]{:S(2)}) %collective-permute-start.4) | collective-permute-done | bytes 196640 | tf_op jit(solution)/shard_map/ppermute | solution.py:219
  41.5 0.0 collective-permute-done.5.refs_7_
  41.5 0.0 copy-done.1
  41.5 0.0 copy-done.3
  41.5 0.0 copy-done.5
  41.6 0.0 copy-done.7
  41.6 1.1 %shard_map.156 = (bf16[64,1024]{1,0:T(8,128)(2,1)}, bf16[64,1024]{1,0:T(8,128)(2,1)}, bf16[64,1024]{1,0:T(8,128)(2,1)}, bf16[64,1024]{1,0:T(8,128)(2,1)}, f32[64,1024]{1,0:T(8,128)}) custom-call(bf16[64,1024]{1,0:T(8,128)(2,1)S(1)} %copy-done.1, bf16[64,1024]{1,0:T(8,128)(2,1)S(1)} %copy-done.3, bf16[64,1024]{1,0:T(8,128)(2,1)S(1)} %copy-done.5, ...), custom_call_target="tpu_custom_call" | custom-call | tf_op jit(solution)/shard_map/pallas_call | solution.py:243
Async XLA Ops:
  0.6 0.9 %copy-start = (bf16[64,1024]{1,0:T(8,128)(2,1)S(1)}, bf16[64,1024]{1,0:T(8,128)(2,1)}, u32[]{:S(2)}) copy-start(bf16[64,1024]{1,0:T(8,128)(2,1)} %refs_0_.3) | copy-start | bytes 393220
  1.5 0.9 %copy-start.2 = (bf16[64,1024]{1,0:T(8,128)(2,1)S(1)}, bf16[64,1024]{1,0:T(8,128)(2,1)}, u32[]{:S(2)}) copy-start(bf16[64,1024]{1,0:T(8,128)(2,1)} %refs_1_.2) | copy-start | bytes 393220
  2.4 0.9 %copy-start.4 = (bf16[64,1024]{1,0:T(8,128)(2,1)S(1)}, bf16[64,1024]{1,0:T(8,128)(2,1)}, u32[]{:S(2)}) copy-start(bf16[64,1024]{1,0:T(8,128)(2,1)} %refs_2_.2) | copy-start | bytes 393220
  3.3 0.9 %copy-start.6 = (bf16[64,1024]{1,0:T(8,128)(2,1)S(1)}, bf16[64,1024]{1,0:T(8,128)(2,1)}, u32[]{:S(2)}) copy-start(bf16[64,1024]{1,0:T(8,128)(2,1)} %refs_3_.2) | copy-start | bytes 393220
  4.3 0.9 %copy-start.8 = (f32[64,1024]{1,0:T(8,128)S(1)}, f32[64,1024]{1,0:T(8,128)}, u32[]{:S(2)}) copy-start(f32[64,1024]{1,0:T(8,128)} %taps.1) | copy-start | bytes 786436
  5.2 14.0 %copy-start.9 = (bf16[2,256,256]{2,1,0:T(8,128)(2,1)S(1)}, bf16[2,256,256]{2,1,0:T(8,128)(2,1)}, u32[]{:S(2)}) copy-start(bf16[2,256,256]{2,1,0:T(8,128)(2,1)} %constant.14.clone.refs_5_) | copy-start | bytes 786436
  5.2 14.0 %copy-start.10 = (bf16[4,32,192]{2,1,0:T(8,128)(2,1)S(1)}, bf16[4,32,192]{2,1,0:T(8,128)(2,1)}, u32[]{:S(2)}) copy-start(bf16[4,32,192]{2,1,0:T(8,128)(2,1)} %constant.12.clone.refs_3_) | copy-start | bytes 147460
  5.2 14.0 %copy-start.11 = (bf16[4,32,192]{2,1,0:T(8,128)(2,1)S(1)}, bf16[4,32,192]{2,1,0:T(8,128)(2,1)}, u32[]{:S(2)}) copy-start(bf16[4,32,192]{2,1,0:T(8,128)(2,1)} %constant.11.clone.refs_2_) | copy-start | bytes 147460
  5.2 14.0 %copy-start.12 = (bf16[4,64,96]{2,1,0:T(8,128)(2,1)S(1)}, bf16[4,64,96]{2,1,0:T(8,128)(2,1)}, u32[]{:S(2)}) copy-start(bf16[4,64,96]{2,1,0:T(8,128)(2,1)} %constant.10.clone.refs_1_) | copy-start | bytes 147460
  5.2 14.0 %copy-start.13 = (f32[2,32,128]{2,1,0:T(8,128)S(1)}, f32[2,32,128]{2,1,0:T(8,128)}, u32[]{:S(2)}) copy-start(f32[2,32,128]{2,1,0:T(8,128)} %constant.13.clone.refs_4_) | copy-start | bytes 98308
  5.4 8.8 %collective-permute-start = (f32[392,128]{1,0:T(8,128)S(1)}, f32[392,128]{1,0:T(8,128)S(1)}, u32[]{:S(2)}, u32[]{:S(2)}) collective-permute-start(f32[392,128]{1,0:T(8,128)S(1)} %get-tuple-element.21), channel_id=1, source_target_pairs={{0,8},{8,0},{16,24},{24,16},{1,9},{9,1},{17,25},{25,17},{2,10},{10... | collective-permute-start | bytes 602120 | tf_op jit(solution)/shard_map/ppermute | solution.py:219
  8.4 10.8 %collective-permute-start.1 = (f32[392,128]{1,0:T(8,128)S(1)}, f32[392,128]{1,0:T(8,128)S(1)}, u32[]{:S(2)}, u32[]{:S(2)}) collective-permute-start(f32[392,128]{1,0:T(8,128)S(1)} %get-tuple-element.22), channel_id=1, source_target_pairs={{0,16},{8,24},{16,0},{24,8},{1,17},{9,25},{17,1},{25,9},{2,18},{10... | collective-permute-start | bytes 602120 | tf_op jit(solution)/shard_map/ppermute | solution.py:219
  10.0 9.3 %copy-start.14 = (f32[64]{0:T(128)S(1)}, f32[64]{0:T(128)}, u32[]{:S(2)}) copy-start(f32[64]{0:T(128)} %refs_0_.2) | copy-start | bytes 772
  10.0 9.2 %collective-permute-start.2 = (f32[392,128]{1,0:T(8,128)S(1)}, f32[392,128]{1,0:T(8,128)S(1)}, u32[]{:S(2)}, u32[]{:S(2)}) collective-permute-start(f32[392,128]{1,0:T(8,128)S(1)} %get-tuple-element.23), channel_id=1, source_target_pairs={{0,24},{8,16},{16,8},{24,0},{1,25},{9,17},{17,9},{25,1},{2,26},{10... | collective-permute-start | bytes 602120 | tf_op jit(solution)/shard_map/ppermute | solution.py:219
  19.2 22.3 %copy-start.1 = (bf16[64,1024]{1,0:T(8,128)(2,1)S(1)}, bf16[64,1024]{1,0:T(8,128)(2,1)}, u32[]{:S(2)}) copy-start(bf16[64,1024]{1,0:T(8,128)(2,1)} %refs_0_.3) | copy-start | bytes 393220
  19.3 22.3 %copy-start.3 = (bf16[64,1024]{1,0:T(8,128)(2,1)S(1)}, bf16[64,1024]{1,0:T(8,128)(2,1)}, u32[]{:S(2)}) copy-start(bf16[64,1024]{1,0:T(8,128)(2,1)} %refs_1_.2) | copy-start | bytes 393220
  19.3 22.3 %copy-start.5 = (bf16[64,1024]{1,0:T(8,128)(2,1)S(1)}, bf16[64,1024]{1,0:T(8,128)(2,1)}, u32[]{:S(2)}) copy-start(bf16[64,1024]{1,0:T(8,128)(2,1)} %refs_2_.2) | copy-start | bytes 393220
  19.3 22.3 %copy-start.7 = (bf16[64,1024]{1,0:T(8,128)(2,1)S(1)}, bf16[64,1024]{1,0:T(8,128)(2,1)}, u32[]{:S(2)}) copy-start(bf16[64,1024]{1,0:T(8,128)(2,1)} %refs_3_.2) | copy-start | bytes 393220
  30.6 7.7 %collective-permute-start.3 = (f32[384,128]{1,0:T(8,128)S(1)}, f32[384,128]{1,0:T(8,128)S(1)}, u32[]{:S(2)}, u32[]{:S(2)}) collective-permute-start(f32[384,128]{1,0:T(8,128)S(1)} %get-tuple-element.25), channel_id=1, source_target_pairs={{0,8},{8,0},{16,24},{24,16},{1,9},{9,1},{17,25},{25,17},{2,10},{10... | collective-permute-start | bytes 589832 | tf_op jit(solution)/shard_map/ppermute | solution.py:219
  31.8 9.7 %collective-permute-start.4 = (f32[384,128]{1,0:T(8,128)S(1)}, f32[384,128]{1,0:T(8,128)S(1)}, u32[]{:S(2)}, u32[]{:S(2)}) collective-permute-start(f32[384,128]{1,0:T(8,128)S(1)} %get-tuple-element.26), channel_id=1, source_target_pairs={{0,16},{8,24},{16,0},{24,8},{1,17},{9,25},{17,1},{25,9},{2,18},{10... | collective-permute-start | bytes 589832 | tf_op jit(solution)/shard_map/ppermute | solution.py:219
  32.7 8.9 %collective-permute-start.5 = (f32[384,128]{1,0:T(8,128)S(1)}, f32[384,128]{1,0:T(8,128)S(1)}, u32[]{:S(2)}, u32[]{:S(2)}) collective-permute-start(f32[384,128]{1,0:T(8,128)S(1)} %get-tuple-element.27), channel_id=1, source_target_pairs={{0,24},{8,16},{16,8},{24,0},{1,25},{9,17},{17,9},{25,1},{2,26},{10... | collective-permute-start | bytes 589832 | tf_op jit(solution)/shard_map/ppermute | solution.py:219
where the time goes:
time: 42.8 us; the launch traced here: 42.6 us
  waiting for transfers between devices  16.7 us (39%)
  Pallas kernels  12.6 us (29%)
  starting transfers between devices  8.03 us (19%)
  local copies, waits for them, and re-layouts  4.61 us (11%)
  between operations  0.75 us (2%)
    ppermute x6, waiting for transfers between devices, swap(): lax.ppermute(pieces[d], 'seq', [(i, i ^ d) for i in range(shards_of)])  16.7 us
    pallas_call x1, Pallas kernels, shards(): pl.pallas_call(functools.partial(spectral_kernel, shards_of, group, per),...  11.3 us
    ppermute x6, starting transfers between devices, swap(): lax.ppermute(pieces[d], 'seq', [(i, i ^ d) for i in range(shards_of)])  8.03 us
    unnamed x30, local copies, waits for them, and re-layouts  4.61 us
    pallas_call x1, Pallas kernels, shards(): pl.pallas_call(functools.partial(gate_kernel, shards_of), out_shape=[wide...  1.06 us
  transfers between devices with their start and end apart: 6, of which 4 were waited for; matrix products, arithmetic and copies ran while one was open for 0% of the time, Pallas kernels for 0%

commit v1 on v0

v1 whole, which is shorter than its diff:
```python
import functools
import math

import jax
import jax.numpy as jnp
import ml_dtypes
import numpy as np
from jax import lax
from jax.experimental import pallas as pl
from jax.experimental.pallas import tpu as pltpu
from jax.sharding import PartitionSpec as P

LANES = 128
CHUNKS = 1
SUBLANES = 8
BF16 = jnp.bfloat16
F32 = jnp.float32


def halves(table):
    high = table.astype(np.float32).astype(ml_dtypes.bfloat16)
    low = (table - high.astype(np.float64)).astype(np.float32).astype(ml_dtypes.bfloat16)
    return high, low


def tables(shards_of, total_len):
    blocks = total_len // LANES
    per_shard = blocks // shards_of
    k = np.arange(blocks)[:, None]
    a = np.arange(blocks)[None, :]
    angle = np.pi * (2 * k + 1) * a / (2 * blocks)
    outer = np.concatenate([np.cos(angle), -np.sin(angle)], axis=0)
    inverse = np.concatenate([np.cos(angle).T, -np.sin(angle).T], axis=1) / total_len
    filter_inverse = inverse / math.sqrt(total_len)
    order = [
        np.concatenate(
            [np.arange(per_shard) + (me ^ d) * per_shard for d in range(shards_of)]
        )
        for me in range(shards_of)
    ]

    def wide(table):
        high, low = halves(table)
        return np.concatenate([high, high, low], axis=1)

    outer_w = np.stack([wide(outer[:, o]) for o in order])
    inverse_w = np.stack([wide(inverse[o]) for o in order])
    filter_w = np.stack([wide(filter_inverse[o]) for o in order])
    b = np.arange(LANES)[None, :]
    turn = np.pi * (2 * k + 1) * b / (2 * total_len)
    twiddle = np.stack([np.cos(turn), np.sin(turn)]).astype(np.float32)
    q = np.arange(LANES)
    inner = 2 * np.pi * (q[:, None] * q[None, :] % LANES) / LANES
    dft = np.block([[np.cos(inner), -np.sin(inner)], [np.sin(inner), np.cos(inner)]])
    dft_high, dft_low = halves(dft)
    return outer_w, inverse_w, filter_w, twiddle, np.concatenate([dft_high, dft_high, dft_low])


def split(x):
    high = x.astype(BF16)
    low = (x - high.astype(F32)).astype(BF16)
    return high, low


def outer_mix(table, x):
    high, low = split(x)
    return jnp.dot(table, jnp.concatenate([high, low, high], axis=0), preferred_element_type=F32)


def triple(x):
    high, low = split(x)
    return jnp.concatenate([high, low, high], axis=1)


def group_rows(ref, index, group):
    if group % 16 == 0:
        return ref[pl.ds(pl.multiple_of(index * group, 16), group), :].astype(F32)
    pair = ref[pl.ds(pl.multiple_of(index // 2 * 16, 16), 16), :].astype(F32)
    return jnp.where(index % 2 == 0, pair[:SUBLANES], pair[SUBLANES:])


def pack_kernel(shards_of, chunks, *refs):
    sources = refs[:5]
    outs = refs[5 : 5 + chunks * shards_of]
    post, pre, signal, cotangent, taps, sems = refs[5 + chunks * shards_of :]
    copies = [
        pltpu.make_async_copy(source, held, sems.at[i])
        for i, (source, held) in enumerate(zip(sources, (post, pre, signal, cotangent, taps)))
    ]
    for copy in copies:
        copy.start()
    for copy in copies:
        copy.wait()
    me = lax.axis_index("seq")
    channels, length = post.shape
    group = channels // shards_of
    width = group // chunks
    per = length // LANES
    field_rows = width * per
    for d in range(shards_of):
        owner = me ^ d
        gated = group_rows(pre, owner, group) * group_rows(signal, owner, group)
        d_conved = group_rows(cotangent, owner, group) * group_rows(post, owner, group)
        for f, x in enumerate((group_rows(taps, owner, group), gated, d_conved)):
            for q in range(chunks):
                for cb in range(0, width, SUBLANES):
                    for a in range(per):
                        start = f * field_rows + cb * per + a
                        top = q * width + cb
                        outs[q * shards_of + d][pl.ds(start, SUBLANES, stride=per), :] = x[
                            top : top + SUBLANES, a * LANES : (a + 1) * LANES
                        ]
    parts = []
    for cb in range(0, channels, 16):
        prod = (pre[cb : cb + 16, :].astype(F32) * signal[cb : cb + 16, :].astype(F32)) * (
            cotangent[cb : cb + 16, :].astype(F32) * post[cb : cb + 16, :].astype(F32)
        )
        parts.append(sum(prod[:, a * LANES : (a + 1) * LANES] for a in range(per)))
    folded = jnp.concatenate(parts + [jnp.zeros((LANES - channels, LANES), F32)], axis=0)
    skip = jnp.sum(folded.T, axis=0, keepdims=True)
    for d in range(shards_of):
        outs[d][3 * field_rows :, :] = jnp.broadcast_to(skip, (SUBLANES, LANES))


def spectral_kernel(shards_of, chunks, q, group, per, *refs):
    skip_gain, outer_w, inverse_w, filter_w, twiddle, dft = refs[:6]
    pieces = refs[6 : 6 + shards_of]
    outs = refs[6 + shards_of : 6 + 2 * shards_of]
    rest = refs[6 + 2 * shards_of :]
    if q == 0:
        d_skip, *rest = rest
    spectra, packed = rest[:3], rest[3:]
    width = group // chunks
    me = lax.axis_index("seq")
    blocks = shards_of * per
    field_rows = width * per
    cos_t = twiddle[0]
    sin_t = twiddle[1]
    forward = outer_w[me]
    total_len = blocks * LANES
    if q == 0:
        skips = sum(pieces[d][3 * field_rows : 3 * field_rows + 1, :] for d in range(shards_of))
        d_skip[...] = skips[:, : d_skip.shape[1]] * (1.0 / math.sqrt(total_len))

    for f in range(3):
        for c in range(0, width, 2):
            cols = []
            for ch in (c, c + 1):
                start = f * field_rows + ch * per
                cols.append(
                    jnp.concatenate([pieces[d][start : start + per, :] for d in range(shards_of)], axis=0)
                )
            mixed = outer_mix(forward, jnp.concatenate(cols, axis=1))
            for i in range(2):
                real = mixed[:blocks, i * LANES : (i + 1) * LANES]
                imag = mixed[blocks:, i * LANES : (i + 1) * LANES]
                row = jnp.concatenate(
                    [real * cos_t + imag * sin_t, imag * cos_t - real * sin_t], axis=1
                )
                packed[f][pl.ds((c + i) * blocks, blocks), :] = triple(row)
        spectra[f][...] = jnp.dot(packed[f][...], dft[...], preferred_element_type=F32)
    back = inverse_w[me]
    filter_back = filter_w[me]
    for ch in range(width):
        rows = pl.ds(ch * blocks, blocks)
        tr, ti = spectra[0][rows, :LANES], spectra[0][rows, LANES:]
        gr, gi = spectra[1][rows, :LANES], spectra[1][rows, LANES:]
        dr, di = spectra[2][rows, :LANES], spectra[2][rows, LANES:]
        tr = tr + skip_gain[me * group + q * width + ch]
        products = (
            (gr * tr - gi * ti, gr * ti + gi * tr),
            (tr * dr + ti * di, tr * di - ti * dr),
            (gr * dr + gi * di, gr * di - gi * dr),
        )
        for f, (real, imag) in enumerate(products):
            packed[f][rows, :] = triple(jnp.concatenate([imag, real], axis=1))
    for f in range(3):
        spectra[f][...] = jnp.dot(packed[f][...], dft[...], preferred_element_type=F32)
        for c in range(0, width, 2):
            cols = []
            for ch in (c, c + 1):
                rows = pl.ds(ch * blocks, blocks)
                imag, real = spectra[f][rows, :LANES], spectra[f][rows, LANES:]
                cols.append(
                    jnp.concatenate(
                        [real * cos_t - imag * sin_t, imag * cos_t + real * sin_t], axis=0
                    )
                )
            y = outer_mix(filter_back if f == 2 else back, jnp.concatenate(cols, axis=1))
            for i in range(2):
                start = f * field_rows + (c + i) * per
                for d in range(shards_of):
                    outs[d][start : start + per, :] = y[
                        d * per : (d + 1) * per, i * LANES : (i + 1) * LANES
                    ]


def gate_kernel(shards_of, chunks, *refs):
    post, pre, signal, cotangent = refs[:4]
    pieces = refs[4 : 4 + chunks * shards_of]
    output, d_post, d_pre, d_signal, d_filter = refs[4 + chunks * shards_of :]
    me = lax.axis_index("seq")
    channels, length = post.shape
    group = channels // shards_of
    per = length // LANES
    width = group // chunks
    field_rows = width * per
    for d in range(shards_of):
        rows = pl.ds(pl.multiple_of((me ^ d) * group, group), group)
        for a in range(per):
            cols = slice(a * LANES, (a + 1) * LANES)

            def field(f):
                return jnp.concatenate(
                    [
                        pieces[q * shards_of + d][
                            pl.ds(f * field_rows + cb * per + a, SUBLANES, stride=per), :
                        ]
                        for q in range(chunks)
                        for cb in range(0, width, SUBLANES)
                    ],
                    axis=0,
                )

            conved, d_gated = field(0), field(1)
            output[rows, cols] = (post[rows, cols].astype(F32) * conved).astype(BF16)
            d_post[rows, cols] = (cotangent[rows, cols].astype(F32) * conved).astype(BF16)
            d_pre[rows, cols] = (signal[rows, cols].astype(F32) * d_gated).astype(BF16)
            d_signal[rows, cols] = (pre[rows, cols].astype(F32) * d_gated).astype(BF16)
            d_filter[rows, cols] = field(2)


def shards(post_gate, pre_gate, signal, cotangent, filter_taps, skip_gain):
    shards_of = lax.axis_size("seq")
    channels, length = post_gate.shape
    group = channels // shards_of
    per = length // LANES
    chunks = CHUNKS if group % (CHUNKS * SUBLANES) == 0 else 1
    width = group // chunks
    field_rows = width * per
    total_len = shards_of * length
    vmem = pl.BlockSpec(memory_space=pltpu.VMEM)
    params = pltpu.CompilerParams(vmem_limit_bytes=48 * 2**20)

    def swap(pieces):
        moved = {
            d: lax.ppermute(pieces[d], "seq", [(i, i ^ d) for i in range(shards_of)])
            for d in reversed(range(1, shards_of))
        }
        return [pieces[0]] + [moved[d] for d in range(1, shards_of)]

    def rows(count):
        return [jax.ShapeDtypeStruct((count, LANES), F32)] * shards_of

    packed = pl.pallas_call(
        functools.partial(pack_kernel, shards_of, chunks),
        out_shape=rows(3 * field_rows + SUBLANES) + rows(3 * field_rows) * (chunks - 1),
        in_specs=[pl.BlockSpec(memory_space=pltpu.HBM)] * 5,
        out_specs=[vmem] * (chunks * shards_of),
        scratch_shapes=[pltpu.VMEM((channels, length), BF16)] * 4
        + [pltpu.VMEM((channels, length), F32), pltpu.SemaphoreType.DMA((5,))],
        compiler_params=params,
    )(
        *(
            pltpu.with_memory_space_constraint(x, pltpu.HBM)
            for x in (post_gate, pre_gate, signal, cotangent, filter_taps)
        )
    )
    arrived = [swap(packed[q * shards_of : (q + 1) * shards_of]) for q in range(chunks)]
    consts = [jnp.asarray(t) for t in tables(shards_of, total_len)]
    spectrum_rows = width * shards_of * per
    mixed = []
    for q in range(chunks):
        out = pl.pallas_call(
            functools.partial(spectral_kernel, shards_of, chunks, q, group, per),
            out_shape=rows(3 * field_rows)
            + [jax.ShapeDtypeStruct((1, channels), F32)] * (q == 0),
            in_specs=[pl.BlockSpec(memory_space=pltpu.SMEM)] + [vmem] * (5 + shards_of),
            out_specs=[vmem] * (shards_of + (q == 0)),
            scratch_shapes=[pltpu.VMEM((spectrum_rows, 2 * LANES), F32)] * 3
            + [pltpu.VMEM((spectrum_rows, 6 * LANES), BF16)] * 3,
            compiler_params=params,
        )(skip_gain, *consts, *arrived[q])
        if q == 0:
            d_skip = out[shards_of]
        mixed += swap(out[:shards_of])
    wide = jax.ShapeDtypeStruct((channels, length), BF16)
    output, d_post, d_pre, d_signal, d_filter = pl.pallas_call(
        functools.partial(gate_kernel, shards_of, chunks),
        out_shape=[wide] * 4 + [jax.ShapeDtypeStruct((channels, length), F32)],
        in_specs=[vmem] * (4 + chunks * shards_of),
        out_specs=[vmem] * 5,
        compiler_params=params,
    )(post_gate, pre_gate, signal, cotangent, *mixed)
    return (output, d_post, d_pre, d_signal, d_skip.reshape(channels), d_filter)


def solution(mesh):
    both = P("chan", "seq")
    return jax.shard_map(
        shards,
        mesh=mesh,
        in_specs=(both,) * 5 + (P("chan"),),
        out_specs=(both,) * 4 + (P("chan"), both),
        check_vma=False,
    )
```

time: 42.8 us -> 32 us (0.75)
  Pallas kernels: 12.6 us -> 6.32 us
  local copies, waits for them, and re-layouts: 4.61 us -> 0.06 us
    pallas_call x3, Pallas kernels: 12.6 us -> 6.32 us  [the longest x1 3.75 us: shards(): pl.pallas_call(functools.partial(spectral_kernel, shards_of, chunks, q, g...]
    unnamed x30 -> x20, local copies, waits for them, and re-layouts: 4.61 us -> 0.06 us
where the time goes in v1:
time: 32 us; the launch traced here: 31.8 us
  waiting for transfers between devices  16.7 us (52%)
  starting transfers between devices  8.03 us (25%)
  Pallas kernels  6.32 us (20%)
  between operations  0.77 us (2%)
    ppermute x6, waiting for transfers between devices, swap(): lax.ppermute(pieces[d], 'seq', [(i, i ^ d) for i in range(shards_of)])  16.7 us
    ppermute x6, starting transfers between devices, swap(): lax.ppermute(pieces[d], 'seq', [(i, i ^ d) for i in range(shards_of)])  8.03 us
    pallas_call x1, Pallas kernels, shards(): pl.pallas_call(functools.partial(spectral_kernel, shards_of, chunks, q, g...  3.75 us
    pallas_call x1, Pallas kernels, shards(): pl.pallas_call(functools.partial(pack_kernel, shards_of, chunks), out_sha...  1.5 us
    pallas_call x1, Pallas kernels, shards(): pl.pallas_call(functools.partial(gate_kernel, shards_of, chunks), out_sha...  1.06 us
  transfers between devices with their start and end apart: 6, of which 4 were waited for; matrix products, arithmetic and copies ran while one was open for 0% of the time, Pallas kernels for 0%

profile of v1, /device:TPU:0, one launch (start us, length us, event | category | flops | bytes accessed | tf_op | source)
XLA Modules:
  0.0 31.8 jit_solution(6913592525147863833)
XLA Ops:
  0.6 0.0 copy-start.4
  0.6 0.0 copy-start.5
  0.7 0.0 copy-start.6
  0.7 0.0 copy-start.7
  0.7 0.0 copy-start.8
  0.7 1.5 %shard_map.154 = (f32[392,128]{1,0:T(8,128)S(1)}, f32[392,128]{1,0:T(8,128)S(1)}, f32[392,128]{1,0:T(8,128)S(1)}, f32[392,128]{1,0:T(8,128)S(1)}) custom-call(bf16[64,1024]{1,0:T(8,128)(2,1)} %refs_0_.5, bf16[64,1024]{1,0:T(8,128)(2,1)} %refs_1_.4, bf16[64,1024]{1,0:T(8,128)(2,1)} %refs_2_.4, bf16[64,1024]{1,0:T(8,128)(2,1)} %refs_3_.4, f32[64,1024]{1,0:T(8,128)} %refs_4_.2), custom_call_target="tpu_custom_call" | custom-call | tf_op jit(solution)/shard_map/pallas_call | solution.py:255
  2.2 3.0 %collective-permute-start = (f32[392,128]{1,0:T(8,128)S(1)}, f32[392,128]{1,0:T(8,128)S(1)}, u32[]{:S(2)}, u32[]{:S(2)}) collective-permute-start(f32[392,128]{1,0:T(8,128)S(1)} %get-tuple-element.21), channel_id=1, source_target_pairs={{0,8},{8,0},{16,24},{24,16},{1,9},{9,1},{17,25},{25,17},{2,10},{10... | collective-permute-start | bytes 602120 | tf_op jit(solution)/shard_map/ppermute | solution.py:247
  5.2 1.5 %collective-permute-start.1 = (f32[392,128]{1,0:T(8,128)S(1)}, f32[392,128]{1,0:T(8,128)S(1)}, u32[]{:S(2)}, u32[]{:S(2)}) collective-permute-start(f32[392,128]{1,0:T(8,128)S(1)} %get-tuple-element.22), channel_id=1, source_target_pairs={{0,16},{8,24},{16,0},{24,8},{1,17},{9,25},{17,1},{25,9},{2,18},{10... | collective-permute-start | bytes 602120 | tf_op jit(solution)/shard_map/ppermute | solution.py:247
  6.7 0.0 copy-start.9
  6.7 0.0 collective-permute-start.2
  6.8 4.3 %collective-permute-done.refs_7_ = f32[392,128]{1,0:T(8,128)S(1)} collective-permute-done((f32[392,128]{1,0:T(8,128)S(1)}, f32[392,128]{1,0:T(8,128)S(1)}, u32[]{:S(2)}, u32[]{:S(2)}) %collective-permute-start) | collective-permute-done | bytes 200736 | tf_op jit(solution)/shard_map/ppermute | solution.py:247
  11.0 4.9 %collective-permute-done.1.refs_8_ = f32[392,128]{1,0:T(8,128)S(1)} collective-permute-done((f32[392,128]{1,0:T(8,128)S(1)}, f32[392,128]{1,0:T(8,128)S(1)}, u32[]{:S(2)}, u32[]{:S(2)}) %collective-permute-start.1) | collective-permute-done | bytes 200736 | tf_op jit(solution)/shard_map/ppermute | solution.py:247
  16.0 0.0 collective-permute-done.2.refs_9_
  16.0 0.0 copy-done.4
  16.0 0.0 copy-done.5
  16.0 0.0 copy-done.6
  16.0 0.0 copy-done.7
  16.0 0.0 copy-done.8
  16.0 0.0 copy-done.9
  16.0 0.0 copy-start
  16.0 0.0 copy-start.1
  16.0 0.0 copy-start.2
  16.0 0.0 copy-start.3
  16.1 3.8 %shard_map.155 = (f32[384,128]{1,0:T(8,128)S(1)}, f32[384,128]{1,0:T(8,128)S(1)}, f32[384,128]{1,0:T(8,128)S(1)}, f32[384,128]{1,0:T(8,128)S(1)}, f32[1,64]{1,0:T(1,128)}) custom-call(f32[64]{0:T(128)S(1)} %copy-done.9, bf16[4,64,96]{2,1,0:T(8,128)(2,1)S(1)} %copy-done.7, bf16[4,32,192]{2,1,0:T(8,128)(2,1)S(1)} %copy-done.6, ...), custom_call_target="tpu_custom_call" | custom-call | tf_op jit(solution)/shard_map/pallas_call | solution.py:274
  19.8 1.2 %collective-permute-start.3 = (f32[384,128]{1,0:T(8,128)S(1)}, f32[384,128]{1,0:T(8,128)S(1)}, u32[]{:S(2)}, u32[]{:S(2)}) collective-permute-start(f32[384,128]{1,0:T(8,128)S(1)} %get-tuple-element.25), channel_id=1, source_target_pairs={{0,8},{8,0},{16,24},{24,16},{1,9},{9,1},{17,25},{25,17},{2,10},{10... | collective-permute-start | bytes 589832 | tf_op jit(solution)/shard_map/ppermute | solution.py:247
  21.0 0.8 %collective-permute-start.4 = (f32[384,128]{1,0:T(8,128)S(1)}, f32[384,128]{1,0:T(8,128)S(1)}, u32[]{:S(2)}, u32[]{:S(2)}) collective-permute-start(f32[384,128]{1,0:T(8,128)S(1)} %get-tuple-element.26), channel_id=1, source_target_pairs={{0,16},{8,24},{16,0},{24,8},{1,17},{9,25},{17,1},{25,9},{2,18},{10... | collective-permute-start | bytes 589832 | tf_op jit(solution)/shard_map/ppermute | solution.py:247
  21.9 1.4 %collective-permute-start.5 = (f32[384,128]{1,0:T(8,128)S(1)}, f32[384,128]{1,0:T(8,128)S(1)}, u32[]{:S(2)}, u32[]{:S(2)}) collective-permute-start(f32[384,128]{1,0:T(8,128)S(1)} %get-tuple-element.27), channel_id=1, source_target_pairs={{0,24},{8,16},{16,8},{24,0},{1,25},{9,17},{17,9},{25,1},{2,26},{10... | collective-permute-start | bytes 589832 | tf_op jit(solution)/shard_map/ppermute | solution.py:247
  23.3 4.2 %collective-permute-done.3.refs_5_ = f32[384,128]{1,0:T(8,128)S(1)} collective-permute-done((f32[384,128]{1,0:T(8,128)S(1)}, f32[384,128]{1,0:T(8,128)S(1)}, u32[]{:S(2)}, u32[]{:S(2)}) %collective-permute-start.3) | collective-permute-done | bytes 196640 | tf_op jit(solution)/shard_map/ppermute | solution.py:247
  27.5 3.3 %collective-permute-done.4.refs_6_ = f32[384,128]{1,0:T(8,128)S(1)} collective-permute-done((f32[384,128]{1,0:T(8,128)S(1)}, f32[384,128]{1,0:T(8,128)S(1)}, u32[]{:S(2)}, u32[]{:S(2)}) %collective-permute-start.4) | collective-permute-done | bytes 196640 | tf_op jit(solution)/shard_map/ppermute | solution.py:247
  30.7 0.0 collective-permute-done.5.refs_7_
  30.7 0.0 copy-done
  30.7 0.0 copy-done.1
  30.8 0.0 copy-done.2
  30.8 0.0 copy-done.3
  30.8 1.1 %shard_map.156 = (bf16[64,1024]{1,0:T(8,128)(2,1)}, bf16[64,1024]{1,0:T(8,128)(2,1)}, bf16[64,1024]{1,0:T(8,128)(2,1)}, bf16[64,1024]{1,0:T(8,128)(2,1)}, f32[64,1024]{1,0:T(8,128)}) custom-call(bf16[64,1024]{1,0:T(8,128)(2,1)S(1)} %copy-done, bf16[64,1024]{1,0:T(8,128)(2,1)S(1)} %copy-done.1, bf16[64,1024]{1,0:T(8,128)(2,1)S(1)} %copy-done.2, ...), custom_call_target="tpu_custom_call" | custom-call | tf_op jit(solution)/shard_map/pallas_call | solution.py:288
Async XLA Ops:
  0.6 15.3 %copy-start.4 = (bf16[768,256]{1,0:T(8,128)(2,1)S(1)}, bf16[768,256]{1,0:T(8,128)(2,1)}, u32[]{:S(2)}) copy-start(bf16[768,256]{1,0:T(8,128)(2,1)} %constant.14.clone.refs_5_) | copy-start | bytes 1179652
  0.6 15.3 %copy-start.5 = (bf16[4,32,192]{2,1,0:T(8,128)(2,1)S(1)}, bf16[4,32,192]{2,1,0:T(8,128)(2,1)}, u32[]{:S(2)}) copy-start(bf16[4,32,192]{2,1,0:T(8,128)(2,1)} %constant.12.clone.refs_3_) | copy-start | bytes 147460
  0.7 15.3 %copy-start.6 = (bf16[4,32,192]{2,1,0:T(8,128)(2,1)S(1)}, bf16[4,32,192]{2,1,0:T(8,128)(2,1)}, u32[]{:S(2)}) copy-start(bf16[4,32,192]{2,1,0:T(8,128)(2,1)} %constant.11.clone.refs_2_) | copy-start | bytes 147460
  0.7 15.3 %copy-start.7 = (bf16[4,64,96]{2,1,0:T(8,128)(2,1)S(1)}, bf16[4,64,96]{2,1,0:T(8,128)(2,1)}, u32[]{:S(2)}) copy-start(bf16[4,64,96]{2,1,0:T(8,128)(2,1)} %constant.10.clone.refs_1_) | copy-start | bytes 147460
  0.7 15.3 %copy-start.8 = (f32[2,32,128]{2,1,0:T(8,128)S(1)}, f32[2,32,128]{2,1,0:T(8,128)}, u32[]{:S(2)}) copy-start(f32[2,32,128]{2,1,0:T(8,128)} %constant.13.clone.refs_4_) | copy-start | bytes 98308
  2.2 8.8 %collective-permute-start = (f32[392,128]{1,0:T(8,128)S(1)}, f32[392,128]{1,0:T(8,128)S(1)}, u32[]{:S(2)}, u32[]{:S(2)}) collective-permute-start(f32[392,128]{1,0:T(8,128)S(1)} %get-tuple-element.21), channel_id=1, source_target_pairs={{0,8},{8,0},{16,24},{24,16},{1,9},{9,1},{17,25},{25,17},{2,10},{10... | collective-permute-start | bytes 602120 | tf_op jit(solution)/shard_map/ppermute | solution.py:247
  5.2 10.8 %collective-permute-start.1 = (f32[392,128]{1,0:T(8,128)S(1)}, f32[392,128]{1,0:T(8,128)S(1)}, u32[]{:S(2)}, u32[]{:S(2)}) collective-permute-start(f32[392,128]{1,0:T(8,128)S(1)} %get-tuple-element.22), channel_id=1, source_target_pairs={{0,16},{8,24},{16,0},{24,8},{1,17},{9,25},{17,1},{25,9},{2,18},{10... | collective-permute-start | bytes 602120 | tf_op jit(solution)/shard_map/ppermute | solution.py:247
  6.7 9.3 %copy-start.9 = (f32[64]{0:T(128)S(1)}, f32[64]{0:T(128)}, u32[]{:S(2)}) copy-start(f32[64]{0:T(128)} %refs_0_.4) | copy-start | bytes 772
  6.7 9.2 %collective-permute-start.2 = (f32[392,128]{1,0:T(8,128)S(1)}, f32[392,128]{1,0:T(8,128)S(1)}, u32[]{:S(2)}, u32[]{:S(2)}) collective-permute-start(f32[392,128]{1,0:T(8,128)S(1)} %get-tuple-element.23), channel_id=1, source_target_pairs={{0,24},{8,16},{16,8},{24,0},{1,25},{9,17},{17,9},{25,1},{2,26},{10... | collective-permute-start | bytes 602120 | tf_op jit(solution)/shard_map/ppermute | solution.py:247
  16.0 14.7 %copy-start = (bf16[64,1024]{1,0:T(8,128)(2,1)S(1)}, bf16[64,1024]{1,0:T(8,128)(2,1)}, u32[]{:S(2)}) copy-start(bf16[64,1024]{1,0:T(8,128)(2,1)} %refs_0_.5) | copy-start | bytes 393220
  16.0 14.7 %copy-start.1 = (bf16[64,1024]{1,0:T(8,128)(2,1)S(1)}, bf16[64,1024]{1,0:T(8,128)(2,1)}, u32[]{:S(2)}) copy-start(bf16[64,1024]{1,0:T(8,128)(2,1)} %refs_1_.4) | copy-start | bytes 393220
  16.0 14.7 %copy-start.2 = (bf16[64,1024]{1,0:T(8,128)(2,1)S(1)}, bf16[64,1024]{1,0:T(8,128)(2,1)}, u32[]{:S(2)}) copy-start(bf16[64,1024]{1,0:T(8,128)(2,1)} %refs_2_.4) | copy-start | bytes 393220
  16.0 14.7 %copy-start.3 = (bf16[64,1024]{1,0:T(8,128)(2,1)S(1)}, bf16[64,1024]{1,0:T(8,128)(2,1)}, u32[]{:S(2)}) copy-start(bf16[64,1024]{1,0:T(8,128)(2,1)} %refs_3_.4) | copy-start | bytes 393220
  19.8 7.7 %collective-permute-start.3 = (f32[384,128]{1,0:T(8,128)S(1)}, f32[384,128]{1,0:T(8,128)S(1)}, u32[]{:S(2)}, u32[]{:S(2)}) collective-permute-start(f32[384,128]{1,0:T(8,128)S(1)} %get-tuple-element.25), channel_id=1, source_target_pairs={{0,8},{8,0},{16,24},{24,16},{1,9},{9,1},{17,25},{25,17},{2,10},{10... | collective-permute-start | bytes 589832 | tf_op jit(solution)/shard_map/ppermute | solution.py:247
  21.0 9.7 %collective-permute-start.4 = (f32[384,128]{1,0:T(8,128)S(1)}, f32[384,128]{1,0:T(8,128)S(1)}, u32[]{:S(2)}, u32[]{:S(2)}) collective-permute-start(f32[384,128]{1,0:T(8,128)S(1)} %get-tuple-element.26), channel_id=1, source_target_pairs={{0,16},{8,24},{16,0},{24,8},{1,17},{9,25},{17,1},{25,9},{2,18},{10... | collective-permute-start | bytes 589832 | tf_op jit(solution)/shard_map/ppermute | solution.py:247
  21.9 8.9 %collective-permute-start.5 = (f32[384,128]{1,0:T(8,128)S(1)}, f32[384,128]{1,0:T(8,128)S(1)}, u32[]{:S(2)}, u32[]{:S(2)}) collective-permute-start(f32[384,128]{1,0:T(8,128)S(1)} %get-tuple-element.27), channel_id=1, source_target_pairs={{0,24},{8,16},{16,8},{24,0},{1,25},{9,17},{17,9},{25,1},{2,26},{10... | collective-permute-start | bytes 589832 | tf_op jit(solution)/shard_map/ppermute | solution.py:247

commit v2 on v1

--- a/solution.py
+++ b/solution.py
@@ -11,7 +11,7 @@
 from jax.sharding import PartitionSpec as P
 
 LANES = 128
-CHUNKS = 1
+CHUNKS = 2
 SUBLANES = 8
 BF16 = jnp.bfloat16
 F32 = jnp.float32

time: 32 us -> 30.3 us (0.947)
  waiting for transfers between devices: 16.7 us -> 5.32 us
  starting transfers between devices: 8.03 us -> 16.4 us
  Pallas kernels: 6.32 us -> 7.63 us
    ppermute x6 -> x12, waiting for transfers between devices: 16.7 us -> 5.32 us  [swap(): lax.ppermute(pieces[d], 'seq', [(i, i ^ d) for i in range(shards_of)])]
    ppermute x6 -> x12, starting transfers between devices: 8.03 us -> 16.4 us  [swap(): lax.ppermute(pieces[d], 'seq', [(i, i ^ d) for i in range(shards_of)])]
    pallas_call x1 -> x2, Pallas kernels: 3.75 us -> 5.06 us  [shards(): pl.pallas_call(functools.partial(spectral_kernel, shards_of, chunks, q, g...]
  transfers between devices with their start and end apart: 6 -> 12, of which waited for: 4 -> 5; matrix products, arithmetic and copies ran while one was open for 0% -> 0% of each run, Pallas kernels for 0% -> 17%
where the time goes in v2:
time: 30.3 us; the launch traced here: 30.1 us
  starting transfers between devices  16.4 us (54%)
  Pallas kernels  7.63 us (25%)
  waiting for transfers between devices  5.32 us (18%)
  between operations  0.76 us (3%)
    ppermute x12, starting transfers between devices, swap(): lax.ppermute(pieces[d], 'seq', [(i, i ^ d) for i in range(shards_of)])  16.4 us
    ppermute x12, waiting for transfers between devices, swap(): lax.ppermute(pieces[d], 'seq', [(i, i ^ d) for i in range(shards_of)])  5.32 us
    pallas_call x2, Pallas kernels, shards(): pl.pallas_call(functools.partial(spectral_kernel, shards_of, chunks, q, g...  5.06 us
    pallas_call x1, Pallas kernels, shards(): pl.pallas_call(functools.partial(pack_kernel, shards_of, chunks), out_sha...  1.5 us
    pallas_call x1, Pallas kernels, shards(): pl.pallas_call(functools.partial(gate_kernel, shards_of, chunks), out_sha...  1.07 us
  transfers between devices with their start and end apart: 12, of which 5 were waited for; matrix products, arithmetic and copies ran while one was open for 0% of the time, Pallas kernels for 17%

profile of v2, /device:TPU:0, one launch (start us, length us, event | category | flops | bytes accessed | tf_op | source)
XLA Modules:
  0.0 30.1 jit_solution(16954218605642221368)
XLA Ops:
  0.6 0.0 copy-start
  0.6 0.0 copy-start.5
  0.7 0.0 copy-start.6
  0.7 0.0 copy-start.7
  0.7 0.0 copy-start.8
  0.7 1.5 %shard_map.154 = (f32[200,128]{1,0:T(8,128)S(1)}, f32[200,128]{1,0:T(8,128)S(1)}, f32[200,128]{1,0:T(8,128)S(1)}, f32[200,128]{1,0:T(8,128)S(1)}, f32[192,128]{1...) custom-call(bf16[64,1024]{1,0:T(8,128)(2,1)} %refs_0_.7, ...), custom_call_target="tpu_custom_call" | custom-call | tf_op jit(solution)/shard_map/pallas_call | solution.py:255
  2.2 3.0 %collective-permute-start.6 = (f32[192,128]{1,0:T(8,128)S(1)}, f32[192,128]{1,0:T(8,128)S(1)}, u32[]{:S(2)}, u32[]{:S(2)}) collective-permute-start(f32[192,128]{1,0:T(8,128)S(1)} %get-tuple-element.37), channel_id=1, source_target_pairs={{0,8},{8,0},{16,24},{24,16},{1,9},{9,1},{17,25},{25,17},{2,10},{10... | collective-permute-start | bytes 294920 | tf_op jit(solution)/shard_map/ppermute | solution.py:247
  5.2 1.5 %collective-permute-start.7 = (f32[192,128]{1,0:T(8,128)S(1)}, f32[192,128]{1,0:T(8,128)S(1)}, u32[]{:S(2)}, u32[]{:S(2)}) collective-permute-start(f32[192,128]{1,0:T(8,128)S(1)} %get-tuple-element.38), channel_id=1, source_target_pairs={{0,16},{8,24},{16,0},{24,8},{1,17},{9,25},{17,1},{25,9},{2,18},{10... | collective-permute-start | bytes 294920 | tf_op jit(solution)/shard_map/ppermute | solution.py:247
  6.7 0.0 collective-permute-start.8
  6.8 1.9 %collective-permute-start = (f32[200,128]{1,0:T(8,128)S(1)}, f32[200,128]{1,0:T(8,128)S(1)}, u32[]{:S(2)}, u32[]{:S(2)}) collective-permute-start(f32[200,128]{1,0:T(8,128)S(1)} %get-tuple-element.29), channel_id=1, source_target_pairs={{0,8},{8,0},{16,24},{24,16},{1,9},{9,1},{17,25},{25,17},{2,10},{10... | collective-permute-start | bytes 307208 | tf_op jit(solution)/shard_map/ppermute | solution.py:247
  8.7 1.5 %collective-permute-start.1 = (f32[200,128]{1,0:T(8,128)S(1)}, f32[200,128]{1,0:T(8,128)S(1)}, u32[]{:S(2)}, u32[]{:S(2)}) collective-permute-start(f32[200,128]{1,0:T(8,128)S(1)} %get-tuple-element.30), channel_id=1, source_target_pairs={{0,16},{8,24},{16,0},{24,8},{1,17},{9,25},{17,1},{25,9},{2,18},{10... | collective-permute-start | bytes 307208 | tf_op jit(solution)/shard_map/ppermute | solution.py:247
  10.2 0.0 collective-permute-done.6.refs_7_
  10.2 0.0 copy-start.9
  10.2 1.3 %collective-permute-start.2 = (f32[200,128]{1,0:T(8,128)S(1)}, f32[200,128]{1,0:T(8,128)S(1)}, u32[]{:S(2)}, u32[]{:S(2)}) collective-permute-start(f32[200,128]{1,0:T(8,128)S(1)} %get-tuple-element.31), channel_id=1, source_target_pairs={{0,24},{8,16},{16,8},{24,0},{1,25},{9,17},{17,9},{25,1},{2,26},{10... | collective-permute-start | bytes 307208 | tf_op jit(solution)/shard_map/ppermute | solution.py:247
  11.5 0.2 collective-permute-done.7.refs_8_
  11.7 1.7 %collective-permute-done.8.refs_9_ = f32[192,128]{1,0:T(8,128)S(1)} collective-permute-done((f32[192,128]{1,0:T(8,128)S(1)}, f32[192,128]{1,0:T(8,128)S(1)}, u32[]{:S(2)}, u32[]{:S(2)}) %collective-permute-start.8) | collective-permute-done | bytes 98336 | tf_op jit(solution)/shard_map/ppermute | solution.py:247
  13.4 0.0 copy-done
  13.4 0.0 copy-done.5
  13.4 0.0 copy-done.6
  13.4 0.0 copy-done.7
  13.5 0.0 copy-done.8
  13.5 0.0 copy-done.9
  13.5 2.3 %shard_map.156 = (f32[192,128]{1,0:T(8,128)S(1)}, f32[192,128]{1,0:T(8,128)S(1)}, f32[192,128]{1,0:T(8,128)S(1)}, f32[192,128]{1,0:T(8,128)S(1)}) custom-call(f32[64]{0:T(128)S(1)} %copy-done.9, bf16[4,64,96]{2,1,0:T(8,128)(2,1)S(1)} %copy-done.7, bf16[4,32,192]{2,1,0:T(8,128)(2,1)S(1)} %copy-done.6, bf16[4,32,192]{2,1,0:T(8,128)(2,1)S(1)} %copy-done.5, ...), custom_call_target="tpu_custom_call" | custom-call | tf_op jit(solution)/shard_map/pallas_call | solution.py:274
  15.8 0.5 %collective-permute-start.9 = (f32[192,128]{1,0:T(8,128)S(1)}, f32[192,128]{1,0:T(8,128)S(1)}, u32[]{:S(2)}, u32[]{:S(2)}) collective-permute-start(f32[192,128]{1,0:T(8,128)S(1)} %get-tuple-element.41), channel_id=1, source_target_pairs={{0,8},{8,0},{16,24},{24,16},{1,9},{9,1},{17,25},{25,17},{2,10},{10... | collective-permute-start | bytes 294920 | tf_op jit(solution)/shard_map/ppermute | solution.py:247
  16.3 0.9 %collective-permute-start.10 = (f32[192,128]{1,0:T(8,128)S(1)}, f32[192,128]{1,0:T(8,128)S(1)}, u32[]{:S(2)}, u32[]{:S(2)}) collective-permute-start(f32[192,128]{1,0:T(8,128)S(1)} %get-tuple-element.42), channel_id=1, source_target_pairs={{0,16},{8,24},{16,0},{24,8},{1,17},{9,25},{17,1},{25,9},{2,18},{10... | collective-permute-start | bytes 294920 | tf_op jit(solution)/shard_map/ppermute | solution.py:247
  17.2 0.0 collective-permute-done.refs_7_
  17.2 2.1 %collective-permute-start.11 = (f32[192,128]{1,0:T(8,128)S(1)}, f32[192,128]{1,0:T(8,128)S(1)}, u32[]{:S(2)}, u32[]{:S(2)}) collective-permute-start(f32[192,128]{1,0:T(8,128)S(1)} %get-tuple-element.43), channel_id=1, source_target_pairs={{0,24},{8,16},{16,8},{24,0},{1,25},{9,17},{17,9},{25,1},{2,26},{10... | collective-permute-start | bytes 294920 | tf_op jit(solution)/shard_map/ppermute | solution.py:247
  19.4 0.0 collective-permute-done.1.refs_8_
  19.4 0.0 collective-permute-done.2.refs_9_
  19.4 0.0 copy-start.1
  19.4 0.0 copy-start.2
  19.4 0.0 copy-start.3
  19.4 0.0 copy-start.4
  19.4 2.7 %shard_map.155 = (f32[192,128]{1,0:T(8,128)S(1)}, f32[192,128]{1,0:T(8,128)S(1)}, f32[192,128]{1,0:T(8,128)S(1)}, f32[192,128]{1,0:T(8,128)S(1)}, f32[1,64]{1,0:T(1,128)}) custom-call(f32[64]{0:T(128)S(1)} %copy-done.9, bf16[4,64,96]{2,1,0:T(8,128)(2,1)S(1)} %copy-done.7, bf16[4,32,192]{2,1,0:T(8,128)(2,1)S(1)} %copy-done.6, ...), custom_call_target="tpu_custom_call" | custom-call | tf_op jit(solution)/shard_map/pallas_call | solution.py:274
  22.1 0.5 %collective-permute-start.3 = (f32[192,128]{1,0:T(8,128)S(1)}, f32[192,128]{1,0:T(8,128)S(1)}, u32[]{:S(2)}, u32[]{:S(2)}) collective-permute-start(f32[192,128]{1,0:T(8,128)S(1)} %get-tuple-element.33), channel_id=1, source_target_pairs={{0,8},{8,0},{16,24},{24,16},{1,9},{9,1},{17,25},{25,17},{2,10},{10... | collective-permute-start | bytes 294920 | tf_op jit(solution)/shard_map/ppermute | solution.py:247
  22.6 0.9 %collective-permute-start.4 = (f32[192,128]{1,0:T(8,128)S(1)}, f32[192,128]{1,0:T(8,128)S(1)}, u32[]{:S(2)}, u32[]{:S(2)}) collective-permute-start(f32[192,128]{1,0:T(8,128)S(1)} %get-tuple-element.34), channel_id=1, source_target_pairs={{0,16},{8,24},{16,0},{24,8},{1,17},{9,25},{17,1},{25,9},{2,18},{10... | collective-permute-start | bytes 294920 | tf_op jit(solution)/shard_map/ppermute | solution.py:247
  23.5 0.0 collective-permute-done.9.refs_9_
  23.5 2.1 %collective-permute-start.5 = (f32[192,128]{1,0:T(8,128)S(1)}, f32[192,128]{1,0:T(8,128)S(1)}, u32[]{:S(2)}, u32[]{:S(2)}) collective-permute-start(f32[192,128]{1,0:T(8,128)S(1)} %get-tuple-element.35), channel_id=1, source_target_pairs={{0,24},{8,16},{16,8},{24,0},{1,25},{9,17},{17,9},{25,1},{2,26},{10... | collective-permute-start | bytes 294920 | tf_op jit(solution)/shard_map/ppermute | solution.py:247
  25.6 0.0 collective-permute-done.10.refs_10_
  25.6 0.0 collective-permute-done.11.refs_11_
  25.6 1.1 %collective-permute-done.3.refs_5_ = f32[192,128]{1,0:T(8,128)S(1)} collective-permute-done((f32[192,128]{1,0:T(8,128)S(1)}, f32[192,128]{1,0:T(8,128)S(1)}, u32[]{:S(2)}, u32[]{:S(2)}) %collective-permute-start.3) | collective-permute-done | bytes 98336 | tf_op jit(solution)/shard_map/ppermute | solution.py:247
  26.8 0.5 %collective-permute-done.4.refs_6_ = f32[192,128]{1,0:T(8,128)S(1)} collective-permute-done((f32[192,128]{1,0:T(8,128)S(1)}, f32[192,128]{1,0:T(8,128)S(1)}, u32[]{:S(2)}, u32[]{:S(2)}) %collective-permute-start.4) | collective-permute-done | bytes 98336 | tf_op jit(solution)/shard_map/ppermute | solution.py:247
  27.2 1.8 %collective-permute-done.5.refs_7_ = f32[192,128]{1,0:T(8,128)S(1)} collective-permute-done((f32[192,128]{1,0:T(8,128)S(1)}, f32[192,128]{1,0:T(8,128)S(1)}, u32[]{:S(2)}, u32[]{:S(2)}) %collective-permute-start.5) | collective-permute-done | bytes 98336 | tf_op jit(solution)/shard_map/ppermute | solution.py:247
  29.0 0.0 copy-done.1
  29.0 0.0 copy-done.2
  29.0 0.0 copy-done.3
  29.1 0.0 copy-done.4
  29.1 1.1 %shard_map.157 = (bf16[64,1024]{1,0:T(8,128)(2,1)}, bf16[64,1024]{1,0:T(8,128)(2,1)}, bf16[64,1024]{1,0:T(8,128)(2,1)}, bf16[64,1024]{1,0:T(8,128)(2,1)}, f32[64,1024]{1,0:T(8,128)}) custom-call(bf16[64,1024]{1,0:T(8,128)(2,1)S(1)} %copy-done.1, bf16[64,1024]{1,0:T(8,128)(2,1)S(1)} %copy-done.2, bf16[64,1024]{1,0:T(8,128)(2,1)S(1)} %copy-done.3, ...), custom_call_target="tpu_custom_call" | custom-call | tf_op jit(solution)/shard_map/pallas_call | solution.py:288
Async XLA Ops:
  0.6 12.8 %copy-start = (bf16[768,256]{1,0:T(8,128)(2,1)S(1)}, bf16[768,256]{1,0:T(8,128)(2,1)}, u32[]{:S(2)}) copy-start(bf16[768,256]{1,0:T(8,128)(2,1)} %constant.14.clone.refs_5_) | copy-start | bytes 1179652
  0.6 12.8 %copy-start.5 = (bf16[4,32,192]{2,1,0:T(8,128)(2,1)S(1)}, bf16[4,32,192]{2,1,0:T(8,128)(2,1)}, u32[]{:S(2)}) copy-start(bf16[4,32,192]{2,1,0:T(8,128)(2,1)} %constant.12.clone.refs_3_) | copy-start | bytes 147460
  0.7 12.8 %copy-start.6 = (bf16[4,32,192]{2,1,0:T(8,128)(2,1)S(1)}, bf16[4,32,192]{2,1,0:T(8,128)(2,1)}, u32[]{:S(2)}) copy-start(bf16[4,32,192]{2,1,0:T(8,128)(2,1)} %constant.11.clone.refs_2_) | copy-start | bytes 147460
  0.7 12.8 %copy-start.7 = (bf16[4,64,96]{2,1,0:T(8,128)(2,1)S(1)}, bf16[4,64,96]{2,1,0:T(8,128)(2,1)}, u32[]{:S(2)}) copy-start(bf16[4,64,96]{2,1,0:T(8,128)(2,1)} %constant.10.clone.refs_1_) | copy-start | bytes 147460
  0.7 12.8 %copy-start.8 = (f32[2,32,128]{2,1,0:T(8,128)S(1)}, f32[2,32,128]{2,1,0:T(8,128)}, u32[]{:S(2)}) copy-start(f32[2,32,128]{2,1,0:T(8,128)} %constant.13.clone.refs_4_) | copy-start | bytes 98308
  2.2 8.0 %collective-permute-start.6 = (f32[192,128]{1,0:T(8,128)S(1)}, f32[192,128]{1,0:T(8,128)S(1)}, u32[]{:S(2)}, u32[]{:S(2)}) collective-permute-start(f32[192,128]{1,0:T(8,128)S(1)} %get-tuple-element.37), channel_id=1, source_target_pairs={{0,8},{8,0},{16,24},{24,16},{1,9},{9,1},{17,25},{25,17},{2,10},{10... | collective-permute-start | bytes 294920 | tf_op jit(solution)/shard_map/ppermute | solution.py:247
  5.2 6.5 %collective-permute-start.7 = (f32[192,128]{1,0:T(8,128)S(1)}, f32[192,128]{1,0:T(8,128)S(1)}, u32[]{:S(2)}, u32[]{:S(2)}) collective-permute-start(f32[192,128]{1,0:T(8,128)S(1)} %get-tuple-element.38), channel_id=1, source_target_pairs={{0,16},{8,24},{16,0},{24,8},{1,17},{9,25},{17,1},{25,9},{2,18},{10... | collective-permute-start | bytes 294920 | tf_op jit(solution)/shard_map/ppermute | solution.py:247
  6.7 6.7 %collective-permute-start.8 = (f32[192,128]{1,0:T(8,128)S(1)}, f32[192,128]{1,0:T(8,128)S(1)}, u32[]{:S(2)}, u32[]{:S(2)}) collective-permute-start(f32[192,128]{1,0:T(8,128)S(1)} %get-tuple-element.39), channel_id=1, source_target_pairs={{0,24},{8,16},{16,8},{24,0},{1,25},{9,17},{17,9},{25,1},{2,26},{10... | collective-permute-start | bytes 294920 | tf_op jit(solution)/shard_map/ppermute | solution.py:247
  6.8 10.5 %collective-permute-start = (f32[200,128]{1,0:T(8,128)S(1)}, f32[200,128]{1,0:T(8,128)S(1)}, u32[]{:S(2)}, u32[]{:S(2)}) collective-permute-start(f32[200,128]{1,0:T(8,128)S(1)} %get-tuple-element.29), channel_id=1, source_target_pairs={{0,8},{8,0},{16,24},{24,16},{1,9},{9,1},{17,25},{25,17},{2,10},{10... | collective-permute-start | bytes 307208 | tf_op jit(solution)/shard_map/ppermute | solution.py:247
  8.7 10.7 %collective-permute-start.1 = (f32[200,128]{1,0:T(8,128)S(1)}, f32[200,128]{1,0:T(8,128)S(1)}, u32[]{:S(2)}, u32[]{:S(2)}) collective-permute-start(f32[200,128]{1,0:T(8,128)S(1)} %get-tuple-element.30), channel_id=1, source_target_pairs={{0,16},{8,24},{16,0},{24,8},{1,17},{9,25},{17,1},{25,9},{2,18},{10... | collective-permute-start | bytes 307208 | tf_op jit(solution)/shard_map/ppermute | solution.py:247
  10.2 3.2 %copy-start.9 = (f32[64]{0:T(128)S(1)}, f32[64]{0:T(128)}, u32[]{:S(2)}) copy-start(f32[64]{0:T(128)} %refs_0_.6) | copy-start | bytes 772
  10.2 9.1 %collective-permute-start.2 = (f32[200,128]{1,0:T(8,128)S(1)}, f32[200,128]{1,0:T(8,128)S(1)}, u32[]{:S(2)}, u32[]{:S(2)}) collective-permute-start(f32[200,128]{1,0:T(8,128)S(1)} %get-tuple-element.31), channel_id=1, source_target_pairs={{0,24},{8,16},{16,8},{24,0},{1,25},{9,17},{17,9},{25,1},{2,26},{10... | collective-permute-start | bytes 307208 | tf_op jit(solution)/shard_map/ppermute | solution.py:247
  15.8 7.7 %collective-permute-start.9 = (f32[192,128]{1,0:T(8,128)S(1)}, f32[192,128]{1,0:T(8,128)S(1)}, u32[]{:S(2)}, u32[]{:S(2)}) collective-permute-start(f32[192,128]{1,0:T(8,128)S(1)} %get-tuple-element.41), channel_id=1, source_target_pairs={{0,8},{8,0},{16,24},{24,16},{1,9},{9,1},{17,25},{25,17},{2,10},{10... | collective-permute-start | bytes 294920 | tf_op jit(solution)/shard_map/ppermute | solution.py:247
  16.3 9.3 %collective-permute-start.10 = (f32[192,128]{1,0:T(8,128)S(1)}, f32[192,128]{1,0:T(8,128)S(1)}, u32[]{:S(2)}, u32[]{:S(2)}) collective-permute-start(f32[192,128]{1,0:T(8,128)S(1)} %get-tuple-element.42), channel_id=1, source_target_pairs={{0,16},{8,24},{16,0},{24,8},{1,17},{9,25},{17,1},{25,9},{2,18},{10... | collective-permute-start | bytes 294920 | tf_op jit(solution)/shard_map/ppermute | solution.py:247
  17.2 8.4 %collective-permute-start.11 = (f32[192,128]{1,0:T(8,128)S(1)}, f32[192,128]{1,0:T(8,128)S(1)}, u32[]{:S(2)}, u32[]{:S(2)}) collective-permute-start(f32[192,128]{1,0:T(8,128)S(1)} %get-tuple-element.43), channel_id=1, source_target_pairs={{0,24},{8,16},{16,8},{24,0},{1,25},{9,17},{17,9},{25,1},{2,26},{10... | collective-permute-start | bytes 294920 | tf_op jit(solution)/shard_map/ppermute | solution.py:247
  19.4 9.7 %copy-start.1 = (bf16[64,1024]{1,0:T(8,128)(2,1)S(1)}, bf16[64,1024]{1,0:T(8,128)(2,1)}, u32[]{:S(2)}) copy-start(bf16[64,1024]{1,0:T(8,128)(2,1)} %refs_0_.7) | copy-start | bytes 393220
  19.4 9.7 %copy-start.2 = (bf16[64,1024]{1,0:T(8,128)(2,1)S(1)}, bf16[64,1024]{1,0:T(8,128)(2,1)}, u32[]{:S(2)}) copy-start(bf16[64,1024]{1,0:T(8,128)(2,1)} %refs_1_.5) | copy-start | bytes 393220
  19.4 9.7 %copy-start.3 = (bf16[64,1024]{1,0:T(8,128)(2,1)S(1)}, bf16[64,1024]{1,0:T(8,128)(2,1)}, u32[]{:S(2)}) copy-start(bf16[64,1024]{1,0:T(8,128)(2,1)} %refs_2_.5) | copy-start | bytes 393220
  19.4 9.7 %copy-start.4 = (bf16[64,1024]{1,0:T(8,128)(2,1)S(1)}, bf16[64,1024]{1,0:T(8,128)(2,1)}, u32[]{:S(2)}) copy-start(bf16[64,1024]{1,0:T(8,128)(2,1)} %refs_3_.5) | copy-start | bytes 393220
  22.1 4.6 %collective-permute-start.3 = (f32[192,128]{1,0:T(8,128)S(1)}, f32[192,128]{1,0:T(8,128)S(1)}, u32[]{:S(2)}, u32[]{:S(2)}) collective-permute-start(f32[192,128]{1,0:T(8,128)S(1)} %get-tuple-element.33), channel_id=1, source_target_pairs={{0,8},{8,0},{16,24},{24,16},{1,9},{9,1},{17,25},{25,17},{2,10},{10... | collective-permute-start | bytes 294920 | tf_op jit(solution)/shard_map/ppermute | solution.py:247
  22.6 4.6 %collective-permute-start.4 = (f32[192,128]{1,0:T(8,128)S(1)}, f32[192,128]{1,0:T(8,128)S(1)}, u32[]{:S(2)}, u32[]{:S(2)}) collective-permute-start(f32[192,128]{1,0:T(8,128)S(1)} %get-tuple-element.34), channel_id=1, source_target_pairs={{0,16},{8,24},{16,0},{24,8},{1,17},{9,25},{17,1},{25,9},{2,18},{10... | collective-permute-start | bytes 294920 | tf_op jit(solution)/shard_map/ppermute | solution.py:247
  23.5 5.5 %collective-permute-start.5 = (f32[192,128]{1,0:T(8,128)S(1)}, f32[192,128]{1,0:T(8,128)S(1)}, u32[]{:S(2)}, u32[]{:S(2)}) collective-permute-start(f32[192,128]{1,0:T(8,128)S(1)} %get-tuple-element.35), channel_id=1, source_target_pairs={{0,24},{8,16},{16,8},{24,0},{1,25},{9,17},{17,9},{25,1},{2,26},{10... | collective-permute-start | bytes 294920 | tf_op jit(solution)/shard_map/ppermute | solution.py:247

commit v3 on v2

v3 whole, which is shorter than its diff:
```python
import functools
import math

import jax
import jax.numpy as jnp
import ml_dtypes
import numpy as np
from jax import lax
from jax.experimental import pallas as pl
from jax.experimental.pallas import tpu as pltpu
from jax.sharding import PartitionSpec as P

LANES = 128
SUBLANES = 8
CHUNKS = 2
BF16 = jnp.bfloat16
F32 = jnp.float32


def halves(table):
    high = table.astype(np.float32).astype(ml_dtypes.bfloat16)
    low = (table - high.astype(np.float64)).astype(np.float32).astype(ml_dtypes.bfloat16)
    return high, low


def tables(shards_of, total_len):
    blocks = total_len // LANES
    per_shard = blocks // shards_of
    k = np.arange(blocks)[:, None]
    a = np.arange(blocks)[None, :]
    angle = np.pi * (2 * k + 1) * a / (2 * blocks)
    outer = np.concatenate([np.cos(angle), -np.sin(angle)], axis=0)
    inverse = np.concatenate([np.cos(angle).T, -np.sin(angle).T], axis=1) / total_len
    filter_inverse = inverse / math.sqrt(total_len)
    order = [
        np.concatenate(
            [np.arange(per_shard) + (me ^ d) * per_shard for d in range(shards_of)]
        )
        for me in range(shards_of)
    ]

    def wide(table):
        high, low = halves(table)
        return np.concatenate([high, high, low], axis=1)

    outer_w = np.stack([wide(outer[:, o]) for o in order])
    inverse_w = np.stack([wide(inverse[o]) for o in order])
    filter_w = np.stack([wide(filter_inverse[o]) for o in order])
    b = np.arange(LANES)[None, :]
    turn = np.pi * (2 * k + 1) * b / (2 * total_len)
    twiddle = np.stack([np.cos(turn), np.sin(turn)]).astype(np.float32)
    q = np.arange(LANES)
    inner = 2 * np.pi * (q[:, None] * q[None, :] % LANES) / LANES
    dft = np.block([[np.cos(inner), -np.sin(inner)], [np.sin(inner), np.cos(inner)]])
    dft_high, dft_low = halves(dft)
    return outer_w, inverse_w, filter_w, twiddle, np.concatenate([dft_high, dft_high, dft_low])


def triple(x, axis):
    high = x.astype(BF16)
    low = (x - high.astype(F32)).astype(BF16)
    return jnp.concatenate([high, low, high], axis=axis)


def matmul(a, b):
    return jnp.dot(a, b, preferred_element_type=F32)


def pack_kernel(shards_of, chunks, *refs):
    sources = refs[:5]
    outs = refs[5 : 5 + chunks * shards_of]
    post, pre, signal, cotangent, taps, gated, d_conved, sems = refs[5 + chunks * shards_of :]
    copies = [
        pltpu.make_async_copy(source, held, sems.at[i])
        for i, (source, held) in enumerate(zip(sources, (post, pre, signal, cotangent, taps)))
    ]
    for copy in copies:
        copy.start()
    for copy in copies:
        copy.wait()
    me = lax.axis_index("seq")
    channels, length = post.shape
    chunk_rows = channels // chunks
    width = chunk_rows // shards_of
    per = length // LANES
    field_rows = width * per
    parts = []
    for c in range(0, channels, 16):
        rows = slice(c, c + 16)
        g = pre[rows, :].astype(F32) * signal[rows, :].astype(F32)
        dc = cotangent[rows, :].astype(F32) * post[rows, :].astype(F32)
        gated[rows, :] = g
        d_conved[rows, :] = dc
        prod = g * dc
        parts.append(sum(prod[:, a * LANES : (a + 1) * LANES] for a in range(per)))
    folded = jnp.concatenate(parts + [jnp.zeros((LANES - channels, LANES), F32)], axis=0)
    skip = jnp.sum(folded.T, axis=0, keepdims=True)
    for q in range(chunks):
        for d in range(shards_of):
            out = outs[q * shards_of + d]
            top = q * chunk_rows + (me ^ d) * width
            for f, field in enumerate((taps, gated, d_conved)):
                for c in range(0, width, SUBLANES):
                    rows = pl.ds(pl.multiple_of(top + c, SUBLANES), SUBLANES)
                    for a in range(per):
                        out[pl.ds(f * field_rows + c * per + a, SUBLANES, stride=per), :] = field[
                            rows, a * LANES : (a + 1) * LANES
                        ]
            if q == 0:
                out[3 * field_rows :, :] = jnp.broadcast_to(skip, (SUBLANES, LANES))


def spectral_kernel(shards_of, chunks, q, channels, per, *refs):
    skip_gain, outer_w, inverse_w, filter_w, twiddle, dft = refs[:6]
    pieces = refs[6 : 6 + shards_of]
    outs = refs[6 + shards_of : 6 + 2 * shards_of]
    rest = refs[6 + 2 * shards_of :]
    if q == 0:
        d_skip, *rest = rest
    spectra, packed = rest
    me = lax.axis_index("seq")
    chunk_rows = channels // chunks
    width = chunk_rows // shards_of
    blocks = shards_of * per
    field_rows = width * per
    spectrum_rows = width * blocks
    cos_t = twiddle[0]
    sin_t = twiddle[1]
    forward = outer_w[me]
    back = (inverse_w[me], inverse_w[me], filter_w[me])
    if q == 0:
        skips = sum(pieces[d][3 * field_rows : 3 * field_rows + 1, :] for d in range(shards_of))
        d_skip[...] = skips[:, : d_skip.shape[1]] * (1.0 / math.sqrt(blocks * LANES))

    def held(f, ch):
        start = f * field_rows + ch * per
        return jnp.concatenate([pieces[d][start : start + per, :] for d in range(shards_of)], axis=0)

    def spectrum(f, ch):
        start = f * spectrum_rows + ch * blocks
        return slice(start, start + blocks)

    def inner(f):
        rows = slice(f * spectrum_rows, (f + 1) * spectrum_rows)
        spectra[rows, :] = matmul(packed[rows, :], dft[...])

    for f in range(3):
        for c in range(0, width, 2):
            x = jnp.concatenate([held(f, c), held(f, c + 1)], axis=1)
            mixed = matmul(forward, triple(x, 0))
            for i in range(2):
                real = mixed[:blocks, i * LANES : (i + 1) * LANES]
                imag = mixed[blocks:, i * LANES : (i + 1) * LANES]
                turned = [real * cos_t + imag * sin_t, imag * cos_t - real * sin_t]
                packed[spectrum(f, c + i), :] = triple(jnp.concatenate(turned, axis=1), 1)
    for f in range(3):
        inner(f)
    for ch in range(width):
        tr, ti = spectra[spectrum(0, ch), :LANES], spectra[spectrum(0, ch), LANES:]
        gr, gi = spectra[spectrum(1, ch), :LANES], spectra[spectrum(1, ch), LANES:]
        dr, di = spectra[spectrum(2, ch), :LANES], spectra[spectrum(2, ch), LANES:]
        tr = tr + skip_gain[q * chunk_rows + me * width + ch]
        products = (
            (gr * tr - gi * ti, gr * ti + gi * tr),
            (tr * dr + ti * di, tr * di - ti * dr),
            (gr * dr + gi * di, gr * di - gi * dr),
        )
        for f, (real, imag) in enumerate(products):
            packed[spectrum(f, ch), :] = triple(jnp.concatenate([imag, real], axis=1), 1)
    for f in range(3):
        inner(f)
    for f in range(3):
        for c in range(0, width, 2):
            turned = []
            for ch in (c, c + 1):
                imag, real = spectra[spectrum(f, ch), :LANES], spectra[spectrum(f, ch), LANES:]
                both = [real * cos_t - imag * sin_t, imag * cos_t + real * sin_t]
                turned.append(jnp.concatenate(both, axis=0))
            y = matmul(back[f], triple(jnp.concatenate(turned, axis=1), 0))
            for i in range(2):
                start = f * field_rows + (c + i) * per
                for d in range(shards_of):
                    outs[d][start : start + per, :] = y[
                        d * per : (d + 1) * per, i * LANES : (i + 1) * LANES
                    ]


def gate_kernel(shards_of, chunks, *refs):
    post, pre, signal, cotangent = refs[:4]
    pieces = refs[4 : 4 + chunks * shards_of]
    refs = refs[4 + chunks * shards_of :]
    outs, (fields, output, d_post, d_pre, d_signal, sems) = refs[:5], refs[5:]
    me = lax.axis_index("seq")
    channels, length = post.shape
    chunk_rows = channels // chunks
    width = chunk_rows // shards_of
    per = length // LANES
    field_rows = width * per
    copies = []

    def ship(q, i, held):
        rows = pl.ds(q * chunk_rows, chunk_rows)
        copy = pltpu.make_async_copy(held.at[rows, :], outs[i].at[rows, :], sems.at[q, i])
        copy.start()
        copies.append(copy)

    def gather(q, f):
        for d in range(shards_of):
            for c in range(0, width, SUBLANES):
                top = q * chunk_rows + (me ^ d) * width + c
                held = pl.ds(pl.multiple_of(top, SUBLANES), SUBLANES)
                for a in range(per):
                    fields[f, held, a * LANES : (a + 1) * LANES] = pieces[q * shards_of + d][
                        pl.ds(f * field_rows + c * per + a, SUBLANES, stride=per), :
                    ]

    for q in range(chunks):
        rows = slice(q * chunk_rows, (q + 1) * chunk_rows)
        gather(q, 2)
        ship(q, 4, fields.at[2])
        gather(q, 0)
        conved = fields[0, rows, :]
        output[rows, :] = (post[rows, :].astype(F32) * conved).astype(BF16)
        ship(q, 0, output)
        d_post[rows, :] = (cotangent[rows, :].astype(F32) * conved).astype(BF16)
        ship(q, 1, d_post)
        gather(q, 1)
        d_gated = fields[1, rows, :]
        d_pre[rows, :] = (signal[rows, :].astype(F32) * d_gated).astype(BF16)
        ship(q, 2, d_pre)
        d_signal[rows, :] = (pre[rows, :].astype(F32) * d_gated).astype(BF16)
        ship(q, 3, d_signal)
    for copy in copies:
        copy.wait()


def shards(post_gate, pre_gate, signal, cotangent, filter_taps, skip_gain):
    shards_of = lax.axis_size("seq")
    channels, length = post_gate.shape
    chunks = CHUNKS if channels % (CHUNKS * shards_of * SUBLANES) == 0 else 1
    chunk_rows = channels // chunks
    width = chunk_rows // shards_of
    per = length // LANES
    field_rows = width * per
    total_len = shards_of * length
    vmem = pl.BlockSpec(memory_space=pltpu.VMEM)
    hbm = pl.BlockSpec(memory_space=pltpu.HBM)
    params = pltpu.CompilerParams(vmem_limit_bytes=48 * 2**20)

    def swap(pieces):
        moved = {
            d: lax.ppermute(pieces[d], "seq", [(i, i ^ d) for i in range(shards_of)])
            for d in reversed(range(1, shards_of))
        }
        return [pieces[0]] + [moved[d] for d in range(1, shards_of)]

    def rows(count):
        return [jax.ShapeDtypeStruct((count, LANES), F32)] * shards_of

    packed = pl.pallas_call(
        functools.partial(pack_kernel, shards_of, chunks),
        out_shape=rows(3 * field_rows + SUBLANES) + rows(3 * field_rows) * (chunks - 1),
        in_specs=[hbm] * 5,
        out_specs=[vmem] * (chunks * shards_of),
        scratch_shapes=[pltpu.VMEM((channels, length), BF16)] * 4
        + [pltpu.VMEM((channels, length), F32)] * 3
        + [pltpu.SemaphoreType.DMA((5,))],
        compiler_params=params,
    )(
        *(
            pltpu.with_memory_space_constraint(x, pltpu.HBM)
            for x in (post_gate, pre_gate, signal, cotangent, filter_taps)
        )
    )
    arrived = [swap(packed[q * shards_of : (q + 1) * shards_of]) for q in range(chunks)]
    consts = [jnp.asarray(t) for t in tables(shards_of, total_len)]
    spectrum_rows = width * shards_of * per
    back = []
    for q in range(chunks):
        mixed = pl.pallas_call(
            functools.partial(spectral_kernel, shards_of, chunks, q, channels, per),
            out_shape=rows(3 * field_rows)
            + [jax.ShapeDtypeStruct((1, channels), F32)] * (q == 0),
            in_specs=[pl.BlockSpec(memory_space=pltpu.SMEM)] + [vmem] * (5 + shards_of),
            out_specs=[vmem] * (shards_of + (q == 0)),
            scratch_shapes=[
                pltpu.VMEM((3 * spectrum_rows, 2 * LANES), F32),
                pltpu.VMEM((3 * spectrum_rows, 6 * LANES), BF16),
            ],
            compiler_params=params,
        )(skip_gain, *consts, *arrived[q])
        if q == 0:
            d_skip = mixed[shards_of]
        back += swap(mixed[:shards_of])
    output, d_post, d_pre, d_signal, d_filter = pl.pallas_call(
        functools.partial(gate_kernel, shards_of, chunks),
        out_shape=[pltpu.HBM((channels, length), BF16)] * 4 + [pltpu.HBM((channels, length), F32)],
        in_specs=[vmem] * (4 + chunks * shards_of),
        out_specs=[hbm] * 5,
        scratch_shapes=[pltpu.VMEM((3, channels, length), F32)]
        + [pltpu.VMEM((channels, length), BF16)] * 4
        + [pltpu.SemaphoreType.DMA((chunks, 5))],
        compiler_params=params,
    )(post_gate, pre_gate, signal, cotangent, *back)
    return (output, d_post, d_pre, d_signal, d_skip.reshape(channels), d_filter)


def solution(mesh):
    both = P("chan", "seq")
    return jax.shard_map(
        shards,
        mesh=mesh,
        in_specs=(both,) * 5 + (P("chan"),),
        out_specs=(both,) * 4 + (P("chan"), both),
        check_vma=False,
    )
```

time: 30.3 us -> 29.1 us (0.960)
  Pallas kernels: 7.63 us -> 6.5 us
    pallas_call x2, Pallas kernels: 5.06 us -> 3.94 us  [shards(): pl.pallas_call(functools.partial(spectral_kernel, shards_of, chunks, q, c...]
  transfers between devices with their start and end apart: 12 -> 12, of which waited for: 5 -> 5; matrix products, arithmetic and copies ran while one was open for 0% -> 0% of each run, Pallas kernels for 17% -> 14%
where the time goes in v3:
time: 29.1 us; the launch traced here: 29 us
  starting transfers between devices  16.4 us (56%)
  Pallas kernels  6.5 us (22%)
  waiting for transfers between devices  5.32 us (18%)
  between operations  0.76 us (3%)
    ppermute x12, starting transfers between devices, swap(): lax.ppermute(pieces[d], 'seq', [(i, i ^ d) for i in range(shards_of)])  16.4 us
    ppermute x12, waiting for transfers between devices, swap(): lax.ppermute(pieces[d], 'seq', [(i, i ^ d) for i in range(shards_of)])  5.32 us
    pallas_call x2, Pallas kernels, shards(): pl.pallas_call(functools.partial(spectral_kernel, shards_of, chunks, q, c...  3.94 us
    pallas_call x1, Pallas kernels, shards(): pl.pallas_call(functools.partial(pack_kernel, shards_of, chunks), out_sha...  1.57 us
    pallas_call x1, Pallas kernels, shards(): pl.pallas_call(functools.partial(gate_kernel, shards_of, chunks), out_sha...  0.99 us
  transfers between devices with their start and end apart: 12, of which 5 were waited for; matrix products, arithmetic and copies ran while one was open for 0% of the time, Pallas kernels for 14%

profile of v3, /device:TPU:0, one launch (start us, length us, event | category | flops | bytes accessed | tf_op | source)
XLA Modules:
  0.0 29.0 jit_solution(16961298725241720699)
XLA Ops:
  0.6 0.0 copy-start
  0.6 0.0 copy-start.5
  0.7 0.0 copy-start.6
  0.7 0.0 copy-start.7
  0.7 0.0 copy-start.8
  0.7 1.6 %shard_map.154 = (f32[200,128]{1,0:T(8,128)S(1)}, f32[200,128]{1,0:T(8,128)S(1)}, f32[200,128]{1,0:T(8,128)S(1)}, f32[200,128]{1,0:T(8,128)S(1)}, f32[192,128]{1...) custom-call(bf16[64,1024]{1,0:T(8,128)(2,1)} %refs_0_.7, ...), custom_call_target="tpu_custom_call" | custom-call | tf_op jit(solution)/shard_map/pallas_call | solution.py:260
  2.3 3.0 %collective-permute-start.6 = (f32[192,128]{1,0:T(8,128)S(1)}, f32[192,128]{1,0:T(8,128)S(1)}, u32[]{:S(2)}, u32[]{:S(2)}) collective-permute-start(f32[192,128]{1,0:T(8,128)S(1)} %get-tuple-element.37), channel_id=1, source_target_pairs={{0,8},{8,0},{16,24},{24,16},{1,9},{9,1},{17,25},{25,17},{2,10},{10... | collective-permute-start | bytes 294920 | tf_op jit(solution)/shard_map/ppermute | solution.py:252
  5.3 1.5 %collective-permute-start.7 = (f32[192,128]{1,0:T(8,128)S(1)}, f32[192,128]{1,0:T(8,128)S(1)}, u32[]{:S(2)}, u32[]{:S(2)}) collective-permute-start(f32[192,128]{1,0:T(8,128)S(1)} %get-tuple-element.38), channel_id=1, source_target_pairs={{0,16},{8,24},{16,0},{24,8},{1,17},{9,25},{17,1},{25,9},{2,18},{10... | collective-permute-start | bytes 294920 | tf_op jit(solution)/shard_map/ppermute | solution.py:252
  6.8 0.0 collective-permute-start.8
  6.8 1.9 %collective-permute-start = (f32[200,128]{1,0:T(8,128)S(1)}, f32[200,128]{1,0:T(8,128)S(1)}, u32[]{:S(2)}, u32[]{:S(2)}) collective-permute-start(f32[200,128]{1,0:T(8,128)S(1)} %get-tuple-element.29), channel_id=1, source_target_pairs={{0,8},{8,0},{16,24},{24,16},{1,9},{9,1},{17,25},{25,17},{2,10},{10... | collective-permute-start | bytes 307208 | tf_op jit(solution)/shard_map/ppermute | solution.py:252
  8.8 1.5 %collective-permute-start.1 = (f32[200,128]{1,0:T(8,128)S(1)}, f32[200,128]{1,0:T(8,128)S(1)}, u32[]{:S(2)}, u32[]{:S(2)}) collective-permute-start(f32[200,128]{1,0:T(8,128)S(1)} %get-tuple-element.30), channel_id=1, source_target_pairs={{0,16},{8,24},{16,0},{24,8},{1,17},{9,25},{17,1},{25,9},{2,18},{10... | collective-permute-start | bytes 307208 | tf_op jit(solution)/shard_map/ppermute | solution.py:252
  10.3 0.0 collective-permute-done.6.refs_7_
  10.3 0.0 copy-start.9
  10.3 1.3 %collective-permute-start.2 = (f32[200,128]{1,0:T(8,128)S(1)}, f32[200,128]{1,0:T(8,128)S(1)}, u32[]{:S(2)}, u32[]{:S(2)}) collective-permute-start(f32[200,128]{1,0:T(8,128)S(1)} %get-tuple-element.31), channel_id=1, source_target_pairs={{0,24},{8,16},{16,8},{24,0},{1,25},{9,17},{17,9},{25,1},{2,26},{10... | collective-permute-start | bytes 307208 | tf_op jit(solution)/shard_map/ppermute | solution.py:252
  11.6 0.2 collective-permute-done.7.refs_8_
  11.8 1.7 %collective-permute-done.8.refs_9_ = f32[192,128]{1,0:T(8,128)S(1)} collective-permute-done((f32[192,128]{1,0:T(8,128)S(1)}, f32[192,128]{1,0:T(8,128)S(1)}, u32[]{:S(2)}, u32[]{:S(2)}) %collective-permute-start.8) | collective-permute-done | bytes 98336 | tf_op jit(solution)/shard_map/ppermute | solution.py:252
  13.5 0.0 copy-done
  13.5 0.0 copy-done.5
  13.5 0.0 copy-done.6
  13.5 0.0 copy-done.7
  13.5 0.0 copy-done.8
  13.5 0.0 copy-done.9
  13.6 1.8 %shard_map.156 = (f32[192,128]{1,0:T(8,128)S(1)}, f32[192,128]{1,0:T(8,128)S(1)}, f32[192,128]{1,0:T(8,128)S(1)}, f32[192,128]{1,0:T(8,128)S(1)}) custom-call(f32[64]{0:T(128)S(1)} %copy-done.9, bf16[4,64,96]{2,1,0:T(8,128)(2,1)S(1)} %copy-done.7, bf16[4,32,192]{2,1,0:T(8,128)(2,1)S(1)} %copy-done.6, bf16[4,32,192]{2,1,0:T(8,128)(2,1)S(1)} %copy-done.5, ...), custom_call_target="tpu_custom_call" | custom-call | tf_op jit(solution)/shard_map/pallas_call | solution.py:280
  15.3 0.5 %collective-permute-start.9 = (f32[192,128]{1,0:T(8,128)S(1)}, f32[192,128]{1,0:T(8,128)S(1)}, u32[]{:S(2)}, u32[]{:S(2)}) collective-permute-start(f32[192,128]{1,0:T(8,128)S(1)} %get-tuple-element.41), channel_id=1, source_target_pairs={{0,8},{8,0},{16,24},{24,16},{1,9},{9,1},{17,25},{25,17},{2,10},{10... | collective-permute-start | bytes 294920 | tf_op jit(solution)/shard_map/ppermute | solution.py:252
  15.8 0.9 %collective-permute-start.10 = (f32[192,128]{1,0:T(8,128)S(1)}, f32[192,128]{1,0:T(8,128)S(1)}, u32[]{:S(2)}, u32[]{:S(2)}) collective-permute-start(f32[192,128]{1,0:T(8,128)S(1)} %get-tuple-element.42), channel_id=1, source_target_pairs={{0,16},{8,24},{16,0},{24,8},{1,17},{9,25},{17,1},{25,9},{2,18},{10... | collective-permute-start | bytes 294920 | tf_op jit(solution)/shard_map/ppermute | solution.py:252
  16.8 0.0 collective-permute-done.refs_7_
  16.8 2.1 %collective-permute-start.11 = (f32[192,128]{1,0:T(8,128)S(1)}, f32[192,128]{1,0:T(8,128)S(1)}, u32[]{:S(2)}, u32[]{:S(2)}) collective-permute-start(f32[192,128]{1,0:T(8,128)S(1)} %get-tuple-element.43), channel_id=1, source_target_pairs={{0,24},{8,16},{16,8},{24,0},{1,25},{9,17},{17,9},{25,1},{2,26},{10... | collective-permute-start | bytes 294920 | tf_op jit(solution)/shard_map/ppermute | solution.py:252
  18.9 0.0 collective-permute-done.1.refs_8_
  18.9 0.0 collective-permute-done.2.refs_9_
  18.9 0.0 copy-start.1
  18.9 0.0 copy-start.2
  18.9 0.0 copy-start.3
  18.9 0.0 copy-start.4
  18.9 2.2 %shard_map.155 = (f32[192,128]{1,0:T(8,128)S(1)}, f32[192,128]{1,0:T(8,128)S(1)}, f32[192,128]{1,0:T(8,128)S(1)}, f32[192,128]{1,0:T(8,128)S(1)}, f32[1,64]{1,0:T(1,128)}) custom-call(f32[64]{0:T(128)S(1)} %copy-done.9, bf16[4,64,96]{2,1,0:T(8,128)(2,1)S(1)} %copy-done.7, bf16[4,32,192]{2,1,0:T(8,128)(2,1)S(1)} %copy-done.6, ...), custom_call_target="tpu_custom_call" | custom-call | tf_op jit(solution)/shard_map/pallas_call | solution.py:280
  21.1 0.5 %collective-permute-start.3 = (f32[192,128]{1,0:T(8,128)S(1)}, f32[192,128]{1,0:T(8,128)S(1)}, u32[]{:S(2)}, u32[]{:S(2)}) collective-permute-start(f32[192,128]{1,0:T(8,128)S(1)} %get-tuple-element.33), channel_id=1, source_target_pairs={{0,8},{8,0},{16,24},{24,16},{1,9},{9,1},{17,25},{25,17},{2,10},{10... | collective-permute-start | bytes 294920 | tf_op jit(solution)/shard_map/ppermute | solution.py:252
  21.6 0.9 %collective-permute-start.4 = (f32[192,128]{1,0:T(8,128)S(1)}, f32[192,128]{1,0:T(8,128)S(1)}, u32[]{:S(2)}, u32[]{:S(2)}) collective-permute-start(f32[192,128]{1,0:T(8,128)S(1)} %get-tuple-element.34), channel_id=1, source_target_pairs={{0,16},{8,24},{16,0},{24,8},{1,17},{9,25},{17,1},{25,9},{2,18},{10... | collective-permute-start | bytes 294920 | tf_op jit(solution)/shard_map/ppermute | solution.py:252
  22.5 0.0 collective-permute-done.9.refs_9_
  22.5 2.1 %collective-permute-start.5 = (f32[192,128]{1,0:T(8,128)S(1)}, f32[192,128]{1,0:T(8,128)S(1)}, u32[]{:S(2)}, u32[]{:S(2)}) collective-permute-start(f32[192,128]{1,0:T(8,128)S(1)} %get-tuple-element.35), channel_id=1, source_target_pairs={{0,24},{8,16},{16,8},{24,0},{1,25},{9,17},{17,9},{25,1},{2,26},{10... | collective-permute-start | bytes 294920 | tf_op jit(solution)/shard_map/ppermute | solution.py:252
  24.6 0.0 collective-permute-done.10.refs_10_
  24.6 0.0 collective-permute-done.11.refs_11_
  24.6 1.1 %collective-permute-done.3.refs_5_ = f32[192,128]{1,0:T(8,128)S(1)} collective-permute-done((f32[192,128]{1,0:T(8,128)S(1)}, f32[192,128]{1,0:T(8,128)S(1)}, u32[]{:S(2)}, u32[]{:S(2)}) %collective-permute-start.3) | collective-permute-done | bytes 98336 | tf_op jit(solution)/shard_map/ppermute | solution.py:252
  25.7 0.5 %collective-permute-done.4.refs_6_ = f32[192,128]{1,0:T(8,128)S(1)} collective-permute-done((f32[192,128]{1,0:T(8,128)S(1)}, f32[192,128]{1,0:T(8,128)S(1)}, u32[]{:S(2)}, u32[]{:S(2)}) %collective-permute-start.4) | collective-permute-done | bytes 98336 | tf_op jit(solution)/shard_map/ppermute | solution.py:252
  26.2 1.8 %collective-permute-done.5.refs_7_ = f32[192,128]{1,0:T(8,128)S(1)} collective-permute-done((f32[192,128]{1,0:T(8,128)S(1)}, f32[192,128]{1,0:T(8,128)S(1)}, u32[]{:S(2)}, u32[]{:S(2)}) %collective-permute-start.5) | collective-permute-done | bytes 98336 | tf_op jit(solution)/shard_map/ppermute | solution.py:252
  28.0 0.0 copy-done.1
  28.0 0.0 copy-done.2
  28.0 0.0 copy-done.3
  28.0 0.0 copy-done.4
  28.0 1.0 %shard_map.157 = (bf16[64,1024]{1,0:T(8,128)(2,1)}, bf16[64,1024]{1,0:T(8,128)(2,1)}, bf16[64,1024]{1,0:T(8,128)(2,1)}, bf16[64,1024]{1,0:T(8,128)(2,1)}, f32[64,1024]{1,0:T(8,128)}) custom-call(bf16[64,1024]{1,0:T(8,128)(2,1)S(1)} %copy-done.1, bf16[64,1024]{1,0:T(8,128)(2,1)S(1)} %copy-done.2, bf16[64,1024]{1,0:T(8,128)(2,1)S(1)} %copy-done.3, ...), custom_call_target="tpu_custom_call" | custom-call | tf_op jit(solution)/shard_map/pallas_call | solution.py:295
Async XLA Ops:
  0.6 12.9 %copy-start = (bf16[768,256]{1,0:T(8,128)(2,1)S(1)}, bf16[768,256]{1,0:T(8,128)(2,1)}, u32[]{:S(2)}) copy-start(bf16[768,256]{1,0:T(8,128)(2,1)} %constant.14.clone.refs_5_) | copy-start | bytes 1179652
  0.6 12.9 %copy-start.5 = (bf16[4,32,192]{2,1,0:T(8,128)(2,1)S(1)}, bf16[4,32,192]{2,1,0:T(8,128)(2,1)}, u32[]{:S(2)}) copy-start(bf16[4,32,192]{2,1,0:T(8,128)(2,1)} %constant.12.clone.refs_3_) | copy-start | bytes 147460
  0.7 12.9 %copy-start.6 = (bf16[4,32,192]{2,1,0:T(8,128)(2,1)S(1)}, bf16[4,32,192]{2,1,0:T(8,128)(2,1)}, u32[]{:S(2)}) copy-start(bf16[4,32,192]{2,1,0:T(8,128)(2,1)} %constant.11.clone.refs_2_) | copy-start | bytes 147460
  0.7 12.9 %copy-start.7 = (bf16[4,64,96]{2,1,0:T(8,128)(2,1)S(1)}, bf16[4,64,96]{2,1,0:T(8,128)(2,1)}, u32[]{:S(2)}) copy-start(bf16[4,64,96]{2,1,0:T(8,128)(2,1)} %constant.10.clone.refs_1_) | copy-start | bytes 147460
  0.7 12.9 %copy-start.8 = (f32[2,32,128]{2,1,0:T(8,128)S(1)}, f32[2,32,128]{2,1,0:T(8,128)}, u32[]{:S(2)}) copy-start(f32[2,32,128]{2,1,0:T(8,128)} %constant.13.clone.refs_4_) | copy-start | bytes 98308
  2.3 8.0 %collective-permute-start.6 = (f32[192,128]{1,0:T(8,128)S(1)}, f32[192,128]{1,0:T(8,128)S(1)}, u32[]{:S(2)}, u32[]{:S(2)}) collective-permute-start(f32[192,128]{1,0:T(8,128)S(1)} %get-tuple-element.37), channel_id=1, source_target_pairs={{0,8},{8,0},{16,24},{24,16},{1,9},{9,1},{17,25},{25,17},{2,10},{10... | collective-permute-start | bytes 294920 | tf_op jit(solution)/shard_map/ppermute | solution.py:252
  5.3 6.5 %collective-permute-start.7 = (f32[192,128]{1,0:T(8,128)S(1)}, f32[192,128]{1,0:T(8,128)S(1)}, u32[]{:S(2)}, u32[]{:S(2)}) collective-permute-start(f32[192,128]{1,0:T(8,128)S(1)} %get-tuple-element.38), channel_id=1, source_target_pairs={{0,16},{8,24},{16,0},{24,8},{1,17},{9,25},{17,1},{25,9},{2,18},{10... | collective-permute-start | bytes 294920 | tf_op jit(solution)/shard_map/ppermute | solution.py:252
  6.8 6.7 %collective-permute-start.8 = (f32[192,128]{1,0:T(8,128)S(1)}, f32[192,128]{1,0:T(8,128)S(1)}, u32[]{:S(2)}, u32[]{:S(2)}) collective-permute-start(f32[192,128]{1,0:T(8,128)S(1)} %get-tuple-element.39), channel_id=1, source_target_pairs={{0,24},{8,16},{16,8},{24,0},{1,25},{9,17},{17,9},{25,1},{2,26},{10... | collective-permute-start | bytes 294920 | tf_op jit(solution)/shard_map/ppermute | solution.py:252
  6.8 9.9 %collective-permute-start = (f32[200,128]{1,0:T(8,128)S(1)}, f32[200,128]{1,0:T(8,128)S(1)}, u32[]{:S(2)}, u32[]{:S(2)}) collective-permute-start(f32[200,128]{1,0:T(8,128)S(1)} %get-tuple-element.29), channel_id=1, source_target_pairs={{0,8},{8,0},{16,24},{24,16},{1,9},{9,1},{17,25},{25,17},{2,10},{10... | collective-permute-start | bytes 307208 | tf_op jit(solution)/shard_map/ppermute | solution.py:252
  8.8 10.1 %collective-permute-start.1 = (f32[200,128]{1,0:T(8,128)S(1)}, f32[200,128]{1,0:T(8,128)S(1)}, u32[]{:S(2)}, u32[]{:S(2)}) collective-permute-start(f32[200,128]{1,0:T(8,128)S(1)} %get-tuple-element.30), channel_id=1, source_target_pairs={{0,16},{8,24},{16,0},{24,8},{1,17},{9,25},{17,1},{25,9},{2,18},{10... | collective-permute-start | bytes 307208 | tf_op jit(solution)/shard_map/ppermute | solution.py:252
  10.3 3.3 %copy-start.9 = (f32[64]{0:T(128)S(1)}, f32[64]{0:T(128)}, u32[]{:S(2)}) copy-start(f32[64]{0:T(128)} %refs_0_.6) | copy-start | bytes 772
  10.3 8.6 %collective-permute-start.2 = (f32[200,128]{1,0:T(8,128)S(1)}, f32[200,128]{1,0:T(8,128)S(1)}, u32[]{:S(2)}, u32[]{:S(2)}) collective-permute-start(f32[200,128]{1,0:T(8,128)S(1)} %get-tuple-element.31), channel_id=1, source_target_pairs={{0,24},{8,16},{16,8},{24,0},{1,25},{9,17},{17,9},{25,1},{2,26},{10... | collective-permute-start | bytes 307208 | tf_op jit(solution)/shard_map/ppermute | solution.py:252
  15.3 7.1 %collective-permute-start.9 = (f32[192,128]{1,0:T(8,128)S(1)}, f32[192,128]{1,0:T(8,128)S(1)}, u32[]{:S(2)}, u32[]{:S(2)}) collective-permute-start(f32[192,128]{1,0:T(8,128)S(1)} %get-tuple-element.41), channel_id=1, source_target_pairs={{0,8},{8,0},{16,24},{24,16},{1,9},{9,1},{17,25},{25,17},{2,10},{10... | collective-permute-start | bytes 294920 | tf_op jit(solution)/shard_map/ppermute | solution.py:252
  15.8 8.7 %collective-permute-start.10 = (f32[192,128]{1,0:T(8,128)S(1)}, f32[192,128]{1,0:T(8,128)S(1)}, u32[]{:S(2)}, u32[]{:S(2)}) collective-permute-start(f32[192,128]{1,0:T(8,128)S(1)} %get-tuple-element.42), channel_id=1, source_target_pairs={{0,16},{8,24},{16,0},{24,8},{1,17},{9,25},{17,1},{25,9},{2,18},{10... | collective-permute-start | bytes 294920 | tf_op jit(solution)/shard_map/ppermute | solution.py:252
  16.8 7.8 %collective-permute-start.11 = (f32[192,128]{1,0:T(8,128)S(1)}, f32[192,128]{1,0:T(8,128)S(1)}, u32[]{:S(2)}, u32[]{:S(2)}) collective-permute-start(f32[192,128]{1,0:T(8,128)S(1)} %get-tuple-element.43), channel_id=1, source_target_pairs={{0,24},{8,16},{16,8},{24,0},{1,25},{9,17},{17,9},{25,1},{2,26},{10... | collective-permute-start | bytes 294920 | tf_op jit(solution)/shard_map/ppermute | solution.py:252
  18.9 9.1 %copy-start.1 = (bf16[64,1024]{1,0:T(8,128)(2,1)S(1)}, bf16[64,1024]{1,0:T(8,128)(2,1)}, u32[]{:S(2)}) copy-start(bf16[64,1024]{1,0:T(8,128)(2,1)} %refs_0_.7) | copy-start | bytes 393220
  18.9 9.1 %copy-start.2 = (bf16[64,1024]{1,0:T(8,128)(2,1)S(1)}, bf16[64,1024]{1,0:T(8,128)(2,1)}, u32[]{:S(2)}) copy-start(bf16[64,1024]{1,0:T(8,128)(2,1)} %refs_1_.5) | copy-start | bytes 393220
  18.9 9.1 %copy-start.3 = (bf16[64,1024]{1,0:T(8,128)(2,1)S(1)}, bf16[64,1024]{1,0:T(8,128)(2,1)}, u32[]{:S(2)}) copy-start(bf16[64,1024]{1,0:T(8,128)(2,1)} %refs_2_.5) | copy-start | bytes 393220
  18.9 9.1 %copy-start.4 = (bf16[64,1024]{1,0:T(8,128)(2,1)S(1)}, bf16[64,1024]{1,0:T(8,128)(2,1)}, u32[]{:S(2)}) copy-start(bf16[64,1024]{1,0:T(8,128)(2,1)} %refs_3_.5) | copy-start | bytes 393220
  21.1 4.6 %collective-permute-start.3 = (f32[192,128]{1,0:T(8,128)S(1)}, f32[192,128]{1,0:T(8,128)S(1)}, u32[]{:S(2)}, u32[]{:S(2)}) collective-permute-start(f32[192,128]{1,0:T(8,128)S(1)} %get-tuple-element.33), channel_id=1, source_target_pairs={{0,8},{8,0},{16,24},{24,16},{1,9},{9,1},{17,25},{25,17},{2,10},{10... | collective-permute-start | bytes 294920 | tf_op jit(solution)/shard_map/ppermute | solution.py:252
  21.6 4.6 %collective-permute-start.4 = (f32[192,128]{1,0:T(8,128)S(1)}, f32[192,128]{1,0:T(8,128)S(1)}, u32[]{:S(2)}, u32[]{:S(2)}) collective-permute-start(f32[192,128]{1,0:T(8,128)S(1)} %get-tuple-element.34), channel_id=1, source_target_pairs={{0,16},{8,24},{16,0},{24,8},{1,17},{9,25},{17,1},{25,9},{2,18},{10... | collective-permute-start | bytes 294920 | tf_op jit(solution)/shard_map/ppermute | solution.py:252
  22.5 5.5 %collective-permute-start.5 = (f32[192,128]{1,0:T(8,128)S(1)}, f32[192,128]{1,0:T(8,128)S(1)}, u32[]{:S(2)}, u32[]{:S(2)}) collective-permute-start(f32[192,128]{1,0:T(8,128)S(1)} %get-tuple-element.35), channel_id=1, source_target_pairs={{0,24},{8,16},{16,8},{24,0},{1,25},{9,17},{17,9},{25,1},{2,26},{10... | collective-permute-start | bytes 294920 | tf_op jit(solution)/shard_map/ppermute | solution.py:252

commit v4 on v3

--- a/solution.py
+++ b/solution.py
@@ -66,56 +66,69 @@
     return jnp.dot(a, b, preferred_element_type=F32)
 
 
-def pack_kernel(shards_of, chunks, *refs):
-    sources = refs[:5]
-    outs = refs[5 : 5 + chunks * shards_of]
-    post, pre, signal, cotangent, taps, gated, d_conved, sems = refs[5 + chunks * shards_of :]
-    copies = [
-        pltpu.make_async_copy(source, held, sems.at[i])
-        for i, (source, held) in enumerate(zip(sources, (post, pre, signal, cotangent, taps)))
-    ]
-    for copy in copies:
-        copy.start()
-    for copy in copies:
-        copy.wait()
+def pack_kernel(shards_of, chunks, q, *refs):
+    sources, refs = refs[:6], refs[6:]
+    outs, (fields, *held) = refs[:shards_of], refs[shards_of:]
+    channels, length = sources[0].shape
+    chunk_rows = channels // chunks
+    last = q == chunks - 1
+    if q == 0:
+        *held, sems = held
+        rows = slice(0, chunk_rows)
+        copies = [
+            pltpu.make_async_copy(source.at[rows, :] if i < 5 else source, copied, sems.at[i])
+            for i, (source, copied) in enumerate(zip(sources, held))
+        ]
+        for copy in copies:
+            copy.start()
+        for copy in copies:
+            copy.wait()
+        sources = held
+    post, pre, signal, cotangent, taps, skip_gain = sources
     me = lax.axis_index("seq")
-    channels, length = post.shape
-    chunk_rows = channels // chunks
     width = chunk_rows // shards_of
     per = length // LANES
     field_rows = width * per
+    turn = lax.broadcasted_iota(jnp.int32, (channels, channels), 0)
+    lane = lax.broadcasted_iota(jnp.int32, (channels, channels), 1)
+    gains = jnp.broadcast_to(skip_gain[...], (channels, channels))
+    gain = jnp.sum(jnp.where(turn == lane, gains, 0.0), axis=1, keepdims=True)
+    first = (lax.broadcasted_iota(jnp.int32, (16, LANES), 1) == 0) & (me == 0)
     parts = []
-    for c in range(0, channels, 16):
+    for c in range(0 if last else q * chunk_rows, (q + 1) * chunk_rows, 16):
         rows = slice(c, c + 16)
         g = pre[rows, :].astype(F32) * signal[rows, :].astype(F32)
         dc = cotangent[rows, :].astype(F32) * post[rows, :].astype(F32)
-        gated[rows, :] = g
-        d_conved[rows, :] = dc
-        prod = g * dc
-        parts.append(sum(prod[:, a * LANES : (a + 1) * LANES] for a in range(per)))
-    folded = jnp.concatenate(parts + [jnp.zeros((LANES - channels, LANES), F32)], axis=0)
-    skip = jnp.sum(folded.T, axis=0, keepdims=True)
-    for q in range(chunks):
+        if c >= q * chunk_rows:
+            to = slice(c - q * chunk_rows, c - q * chunk_rows + 16)
+            fields[0, to, :] = taps[rows, :]
+            fields[0, to, :LANES] = taps[rows, :LANES] + jnp.where(first, gain[rows], 0.0)
+            fields[1, to, :] = g
+            fields[2, to, :] = dc
+        if last:
+            prod = g * dc
+            parts.append(sum(prod[:, a * LANES : (a + 1) * LANES] for a in range(per)))
+    for d in range(shards_of):
+        for f in range(3):
+            for c in range(0, width, SUBLANES):
+                rows = pl.ds(pl.multiple_of((me ^ d) * width + c, SUBLANES), SUBLANES)
+                for a in range(per):
+                    outs[d][pl.ds(f * field_rows + c * per + a, SUBLANES, stride=per), :] = fields[
+                        f, rows, a * LANES : (a + 1) * LANES
+                    ]
+    if last:
+        folded = jnp.concatenate(parts + [jnp.zeros((LANES - channels, LANES), F32)], axis=0)
+        skip = jnp.sum(folded.T, axis=0, keepdims=True)
         for d in range(shards_of):
-            out = outs[q * shards_of + d]
-            top = q * chunk_rows + (me ^ d) * width
-            for f, field in enumerate((taps, gated, d_conved)):
-                for c in range(0, width, SUBLANES):
-                    rows = pl.ds(pl.multiple_of(top + c, SUBLANES), SUBLANES)
-                    for a in range(per):
-                        out[pl.ds(f * field_rows + c * per + a, SUBLANES, stride=per), :] = field[
-                            rows, a * LANES : (a + 1) * LANES
-                        ]
-            if q == 0:
-                out[3 * field_rows :, :] = jnp.broadcast_to(skip, (SUBLANES, LANES))
-
-
-def spectral_kernel(shards_of, chunks, q, channels, per, *refs):
-    skip_gain, outer_w, inverse_w, filter_w, twiddle, dft = refs[:6]
-    pieces = refs[6 : 6 + shards_of]
-    outs = refs[6 + shards_of : 6 + 2 * shards_of]
-    rest = refs[6 + 2 * shards_of :]
-    if q == 0:
+            outs[d][3 * field_rows :, :] = jnp.broadcast_to(skip, (SUBLANES, LANES))
+
+
+def spectral_kernel(shards_of, chunks, last, channels, per, *refs):
+    outer_w, inverse_w, filter_w, twiddle, dft = refs[:5]
+    pieces = refs[5 : 5 + shards_of]
+    outs = refs[5 + shards_of : 5 + 2 * shards_of]
+    rest = refs[5 + 2 * shards_of :]
+    if last:
         d_skip, *rest = rest
     spectra, packed = rest
     me = lax.axis_index("seq")
@@ -128,7 +141,7 @@
     sin_t = twiddle[1]
     forward = outer_w[me]
     back = (inverse_w[me], inverse_w[me], filter_w[me])
-    if q == 0:
+    if last:
         skips = sum(pieces[d][3 * field_rows : 3 * field_rows + 1, :] for d in range(shards_of))
         d_skip[...] = skips[:, : d_skip.shape[1]] * (1.0 / math.sqrt(blocks * LANES))
 
@@ -159,7 +172,6 @@
         tr, ti = spectra[spectrum(0, ch), :LANES], spectra[spectrum(0, ch), LANES:]
         gr, gi = spectra[spectrum(1, ch), :LANES], spectra[spectrum(1, ch), LANES:]
         dr, di = spectra[spectrum(2, ch), :LANES], spectra[spectrum(2, ch), LANES:]
-        tr = tr + skip_gain[q * chunk_rows + me * width + ch]
         products = (
             (gr * tr - gi * ti, gr * ti + gi * tr),
             (tr * dr + ti * di, tr * di - ti * dr),
@@ -257,39 +269,41 @@
     def rows(count):
         return [jax.ShapeDtypeStruct((count, LANES), F32)] * shards_of
 
-    packed = pl.pallas_call(
-        functools.partial(pack_kernel, shards_of, chunks),
-        out_shape=rows(3 * field_rows + SUBLANES) + rows(3 * field_rows) * (chunks - 1),
-        in_specs=[hbm] * 5,
-        out_specs=[vmem] * (chunks * shards_of),
-        scratch_shapes=[pltpu.VMEM((channels, length), BF16)] * 4
-        + [pltpu.VMEM((channels, length), F32)] * 3
-        + [pltpu.SemaphoreType.DMA((5,))],
-        compiler_params=params,
-    )(
-        *(
-            pltpu.with_memory_space_constraint(x, pltpu.HBM)
-            for x in (post_gate, pre_gate, signal, cotangent, filter_taps)
-        )
-    )
-    arrived = [swap(packed[q * shards_of : (q + 1) * shards_of]) for q in range(chunks)]
+    arrays = (post_gate, pre_gate, signal, cotangent, filter_taps, skip_gain.reshape(1, channels))
+    arrived = []
+    for q in range(chunks):
+        last = q == chunks - 1
+        scratch = [pltpu.VMEM((3, chunk_rows, length), F32)]
+        if q == 0:
+            scratch += [pltpu.VMEM((chunk_rows, length), BF16)] * 4
+            scratch += [pltpu.VMEM((chunk_rows, length), F32), pltpu.VMEM((1, channels), F32)]
+            scratch += [pltpu.SemaphoreType.DMA((6,))]
+        packed = pl.pallas_call(
+            functools.partial(pack_kernel, shards_of, chunks, q),
+            out_shape=rows(3 * field_rows + SUBLANES * last),
+            in_specs=[hbm if q == 0 else vmem] * 6,
+            out_specs=[vmem] * shards_of,
+            scratch_shapes=scratch,
+            compiler_params=params,
+        )(*(pltpu.with_memory_space_constraint(x, pltpu.HBM) if q == 0 else x for x in arrays))
+        arrived.append(swap(packed))
     consts = [jnp.asarray(t) for t in tables(shards_of, total_len)]
     spectrum_rows = width * shards_of * per
     back = []
     for q in range(chunks):
+        last = q == chunks - 1
         mixed = pl.pallas_call(
-            functools.partial(spectral_kernel, shards_of, chunks, q, channels, per),
-            out_shape=rows(3 * field_rows)
-            + [jax.ShapeDtypeStruct((1, channels), F32)] * (q == 0),
-            in_specs=[pl.BlockSpec(memory_space=pltpu.SMEM)] + [vmem] * (5 + shards_of),
-            out_specs=[vmem] * (shards_of + (q == 0)),
+            functools.partial(spectral_kernel, shards_of, chunks, last, channels, per),
+            out_shape=rows(3 * field_rows) + [jax.ShapeDtypeStruct((1, channels), F32)] * last,
+            in_specs=[vmem] * (5 + shards_of),
+            out_specs=[vmem] * (shards_of + last),
             scratch_shapes=[
                 pltpu.VMEM((3 * spectrum_rows, 2 * LANES), F32),
                 pltpu.VMEM((3 * spectrum_rows, 6 * LANES), BF16),
             ],
             compiler_params=params,
-        )(skip_gain, *consts, *arrived[q])
-        if q == 0:
+        )(*consts, *arrived[q])
+        if last:
             d_skip = mixed[shards_of]
         back += swap(mixed[:shards_of])
     output, d_post, d_pre, d_signal, d_filter = pl.pallas_call(

time: 29.1 us -> 27 us (0.928)
  Pallas kernels: 6.5 us -> 5.23 us
  waiting for transfers between devices: 5.32 us -> 4.72 us
  starting transfers between devices: 16.4 us -> 16.1 us
    pallas_call x3 -> x4, Pallas kernels: 5.51 us -> 4.25 us  [the longest x2 2.79 us: shards(): pl.pallas_call(functools.partial(spectral_kernel, shards_of, chunks, last...]
    ppermute x12, waiting for transfers between devices: 5.32 us -> 4.72 us  [swap(): lax.ppermute(pieces[d], 'seq', [(i, i ^ d) for i in range(shards_of)])]
  transfers between devices with their start and end apart: 12 -> 12, of which waited for: 5 -> 4; matrix products, arithmetic and copies ran while one was open for 0% -> 0% of each run, Pallas kernels for 14% -> 11%
where the time goes in v4:
time: 27 us; the launch traced here: 26.9 us
  starting transfers between devices  16.1 us (60%)
  Pallas kernels  5.23 us (19%)
  waiting for transfers between devices  4.72 us (17%)
  between operations  0.76 us (3%)
    ppermute x12, starting transfers between devices, swap(): lax.ppermute(pieces[d], 'seq', [(i, i ^ d) for i in range(shards_of)])  16.1 us
    ppermute x12, waiting for transfers between devices, swap(): lax.ppermute(pieces[d], 'seq', [(i, i ^ d) for i in range(shards_of)])  4.72 us
    pallas_call x2, Pallas kernels, shards(): pl.pallas_call(functools.partial(spectral_kernel, shards_of, chunks, last...  2.79 us
    pallas_call x2, Pallas kernels, shards(): pl.pallas_call(functools.partial(pack_kernel, shards_of, chunks, q), out_...  1.46 us
    pallas_call x1, Pallas kernels, shards(): pl.pallas_call(functools.partial(gate_kernel, shards_of, chunks), out_sha...  0.98 us
  transfers between devices with their start and end apart: 12, of which 4 were waited for; matrix products, arithmetic and copies ran while one was open for 0% of the time, Pallas kernels for 11%

profile of v4, /device:TPU:0, one launch (start us, length us, event | category | flops | bytes accessed | tf_op | source)
XLA Modules:
  0.0 26.9 jit_solution(4028145728445972896)
XLA Ops:
  0.6 0.0 copy-start.1
  0.6 0.0 copy-start.2
  0.7 0.0 copy-start.3
  0.7 0.0 copy-start.4
  0.7 0.0 copy-start.5
  0.7 1.3 %shard_map.154 = (f32[192,128]{1,0:T(8,128)S(1)}, f32[192,128]{1,0:T(8,128)S(1)}, f32[192,128]{1,0:T(8,128)S(1)}, f32[192,128]{1,0:T(8,128)S(1)}) custom-call(bf16[64,1024]{1,0:T(8,128)(2,1)} %refs_0_.7, bf16[64,1024]{1,0:T(8,128)(2,1)} %refs_1_.7, bf16[64,1024]{1,0:T(8,128)(2,1)} %refs_2_.7, bf16[64,1024]{1,0:T(8,128)(2,1)} %refs_3_.7, f32[64,1024]{1,0:T(8,128)} %refs_4_.5, ...), custom_call_target="tpu_custom_call" | custom-call | tf_op jit(solution)/shard_map/pallas_call | solution.py:281
  2.0 3.0 %collective-permute-start = (f32[192,128]{1,0:T(8,128)S(1)}, f32[192,128]{1,0:T(8,128)S(1)}, u32[]{:S(2)}, u32[]{:S(2)}) collective-permute-start(f32[192,128]{1,0:T(8,128)S(1)} %get-tuple-element.29), channel_id=1, source_target_pairs={{0,8},{8,0},{16,24},{24,16},{1,9},{9,1},{17,25},{25,17},{2,10},{10... | collective-permute-start | bytes 294920 | tf_op jit(solution)/shard_map/ppermute | solution.py:264
  5.0 0.0 copy-start.10
  5.0 1.5 %collective-permute-start.1 = (f32[192,128]{1,0:T(8,128)S(1)}, f32[192,128]{1,0:T(8,128)S(1)}, u32[]{:S(2)}, u32[]{:S(2)}) collective-permute-start(f32[192,128]{1,0:T(8,128)S(1)} %get-tuple-element.30), channel_id=1, source_target_pairs={{0,16},{8,24},{16,0},{24,8},{1,17},{9,25},{17,1},{25,9},{2,18},{10... | collective-permute-start | bytes 294920 | tf_op jit(solution)/shard_map/ppermute | solution.py:264
  6.5 0.0 copy-start
  6.5 0.0 copy-start.6
  6.5 0.0 copy-start.7
  6.5 0.0 copy-start.8
  6.5 0.0 copy-start.9
  6.5 0.1 collective-permute-start.2
  6.6 0.0 copy-done.1
  6.6 0.0 copy-done.2
  6.6 0.0 copy-done.3
  6.6 0.0 copy-done.4
  6.7 0.0 copy-done.5
  6.7 0.0 copy-done.10
  6.7 0.2 shard_map.156
  6.8 2.0 %collective-permute-start.6 = (f32[200,128]{1,0:T(8,128)S(1)}, f32[200,128]{1,0:T(8,128)S(1)}, u32[]{:S(2)}, u32[]{:S(2)}) collective-permute-start(f32[200,128]{1,0:T(8,128)S(1)} %get-tuple-element.37), channel_id=1, source_target_pairs={{0,8},{8,0},{16,24},{24,16},{1,9},{9,1},{17,25},{25,17},{2,10},{10... | collective-permute-start | bytes 307208 | tf_op jit(solution)/shard_map/ppermute | solution.py:264
  8.8 1.5 %collective-permute-start.7 = (f32[200,128]{1,0:T(8,128)S(1)}, f32[200,128]{1,0:T(8,128)S(1)}, u32[]{:S(2)}, u32[]{:S(2)}) collective-permute-start(f32[200,128]{1,0:T(8,128)S(1)} %get-tuple-element.38), channel_id=1, source_target_pairs={{0,16},{8,24},{16,0},{24,8},{1,17},{9,25},{17,1},{25,9},{2,18},{10... | collective-permute-start | bytes 307208 | tf_op jit(solution)/shard_map/ppermute | solution.py:264
  10.4 0.0 collective-permute-done.refs_6_
  10.4 0.9 %collective-permute-start.8 = (f32[200,128]{1,0:T(8,128)S(1)}, f32[200,128]{1,0:T(8,128)S(1)}, u32[]{:S(2)}, u32[]{:S(2)}) collective-permute-start(f32[200,128]{1,0:T(8,128)S(1)} %get-tuple-element.39), channel_id=1, source_target_pairs={{0,24},{8,16},{16,8},{24,0},{1,25},{9,17},{17,9},{25,1},{2,26},{10... | collective-permute-start | bytes 307208 | tf_op jit(solution)/shard_map/ppermute | solution.py:264
  11.3 0.0 collective-permute-done.1.refs_7_
  11.3 1.7 %collective-permute-done.2.refs_8_ = f32[192,128]{1,0:T(8,128)S(1)} collective-permute-done((f32[192,128]{1,0:T(8,128)S(1)}, f32[192,128]{1,0:T(8,128)S(1)}, u32[]{:S(2)}, u32[]{:S(2)}) %collective-permute-start.2) | collective-permute-done | bytes 98336 | tf_op jit(solution)/shard_map/ppermute | solution.py:264
  13.0 0.0 copy-done
  13.0 0.0 copy-done.6
  13.0 0.0 copy-done.7
  13.0 0.0 copy-done.8
  13.0 0.0 copy-done.9
  13.0 1.2 %shard_map.155 = (f32[192,128]{1,0:T(8,128)S(1)}, f32[192,128]{1,0:T(8,128)S(1)}, f32[192,128]{1,0:T(8,128)S(1)}, f32[192,128]{1,0:T(8,128)S(1)}) custom-call(bf16[4,64,96]{2,1,0:T(8,128)(2,1)S(1)} %copy-done.8, bf16[4,32,192]{2,1,0:T(8,128)(2,1)S(1)} %copy-done.7, bf16[4,32,192]{2,1,0:T(8,128)(2,1)S(1)} %copy-done.6, f32[2,32,128]{2,1,0:T(8,128)S(1)} %copy-done.9, ...), custom_call_target="tpu_custom_call" | custom-call | tf_op jit(solution)/shard_map/pallas_call | solution.py:295
  14.2 0.8 %collective-permute-start.3 = (f32[192,128]{1,0:T(8,128)S(1)}, f32[192,128]{1,0:T(8,128)S(1)}, u32[]{:S(2)}, u32[]{:S(2)}) collective-permute-start(f32[192,128]{1,0:T(8,128)S(1)} %get-tuple-element.33), channel_id=1, source_target_pairs={{0,8},{8,0},{16,24},{24,16},{1,9},{9,1},{17,25},{25,17},{2,10},{10... | collective-permute-start | bytes 294920 | tf_op jit(solution)/shard_map/ppermute | solution.py:264
  15.1 0.2 collective-permute-start.4
  15.3 0.0 collective-permute-done.6.refs_6_
  15.3 2.5 %collective-permute-start.5 = (f32[192,128]{1,0:T(8,128)S(1)}, f32[192,128]{1,0:T(8,128)S(1)}, u32[]{:S(2)}, u32[]{:S(2)}) collective-permute-start(f32[192,128]{1,0:T(8,128)S(1)} %get-tuple-element.35), channel_id=1, source_target_pairs={{0,24},{8,16},{16,8},{24,0},{1,25},{9,17},{17,9},{25,1},{2,26},{10... | collective-permute-start | bytes 294920 | tf_op jit(solution)/shard_map/ppermute | solution.py:264
  17.8 0.0 collective-permute-done.7.refs_7_
  17.8 0.0 collective-permute-done.8.refs_8_
  17.8 1.6 %shard_map.157 = (f32[192,128]{1,0:T(8,128)S(1)}, f32[192,128]{1,0:T(8,128)S(1)}, f32[192,128]{1,0:T(8,128)S(1)}, f32[192,128]{1,0:T(8,128)S(1)}, f32[1,64]{1,0:T(1,128)}) custom-call(bf16[4,64,96]{2,1,0:T(8,128)(2,1)S(1)} %copy-done.8, bf16[4,32,192]{2,1,0:T(8,128)(2,1)S(1)} %copy-done.7, bf16[4,32,192]{2,1,0:T(8,128)(2,1)S(1)} %copy-done.6, ...), custom_call_target="tpu_custom_call" | custom-call | tf_op jit(solution)/shard_map/pallas_call | solution.py:295
  19.4 0.7 %collective-permute-start.9 = (f32[192,128]{1,0:T(8,128)S(1)}, f32[192,128]{1,0:T(8,128)S(1)}, u32[]{:S(2)}, u32[]{:S(2)}) collective-permute-start(f32[192,128]{1,0:T(8,128)S(1)} %get-tuple-element.41), channel_id=1, source_target_pairs={{0,8},{8,0},{16,24},{24,16},{1,9},{9,1},{17,25},{25,17},{2,10},{10... | collective-permute-start | bytes 294920 | tf_op jit(solution)/shard_map/ppermute | solution.py:264
  20.1 0.2 collective-permute-start.10
  20.4 0.0 collective-permute-done.3.refs_5_
  20.4 2.5 %collective-permute-start.11 = (f32[192,128]{1,0:T(8,128)S(1)}, f32[192,128]{1,0:T(8,128)S(1)}, u32[]{:S(2)}, u32[]{:S(2)}) collective-permute-start(f32[192,128]{1,0:T(8,128)S(1)} %get-tuple-element.43), channel_id=1, source_target_pairs={{0,24},{8,16},{16,8},{24,0},{1,25},{9,17},{17,9},{25,1},{2,26},{10... | collective-permute-start | bytes 294920 | tf_op jit(solution)/shard_map/ppermute | solution.py:264
  22.9 0.0 collective-permute-done.4.refs_6_
  22.9 0.0 collective-permute-done.5.refs_7_
  22.9 1.1 %collective-permute-done.9.refs_9_ = f32[192,128]{1,0:T(8,128)S(1)} collective-permute-done((f32[192,128]{1,0:T(8,128)S(1)}, f32[192,128]{1,0:T(8,128)S(1)}, u32[]{:S(2)}, u32[]{:S(2)}) %collective-permute-start.9) | collective-permute-done | bytes 98336 | tf_op jit(solution)/shard_map/ppermute | solution.py:264
  24.0 0.7 %collective-permute-done.10.refs_10_ = f32[192,128]{1,0:T(8,128)S(1)} collective-permute-done((f32[192,128]{1,0:T(8,128)S(1)}, f32[192,128]{1,0:T(8,128)S(1)}, u32[]{:S(2)}, u32[]{:S(2)}) %collective-permute-start.10) | collective-permute-done | bytes 98336 | tf_op jit(solution)/shard_map/ppermute | solution.py:264
  24.8 1.1 %collective-permute-done.11.refs_11_ = f32[192,128]{1,0:T(8,128)S(1)} collective-permute-done((f32[192,128]{1,0:T(8,128)S(1)}, f32[192,128]{1,0:T(8,128)S(1)}, u32[]{:S(2)}, u32[]{:S(2)}) %collective-permute-start.11) | collective-permute-done | bytes 98336 | tf_op jit(solution)/shard_map/ppermute | solution.py:264
  25.9 1.0 %shard_map.158 = (bf16[64,1024]{1,0:T(8,128)(2,1)}, bf16[64,1024]{1,0:T(8,128)(2,1)}, bf16[64,1024]{1,0:T(8,128)(2,1)}, bf16[64,1024]{1,0:T(8,128)(2,1)}, f32[64,1024]{1,0:T(8,128)}) custom-call(bf16[64,1024]{1,0:T(8,128)(2,1)S(1)} %copy-done.1, bf16[64,1024]{1,0:T(8,128)(2,1)S(1)} %copy-done.2, bf16[64,1024]{1,0:T(8,128)(2,1)S(1)} %copy-done.3, ...), custom_call_target="tpu_custom_call" | custom-call | tf_op jit(solution)/shard_map/pallas_call | solution.py:309
Async XLA Ops:
  0.6 6.0 %copy-start.1 = (bf16[64,1024]{1,0:T(8,128)(2,1)S(1)}, bf16[64,1024]{1,0:T(8,128)(2,1)}, u32[]{:S(2)}) copy-start(bf16[64,1024]{1,0:T(8,128)(2,1)} %refs_0_.7) | copy-start | bytes 393220
  0.6 6.0 %copy-start.2 = (bf16[64,1024]{1,0:T(8,128)(2,1)S(1)}, bf16[64,1024]{1,0:T(8,128)(2,1)}, u32[]{:S(2)}) copy-start(bf16[64,1024]{1,0:T(8,128)(2,1)} %refs_1_.7) | copy-start | bytes 393220
  0.7 6.0 %copy-start.3 = (bf16[64,1024]{1,0:T(8,128)(2,1)S(1)}, bf16[64,1024]{1,0:T(8,128)(2,1)}, u32[]{:S(2)}) copy-start(bf16[64,1024]{1,0:T(8,128)(2,1)} %refs_2_.7) | copy-start | bytes 393220
  0.7 6.0 %copy-start.4 = (bf16[64,1024]{1,0:T(8,128)(2,1)S(1)}, bf16[64,1024]{1,0:T(8,128)(2,1)}, u32[]{:S(2)}) copy-start(bf16[64,1024]{1,0:T(8,128)(2,1)} %refs_3_.7) | copy-start | bytes 393220
  0.7 6.0 %copy-start.5 = (f32[64,1024]{1,0:T(8,128)S(1)}, f32[64,1024]{1,0:T(8,128)}, u32[]{:S(2)}) copy-start(f32[64,1024]{1,0:T(8,128)} %refs_4_.5) | copy-start | bytes 786436
  2.0 8.4 %collective-permute-start = (f32[192,128]{1,0:T(8,128)S(1)}, f32[192,128]{1,0:T(8,128)S(1)}, u32[]{:S(2)}, u32[]{:S(2)}) collective-permute-start(f32[192,128]{1,0:T(8,128)S(1)} %get-tuple-element.29), channel_id=1, source_target_pairs={{0,8},{8,0},{16,24},{24,16},{1,9},{9,1},{17,25},{25,17},{2,10},{10... | collective-permute-start | bytes 294920 | tf_op jit(solution)/shard_map/ppermute | solution.py:264
  5.0 1.7 %copy-start.10 = (f32[64]{0:T(128)S(1)}, f32[64]{0:T(128)}, u32[]{:S(2)}) copy-start(f32[64]{0:T(128)} %param.16) | copy-start | bytes 772
  5.0 6.3 %collective-permute-start.1 = (f32[192,128]{1,0:T(8,128)S(1)}, f32[192,128]{1,0:T(8,128)S(1)}, u32[]{:S(2)}, u32[]{:S(2)}) collective-permute-start(f32[192,128]{1,0:T(8,128)S(1)} %get-tuple-element.30), channel_id=1, source_target_pairs={{0,16},{8,24},{16,0},{24,8},{1,17},{9,25},{17,1},{25,9},{2,18},{10... | collective-permute-start | bytes 294920 | tf_op jit(solution)/shard_map/ppermute | solution.py:264
  6.5 6.5 %copy-start = (bf16[768,256]{1,0:T(8,128)(2,1)S(1)}, bf16[768,256]{1,0:T(8,128)(2,1)}, u32[]{:S(2)}) copy-start(bf16[768,256]{1,0:T(8,128)(2,1)} %constant.14.clone.refs_4_) | copy-start | bytes 1179652
  6.5 6.5 %copy-start.6 = (bf16[4,32,192]{2,1,0:T(8,128)(2,1)S(1)}, bf16[4,32,192]{2,1,0:T(8,128)(2,1)}, u32[]{:S(2)}) copy-start(bf16[4,32,192]{2,1,0:T(8,128)(2,1)} %constant.12.clone.refs_2_) | copy-start | bytes 147460
  6.5 6.5 %copy-start.7 = (bf16[4,32,192]{2,1,0:T(8,128)(2,1)S(1)}, bf16[4,32,192]{2,1,0:T(8,128)(2,1)}, u32[]{:S(2)}) copy-start(bf16[4,32,192]{2,1,0:T(8,128)(2,1)} %constant.11.clone.refs_1_) | copy-start | bytes 147460
  6.5 6.5 %copy-start.8 = (bf16[4,64,96]{2,1,0:T(8,128)(2,1)S(1)}, bf16[4,64,96]{2,1,0:T(8,128)(2,1)}, u32[]{:S(2)}) copy-start(bf16[4,64,96]{2,1,0:T(8,128)(2,1)} %constant.10.clone.refs_0_) | copy-start | bytes 147460
  6.5 6.5 %copy-start.9 = (f32[2,32,128]{2,1,0:T(8,128)S(1)}, f32[2,32,128]{2,1,0:T(8,128)}, u32[]{:S(2)}) copy-start(f32[2,32,128]{2,1,0:T(8,128)} %constant.13.clone.refs_3_) | copy-start | bytes 98308
  6.5 6.5 %collective-permute-start.2 = (f32[192,128]{1,0:T(8,128)S(1)}, f32[192,128]{1,0:T(8,128)S(1)}, u32[]{:S(2)}, u32[]{:S(2)}) collective-permute-start(f32[192,128]{1,0:T(8,128)S(1)} %get-tuple-element.31), channel_id=1, source_target_pairs={{0,24},{8,16},{16,8},{24,0},{1,25},{9,17},{17,9},{25,1},{2,26},{10... | collective-permute-start | bytes 294920 | tf_op jit(solution)/shard_map/ppermute | solution.py:264
  6.8 8.4 %collective-permute-start.6 = (f32[200,128]{1,0:T(8,128)S(1)}, f32[200,128]{1,0:T(8,128)S(1)}, u32[]{:S(2)}, u32[]{:S(2)}) collective-permute-start(f32[200,128]{1,0:T(8,128)S(1)} %get-tuple-element.37), channel_id=1, source_target_pairs={{0,8},{8,0},{16,24},{24,16},{1,9},{9,1},{17,25},{25,17},{2,10},{10... | collective-permute-start | bytes 307208 | tf_op jit(solution)/shard_map/ppermute | solution.py:264
  8.8 9.0 %collective-permute-start.7 = (f32[200,128]{1,0:T(8,128)S(1)}, f32[200,128]{1,0:T(8,128)S(1)}, u32[]{:S(2)}, u32[]{:S(2)}) collective-permute-start(f32[200,128]{1,0:T(8,128)S(1)} %get-tuple-element.38), channel_id=1, source_target_pairs={{0,16},{8,24},{16,0},{24,8},{1,17},{9,25},{17,1},{25,9},{2,18},{10... | collective-permute-start | bytes 307208 | tf_op jit(solution)/shard_map/ppermute | solution.py:264
  10.4 7.5 %collective-permute-start.8 = (f32[200,128]{1,0:T(8,128)S(1)}, f32[200,128]{1,0:T(8,128)S(1)}, u32[]{:S(2)}, u32[]{:S(2)}) collective-permute-start(f32[200,128]{1,0:T(8,128)S(1)} %get-tuple-element.39), channel_id=1, source_target_pairs={{0,24},{8,16},{16,8},{24,0},{1,25},{9,17},{17,9},{25,1},{2,26},{10... | collective-permute-start | bytes 307208 | tf_op jit(solution)/shard_map/ppermute | solution.py:264
  14.2 6.1 %collective-permute-start.3 = (f32[192,128]{1,0:T(8,128)S(1)}, f32[192,128]{1,0:T(8,128)S(1)}, u32[]{:S(2)}, u32[]{:S(2)}) collective-permute-start(f32[192,128]{1,0:T(8,128)S(1)} %get-tuple-element.33), channel_id=1, source_target_pairs={{0,8},{8,0},{16,24},{24,16},{1,9},{9,1},{17,25},{25,17},{2,10},{10... | collective-permute-start | bytes 294920 | tf_op jit(solution)/shard_map/ppermute | solution.py:264
  15.1 7.8 %collective-permute-start.4 = (f32[192,128]{1,0:T(8,128)S(1)}, f32[192,128]{1,0:T(8,128)S(1)}, u32[]{:S(2)}, u32[]{:S(2)}) collective-permute-start(f32[192,128]{1,0:T(8,128)S(1)} %get-tuple-element.34), channel_id=1, source_target_pairs={{0,16},{8,24},{16,0},{24,8},{1,17},{9,25},{17,1},{25,9},{2,18},{10... | collective-permute-start | bytes 294920 | tf_op jit(solution)/shard_map/ppermute | solution.py:264
  15.3 7.6 %collective-permute-start.5 = (f32[192,128]{1,0:T(8,128)S(1)}, f32[192,128]{1,0:T(8,128)S(1)}, u32[]{:S(2)}, u32[]{:S(2)}) collective-permute-start(f32[192,128]{1,0:T(8,128)S(1)} %get-tuple-element.35), channel_id=1, source_target_pairs={{0,24},{8,16},{16,8},{24,0},{1,25},{9,17},{17,9},{25,1},{2,26},{10... | collective-permute-start | bytes 294920 | tf_op jit(solution)/shard_map/ppermute | solution.py:264
  19.4 4.6 %collective-permute-start.9 = (f32[192,128]{1,0:T(8,128)S(1)}, f32[192,128]{1,0:T(8,128)S(1)}, u32[]{:S(2)}, u32[]{:S(2)}) collective-permute-start(f32[192,128]{1,0:T(8,128)S(1)} %get-tuple-element.41), channel_id=1, source_target_pairs={{0,8},{8,0},{16,24},{24,16},{1,9},{9,1},{17,25},{25,17},{2,10},{10... | collective-permute-start | bytes 294920 | tf_op jit(solution)/shard_map/ppermute | solution.py:264
  20.1 4.6 %collective-permute-start.10 = (f32[192,128]{1,0:T(8,128)S(1)}, f32[192,128]{1,0:T(8,128)S(1)}, u32[]{:S(2)}, u32[]{:S(2)}) collective-permute-start(f32[192,128]{1,0:T(8,128)S(1)} %get-tuple-element.42), channel_id=1, source_target_pairs={{0,16},{8,24},{16,0},{24,8},{1,17},{9,25},{17,1},{25,9},{2,18},{10... | collective-permute-start | bytes 294920 | tf_op jit(solution)/shard_map/ppermute | solution.py:264
  20.4 5.5 %collective-permute-start.11 = (f32[192,128]{1,0:T(8,128)S(1)}, f32[192,128]{1,0:T(8,128)S(1)}, u32[]{:S(2)}, u32[]{:S(2)}) collective-permute-start(f32[192,128]{1,0:T(8,128)S(1)} %get-tuple-element.43), channel_id=1, source_target_pairs={{0,24},{8,16},{16,8},{24,0},{1,25},{9,17},{17,9},{25,1},{2,26},{10... | collective-permute-start | bytes 294920 | tf_op jit(solution)/shard_map/ppermute | solution.py:264

commit v5 on v4

--- a/solution.py
+++ b/solution.py
@@ -198,17 +198,18 @@
 
 
 def gate_kernel(shards_of, chunks, *refs):
-    post, pre, signal, cotangent = refs[:4]
-    pieces = refs[4 : 4 + chunks * shards_of]
-    refs = refs[4 + chunks * shards_of :]
-    outs, (fields, output, d_post, d_pre, d_signal, sems) = refs[:5], refs[5:]
+    post, pre, signal, cotangent, skip = refs[:5]
+    pieces = refs[5 : 5 + chunks * shards_of]
+    refs = refs[5 + chunks * shards_of :]
+    outs, (fields, output, d_post, d_pre, d_signal, sems) = refs[:6], refs[6:]
     me = lax.axis_index("seq")
     channels, length = post.shape
     chunk_rows = channels // chunks
     width = chunk_rows // shards_of
     per = length // LANES
     field_rows = width * per
-    copies = []
+    copies = [pltpu.make_async_copy(skip, outs[5], sems.at[0, 5])]
+    copies[0].start()
 
     def ship(q, i, held):
         rows = pl.ds(q * chunk_rows, chunk_rows)
@@ -306,16 +307,17 @@
         if last:
             d_skip = mixed[shards_of]
         back += swap(mixed[:shards_of])
-    output, d_post, d_pre, d_signal, d_filter = pl.pallas_call(
+    output, d_post, d_pre, d_signal, d_filter, d_skip = pl.pallas_call(
         functools.partial(gate_kernel, shards_of, chunks),
-        out_shape=[pltpu.HBM((channels, length), BF16)] * 4 + [pltpu.HBM((channels, length), F32)],
-        in_specs=[vmem] * (4 + chunks * shards_of),
-        out_specs=[hbm] * 5,
+        out_shape=[pltpu.HBM((channels, length), BF16)] * 4
+        + [pltpu.HBM((channels, length), F32), pltpu.HBM((1, channels), F32)],
+        in_specs=[vmem] * (5 + chunks * shards_of),
+        out_specs=[hbm] * 6,
         scratch_shapes=[pltpu.VMEM((3, channels, length), F32)]
         + [pltpu.VMEM((channels, length), BF16)] * 4
-        + [pltpu.SemaphoreType.DMA((chunks, 5))],
+        + [pltpu.SemaphoreType.DMA((chunks, 6))],
         compiler_params=params,
-    )(post_gate, pre_gate, signal, cotangent, *back)
+    )(post_gate, pre_gate, signal, cotangent, d_skip, *back)
     return (output, d_post, d_pre, d_signal, d_skip.reshape(channels), d_filter)
 
 

time: 27 us -> 26.8 us (level)
  Pallas kernels: 5.23 us -> 4.95 us
    pallas_call x2, Pallas kernels: 2.79 us -> 2.48 us  [shards(): pl.pallas_call(functools.partial(spectral_kernel, shards_of, chunks, last...]
  transfers between devices with their start and end apart: 12 -> 12, of which waited for: 4 -> 4; matrix products, arithmetic and copies ran while one was open for 0% -> 0% of each run, Pallas kernels for 11% -> 10%
where the time goes in v5:
time: 26.8 us; the launch traced here: 26.7 us
  starting transfers between devices  16.2 us (60%)
  Pallas kernels  4.95 us (18%)
  waiting for transfers between devices  4.73 us (18%)
  between operations  0.76 us (3%)
    ppermute x12, starting transfers between devices, swap(): lax.ppermute(pieces[d], 'seq', [(i, i ^ d) for i in range(shards_of)])  16.2 us
    ppermute x12, waiting for transfers between devices, swap(): lax.ppermute(pieces[d], 'seq', [(i, i ^ d) for i in range(shards_of)])  4.73 us
    pallas_call x2, Pallas kernels, shards(): pl.pallas_call(functools.partial(spectral_kernel, shards_of, chunks, last...  2.48 us
    pallas_call x2, Pallas kernels, shards(): pl.pallas_call(functools.partial(pack_kernel, shards_of, chunks, q), out_...  1.47 us
    pallas_call x1, Pallas kernels, shards(): pl.pallas_call(functools.partial(gate_kernel, shards_of, chunks), out_sha...  1.01 us
  transfers between devices with their start and end apart: 12, of which 4 were waited for; matrix products, arithmetic and copies ran while one was open for 0% of the time, Pallas kernels for 10%

profile of v5, /device:TPU:0, one launch (start us, length us, event | category | flops | bytes accessed | tf_op | source)
XLA Modules:
  0.0 26.7 jit_solution(16844772234483031285)
XLA Ops:
  0.6 0.0 copy-start.1
  0.6 0.0 copy-start.2
  0.7 0.0 copy-start.3
  0.7 0.0 copy-start.4
  0.7 0.0 copy-start.5
  0.7 1.3 %shard_map.156 = (f32[192,128]{1,0:T(8,128)S(1)}, f32[192,128]{1,0:T(8,128)S(1)}, f32[192,128]{1,0:T(8,128)S(1)}, f32[192,128]{1,0:T(8,128)S(1)}) custom-call(bf16[64,1024]{1,0:T(8,128)(2,1)} %refs_0_.7, bf16[64,1024]{1,0:T(8,128)(2,1)} %refs_1_.7, bf16[64,1024]{1,0:T(8,128)(2,1)} %refs_2_.7, bf16[64,1024]{1,0:T(8,128)(2,1)} %refs_3_.7, f32[64,1024]{1,0:T(8,128)} %refs_4_.5, ...), custom_call_target="tpu_custom_call" | custom-call | tf_op jit(solution)/shard_map/pallas_call | solution.py:282
  2.0 3.0 %collective-permute-start.3 = (f32[192,128]{1,0:T(8,128)S(1)}, f32[192,128]{1,0:T(8,128)S(1)}, u32[]{:S(2)}, u32[]{:S(2)}) collective-permute-start(f32[192,128]{1,0:T(8,128)S(1)} %get-tuple-element.35), channel_id=1, source_target_pairs={{0,8},{8,0},{16,24},{24,16},{1,9},{9,1},{17,25},{25,17},{2,10},{10... | collective-permute-start | bytes 294920 | tf_op jit(solution)/shard_map/ppermute | solution.py:265
  5.0 0.0 copy-start.10
  5.0 1.5 %collective-permute-start.4 = (f32[192,128]{1,0:T(8,128)S(1)}, f32[192,128]{1,0:T(8,128)S(1)}, u32[]{:S(2)}, u32[]{:S(2)}) collective-permute-start(f32[192,128]{1,0:T(8,128)S(1)} %get-tuple-element.36), channel_id=1, source_target_pairs={{0,16},{8,24},{16,0},{24,8},{1,17},{9,25},{17,1},{25,9},{2,18},{10... | collective-permute-start | bytes 294920 | tf_op jit(solution)/shard_map/ppermute | solution.py:265
  6.5 0.0 copy-start
  6.5 0.0 copy-start.6
  6.5 0.0 copy-start.7
  6.5 0.0 copy-start.8
  6.5 0.0 copy-start.9
  6.5 0.1 collective-permute-start.5
  6.6 0.0 copy-done.1
  6.6 0.0 copy-done.2
  6.6 0.0 copy-done.3
  6.6 0.0 copy-done.4
  6.7 0.0 copy-done.5
  6.7 0.0 copy-done.10
  6.7 0.2 shard_map.154
  6.8 2.0 %collective-permute-start = (f32[200,128]{1,0:T(8,128)S(1)}, f32[200,128]{1,0:T(8,128)S(1)}, u32[]{:S(2)}, u32[]{:S(2)}) collective-permute-start(f32[200,128]{1,0:T(8,128)S(1)} %get-tuple-element.30), channel_id=1, source_target_pairs={{0,8},{8,0},{16,24},{24,16},{1,9},{9,1},{17,25},{25,17},{2,10},{10... | collective-permute-start | bytes 307208 | tf_op jit(solution)/shard_map/ppermute | solution.py:265
  8.8 1.5 %collective-permute-start.1 = (f32[200,128]{1,0:T(8,128)S(1)}, f32[200,128]{1,0:T(8,128)S(1)}, u32[]{:S(2)}, u32[]{:S(2)}) collective-permute-start(f32[200,128]{1,0:T(8,128)S(1)} %get-tuple-element.31), channel_id=1, source_target_pairs={{0,16},{8,24},{16,0},{24,8},{1,17},{9,25},{17,1},{25,9},{2,18},{10... | collective-permute-start | bytes 307208 | tf_op jit(solution)/shard_map/ppermute | solution.py:265
  10.4 0.0 collective-permute-done.3.refs_6_
  10.4 0.9 %collective-permute-start.2 = (f32[200,128]{1,0:T(8,128)S(1)}, f32[200,128]{1,0:T(8,128)S(1)}, u32[]{:S(2)}, u32[]{:S(2)}) collective-permute-start(f32[200,128]{1,0:T(8,128)S(1)} %get-tuple-element.32), channel_id=1, source_target_pairs={{0,24},{8,16},{16,8},{24,0},{1,25},{9,17},{17,9},{25,1},{2,26},{10... | collective-permute-start | bytes 307208 | tf_op jit(solution)/shard_map/ppermute | solution.py:265
  11.3 0.0 collective-permute-done.4.refs_7_
  11.3 1.7 %collective-permute-done.5.refs_8_ = f32[192,128]{1,0:T(8,128)S(1)} collective-permute-done((f32[192,128]{1,0:T(8,128)S(1)}, f32[192,128]{1,0:T(8,128)S(1)}, u32[]{:S(2)}, u32[]{:S(2)}) %collective-permute-start.5) | collective-permute-done | bytes 98336 | tf_op jit(solution)/shard_map/ppermute | solution.py:265
  13.0 0.0 copy-done
  13.0 0.0 copy-done.6
  13.0 0.0 copy-done.7
  13.0 0.0 copy-done.8
  13.0 0.0 copy-done.9
  13.0 1.2 %shard_map.157 = (f32[192,128]{1,0:T(8,128)S(1)}, f32[192,128]{1,0:T(8,128)S(1)}, f32[192,128]{1,0:T(8,128)S(1)}, f32[192,128]{1,0:T(8,128)S(1)}) custom-call(bf16[4,64,96]{2,1,0:T(8,128)(2,1)S(1)} %copy-done.8, bf16[4,32,192]{2,1,0:T(8,128)(2,1)S(1)} %copy-done.7, bf16[4,32,192]{2,1,0:T(8,128)(2,1)S(1)} %copy-done.6, f32[2,32,128]{2,1,0:T(8,128)S(1)} %copy-done.9, ...), custom_call_target="tpu_custom_call" | custom-call | tf_op jit(solution)/shard_map/pallas_call | solution.py:296
  14.3 0.8 %collective-permute-start.6 = (f32[192,128]{1,0:T(8,128)S(1)}, f32[192,128]{1,0:T(8,128)S(1)}, u32[]{:S(2)}, u32[]{:S(2)}) collective-permute-start(f32[192,128]{1,0:T(8,128)S(1)} %get-tuple-element.39), channel_id=1, source_target_pairs={{0,8},{8,0},{16,24},{24,16},{1,9},{9,1},{17,25},{25,17},{2,10},{10... | collective-permute-start | bytes 294920 | tf_op jit(solution)/shard_map/ppermute | solution.py:265
  15.1 0.2 collective-permute-start.7
  15.3 0.0 collective-permute-done.refs_6_
  15.3 2.5 %collective-permute-start.8 = (f32[192,128]{1,0:T(8,128)S(1)}, f32[192,128]{1,0:T(8,128)S(1)}, u32[]{:S(2)}, u32[]{:S(2)}) collective-permute-start(f32[192,128]{1,0:T(8,128)S(1)} %get-tuple-element.41), channel_id=1, source_target_pairs={{0,24},{8,16},{16,8},{24,0},{1,25},{9,17},{17,9},{25,1},{2,26},{10... | collective-permute-start | bytes 294920 | tf_op jit(solution)/shard_map/ppermute | solution.py:265
  17.8 0.0 collective-permute-done.1.refs_7_
  17.8 0.0 collective-permute-done.2.refs_8_
  17.8 1.2 %shard_map.155 = (f32[192,128]{1,0:T(8,128)S(1)}, f32[192,128]{1,0:T(8,128)S(1)}, f32[192,128]{1,0:T(8,128)S(1)}, f32[192,128]{1,0:T(8,128)S(1)}, f32[1,64]{1,0:T(1,128)S(1)}) custom-call(bf16[4,64,96]{2,1,0:T(8,128)(2,1)S(1)} %copy-done.8, bf16[4,32,192]{2,1,0:T(8,128)(2,1)S(1)} %copy-done.7, bf16[4,32,192]{2,1,0:T(8,128)(2,1)S(1)} %copy-done.6, ...), custom_call_target="tpu_custom_call" | custom-call | tf_op jit(solution)/shard_map/pallas_call | solution.py:296
  19.1 0.8 %collective-permute-start.9 = (f32[192,128]{1,0:T(8,128)S(1)}, f32[192,128]{1,0:T(8,128)S(1)}, u32[]{:S(2)}, u32[]{:S(2)}) collective-permute-start(f32[192,128]{1,0:T(8,128)S(1)} %get-tuple-element.43), channel_id=1, source_target_pairs={{0,8},{8,0},{16,24},{24,16},{1,9},{9,1},{17,25},{25,17},{2,10},{10... | collective-permute-start | bytes 294920 | tf_op jit(solution)/shard_map/ppermute | solution.py:265
  19.9 0.2 collective-permute-start.10
  20.1 0.0 collective-permute-done.6.refs_6_
  20.1 2.5 %collective-permute-start.11 = (f32[192,128]{1,0:T(8,128)S(1)}, f32[192,128]{1,0:T(8,128)S(1)}, u32[]{:S(2)}, u32[]{:S(2)}) collective-permute-start(f32[192,128]{1,0:T(8,128)S(1)} %get-tuple-element.45), channel_id=1, source_target_pairs={{0,24},{8,16},{16,8},{24,0},{1,25},{9,17},{17,9},{25,1},{2,26},{10... | collective-permute-start | bytes 294920 | tf_op jit(solution)/shard_map/ppermute | solution.py:265
  22.6 0.0 collective-permute-done.7.refs_7_
  22.7 0.0 collective-permute-done.8.refs_8_
  22.7 1.1 %collective-permute-done.9.refs_10_ = f32[192,128]{1,0:T(8,128)S(1)} collective-permute-done((f32[192,128]{1,0:T(8,128)S(1)}, f32[192,128]{1,0:T(8,128)S(1)}, u32[]{:S(2)}, u32[]{:S(2)}) %collective-permute-start.9) | collective-permute-done | bytes 98336 | tf_op jit(solution)/shard_map/ppermute | solution.py:265
  23.8 0.8 %collective-permute-done.10.refs_11_ = f32[192,128]{1,0:T(8,128)S(1)} collective-permute-done((f32[192,128]{1,0:T(8,128)S(1)}, f32[192,128]{1,0:T(8,128)S(1)}, u32[]{:S(2)}, u32[]{:S(2)}) %collective-permute-start.10) | collective-permute-done | bytes 98336 | tf_op jit(solution)/shard_map/ppermute | solution.py:265
  24.5 1.1 %collective-permute-done.11.refs_12_ = f32[192,128]{1,0:T(8,128)S(1)} collective-permute-done((f32[192,128]{1,0:T(8,128)S(1)}, f32[192,128]{1,0:T(8,128)S(1)}, u32[]{:S(2)}, u32[]{:S(2)}) %collective-permute-start.11) | collective-permute-done | bytes 98336 | tf_op jit(solution)/shard_map/ppermute | solution.py:265
  25.7 1.0 %shard_map.158 = (bf16[64,1024]{1,0:T(8,128)(2,1)}, bf16[64,1024]{1,0:T(8,128)(2,1)}, bf16[64,1024]{1,0:T(8,128)(2,1)}, bf16[64,1024]{1,0:T(8,128)(2,1)}, f32[64,1024]{1,0:T(8,128)}, /*index=5*/f32[1,64]{1,0:T(1,128)}) custom-call(bf16[64,1024]{1,0:T(8,128)(2,1)S(1)} %copy-done.1, bf16[64,1024]{1,0:T(8,128)(2,1)S(1)} %copy-done.2, ...), custom_call_target="tpu_custom_call" | custom-call | tf_op jit(solution)/shard_map/pallas_call | solution.py:310
Async XLA Ops:
  0.6 6.0 %copy-start.1 = (bf16[64,1024]{1,0:T(8,128)(2,1)S(1)}, bf16[64,1024]{1,0:T(8,128)(2,1)}, u32[]{:S(2)}) copy-start(bf16[64,1024]{1,0:T(8,128)(2,1)} %refs_0_.7) | copy-start | bytes 393220
  0.6 6.0 %copy-start.2 = (bf16[64,1024]{1,0:T(8,128)(2,1)S(1)}, bf16[64,1024]{1,0:T(8,128)(2,1)}, u32[]{:S(2)}) copy-start(bf16[64,1024]{1,0:T(8,128)(2,1)} %refs_1_.7) | copy-start | bytes 393220
  0.7 6.0 %copy-start.3 = (bf16[64,1024]{1,0:T(8,128)(2,1)S(1)}, bf16[64,1024]{1,0:T(8,128)(2,1)}, u32[]{:S(2)}) copy-start(bf16[64,1024]{1,0:T(8,128)(2,1)} %refs_2_.7) | copy-start | bytes 393220
  0.7 6.0 %copy-start.4 = (bf16[64,1024]{1,0:T(8,128)(2,1)S(1)}, bf16[64,1024]{1,0:T(8,128)(2,1)}, u32[]{:S(2)}) copy-start(bf16[64,1024]{1,0:T(8,128)(2,1)} %refs_3_.7) | copy-start | bytes 393220
  0.7 6.0 %copy-start.5 = (f32[64,1024]{1,0:T(8,128)S(1)}, f32[64,1024]{1,0:T(8,128)}, u32[]{:S(2)}) copy-start(f32[64,1024]{1,0:T(8,128)} %refs_4_.5) | copy-start | bytes 786436
  2.0 8.4 %collective-permute-start.3 = (f32[192,128]{1,0:T(8,128)S(1)}, f32[192,128]{1,0:T(8,128)S(1)}, u32[]{:S(2)}, u32[]{:S(2)}) collective-permute-start(f32[192,128]{1,0:T(8,128)S(1)} %get-tuple-element.35), channel_id=1, source_target_pairs={{0,8},{8,0},{16,24},{24,16},{1,9},{9,1},{17,25},{25,17},{2,10},{10... | collective-permute-start | bytes 294920 | tf_op jit(solution)/shard_map/ppermute | solution.py:265
  5.0 1.7 %copy-start.10 = (f32[64]{0:T(128)S(1)}, f32[64]{0:T(128)}, u32[]{:S(2)}) copy-start(f32[64]{0:T(128)} %param.16) | copy-start | bytes 772
  5.0 6.3 %collective-permute-start.4 = (f32[192,128]{1,0:T(8,128)S(1)}, f32[192,128]{1,0:T(8,128)S(1)}, u32[]{:S(2)}, u32[]{:S(2)}) collective-permute-start(f32[192,128]{1,0:T(8,128)S(1)} %get-tuple-element.36), channel_id=1, source_target_pairs={{0,16},{8,24},{16,0},{24,8},{1,17},{9,25},{17,1},{25,9},{2,18},{10... | collective-permute-start | bytes 294920 | tf_op jit(solution)/shard_map/ppermute | solution.py:265
  6.5 6.5 %copy-start = (bf16[768,256]{1,0:T(8,128)(2,1)S(1)}, bf16[768,256]{1,0:T(8,128)(2,1)}, u32[]{:S(2)}) copy-start(bf16[768,256]{1,0:T(8,128)(2,1)} %constant.14.clone.refs_4_) | copy-start | bytes 1179652
  6.5 6.5 %copy-start.6 = (bf16[4,32,192]{2,1,0:T(8,128)(2,1)S(1)}, bf16[4,32,192]{2,1,0:T(8,128)(2,1)}, u32[]{:S(2)}) copy-start(bf16[4,32,192]{2,1,0:T(8,128)(2,1)} %constant.12.clone.refs_2_) | copy-start | bytes 147460
  6.5 6.5 %copy-start.7 = (bf16[4,32,192]{2,1,0:T(8,128)(2,1)S(1)}, bf16[4,32,192]{2,1,0:T(8,128)(2,1)}, u32[]{:S(2)}) copy-start(bf16[4,32,192]{2,1,0:T(8,128)(2,1)} %constant.11.clone.refs_1_) | copy-start | bytes 147460
  6.5 6.5 %copy-start.8 = (bf16[4,64,96]{2,1,0:T(8,128)(2,1)S(1)}, bf16[4,64,96]{2,1,0:T(8,128)(2,1)}, u32[]{:S(2)}) copy-start(bf16[4,64,96]{2,1,0:T(8,128)(2,1)} %constant.10.clone.refs_0_) | copy-start | bytes 147460
  6.5 6.5 %copy-start.9 = (f32[2,32,128]{2,1,0:T(8,128)S(1)}, f32[2,32,128]{2,1,0:T(8,128)}, u32[]{:S(2)}) copy-start(f32[2,32,128]{2,1,0:T(8,128)} %constant.13.clone.refs_3_) | copy-start | bytes 98308
  6.5 6.5 %collective-permute-start.5 = (f32[192,128]{1,0:T(8,128)S(1)}, f32[192,128]{1,0:T(8,128)S(1)}, u32[]{:S(2)}, u32[]{:S(2)}) collective-permute-start(f32[192,128]{1,0:T(8,128)S(1)} %get-tuple-element.37), channel_id=1, source_target_pairs={{0,24},{8,16},{16,8},{24,0},{1,25},{9,17},{17,9},{25,1},{2,26},{10... | collective-permute-start | bytes 294920 | tf_op jit(solution)/shard_map/ppermute | solution.py:265
  6.8 8.5 %collective-permute-start = (f32[200,128]{1,0:T(8,128)S(1)}, f32[200,128]{1,0:T(8,128)S(1)}, u32[]{:S(2)}, u32[]{:S(2)}) collective-permute-start(f32[200,128]{1,0:T(8,128)S(1)} %get-tuple-element.30), channel_id=1, source_target_pairs={{0,8},{8,0},{16,24},{24,16},{1,9},{9,1},{17,25},{25,17},{2,10},{10... | collective-permute-start | bytes 307208 | tf_op jit(solution)/shard_map/ppermute | solution.py:265
  8.8 9.0 %collective-permute-start.1 = (f32[200,128]{1,0:T(8,128)S(1)}, f32[200,128]{1,0:T(8,128)S(1)}, u32[]{:S(2)}, u32[]{:S(2)}) collective-permute-start(f32[200,128]{1,0:T(8,128)S(1)} %get-tuple-element.31), channel_id=1, source_target_pairs={{0,16},{8,24},{16,0},{24,8},{1,17},{9,25},{17,1},{25,9},{2,18},{10... | collective-permute-start | bytes 307208 | tf_op jit(solution)/shard_map/ppermute | solution.py:265
  10.4 7.5 %collective-permute-start.2 = (f32[200,128]{1,0:T(8,128)S(1)}, f32[200,128]{1,0:T(8,128)S(1)}, u32[]{:S(2)}, u32[]{:S(2)}) collective-permute-start(f32[200,128]{1,0:T(8,128)S(1)} %get-tuple-element.32), channel_id=1, source_target_pairs={{0,24},{8,16},{16,8},{24,0},{1,25},{9,17},{17,9},{25,1},{2,26},{10... | collective-permute-start | bytes 307208 | tf_op jit(solution)/shard_map/ppermute | solution.py:265
  14.3 5.9 %collective-permute-start.6 = (f32[192,128]{1,0:T(8,128)S(1)}, f32[192,128]{1,0:T(8,128)S(1)}, u32[]{:S(2)}, u32[]{:S(2)}) collective-permute-start(f32[192,128]{1,0:T(8,128)S(1)} %get-tuple-element.39), channel_id=1, source_target_pairs={{0,8},{8,0},{16,24},{24,16},{1,9},{9,1},{17,25},{25,17},{2,10},{10... | collective-permute-start | bytes 294920 | tf_op jit(solution)/shard_map/ppermute | solution.py:265
  15.1 7.5 %collective-permute-start.7 = (f32[192,128]{1,0:T(8,128)S(1)}, f32[192,128]{1,0:T(8,128)S(1)}, u32[]{:S(2)}, u32[]{:S(2)}) collective-permute-start(f32[192,128]{1,0:T(8,128)S(1)} %get-tuple-element.40), channel_id=1, source_target_pairs={{0,16},{8,24},{16,0},{24,8},{1,17},{9,25},{17,1},{25,9},{2,18},{10... | collective-permute-start | bytes 294920 | tf_op jit(solution)/shard_map/ppermute | solution.py:265
  15.3 7.3 %collective-permute-start.8 = (f32[192,128]{1,0:T(8,128)S(1)}, f32[192,128]{1,0:T(8,128)S(1)}, u32[]{:S(2)}, u32[]{:S(2)}) collective-permute-start(f32[192,128]{1,0:T(8,128)S(1)} %get-tuple-element.41), channel_id=1, source_target_pairs={{0,24},{8,16},{16,8},{24,0},{1,25},{9,17},{17,9},{25,1},{2,26},{10... | collective-permute-start | bytes 294920 | tf_op jit(solution)/shard_map/ppermute | solution.py:265
  19.1 4.7 %collective-permute-start.9 = (f32[192,128]{1,0:T(8,128)S(1)}, f32[192,128]{1,0:T(8,128)S(1)}, u32[]{:S(2)}, u32[]{:S(2)}) collective-permute-start(f32[192,128]{1,0:T(8,128)S(1)} %get-tuple-element.43), channel_id=1, source_target_pairs={{0,8},{8,0},{16,24},{24,16},{1,9},{9,1},{17,25},{25,17},{2,10},{10... | collective-permute-start | bytes 294920 | tf_op jit(solution)/shard_map/ppermute | solution.py:265
  19.9 4.6 %collective-permute-start.10 = (f32[192,128]{1,0:T(8,128)S(1)}, f32[192,128]{1,0:T(8,128)S(1)}, u32[]{:S(2)}, u32[]{:S(2)}) collective-permute-start(f32[192,128]{1,0:T(8,128)S(1)} %get-tuple-element.44), channel_id=1, source_target_pairs={{0,16},{8,24},{16,0},{24,8},{1,17},{9,25},{17,1},{25,9},{2,18},{10... | collective-permute-start | bytes 294920 | tf_op jit(solution)/shard_map/ppermute | solution.py:265
  20.1 5.5 %collective-permute-start.11 = (f32[192,128]{1,0:T(8,128)S(1)}, f32[192,128]{1,0:T(8,128)S(1)}, u32[]{:S(2)}, u32[]{:S(2)}) collective-permute-start(f32[192,128]{1,0:T(8,128)S(1)} %get-tuple-element.45), channel_id=1, source_target_pairs={{0,24},{8,16},{16,8},{24,0},{1,25},{9,17},{17,9},{25,1},{2,26},{10... | collective-permute-start | bytes 294920 | tf_op jit(solution)/shard_map/ppermute | solution.py:265

commit v6 on v4

--- a/solution.py
+++ b/solution.py
@@ -197,51 +197,59 @@
                     ]
 
 
-def gate_kernel(shards_of, chunks, *refs):
+def gate_kernel(shards_of, chunks, q, *refs):
     post, pre, signal, cotangent = refs[:4]
-    pieces = refs[4 : 4 + chunks * shards_of]
-    refs = refs[4 + chunks * shards_of :]
-    outs, (fields, output, d_post, d_pre, d_signal, sems) = refs[:5], refs[5:]
+    pieces = refs[4 : 4 + shards_of]
+    last = q == chunks - 1
+    refs = refs[4 + shards_of :]
+    if last:
+        skip, *refs = refs
+    else:
+        refs = refs[1:]
+    refs = refs[5 * (q > 0) :]
+    outs, refs = refs[: 5 + last], refs[5 + last :]
+    fields, output, d_post, d_pre, d_signal, sems = refs
     me = lax.axis_index("seq")
     channels, length = post.shape
     chunk_rows = channels // chunks
     width = chunk_rows // shards_of
     per = length // LANES
     field_rows = width * per
+    rows = slice(q * chunk_rows, (q + 1) * chunk_rows)
     copies = []
 
-    def ship(q, i, held):
-        rows = pl.ds(q * chunk_rows, chunk_rows)
-        copy = pltpu.make_async_copy(held.at[rows, :], outs[i].at[rows, :], sems.at[q, i])
-        copy.start()
-        copies.append(copy)
-
-    def gather(q, f):
+    def ship(i, held, target):
+        copies.append(pltpu.make_async_copy(held, target, sems.at[i]))
+        copies[-1].start()
+
+    def part(i):
+        return outs[i].at[pl.ds(q * chunk_rows, chunk_rows), :]
+
+    def gather(f):
         for d in range(shards_of):
             for c in range(0, width, SUBLANES):
-                top = q * chunk_rows + (me ^ d) * width + c
-                held = pl.ds(pl.multiple_of(top, SUBLANES), SUBLANES)
+                held = pl.ds(pl.multiple_of((me ^ d) * width + c, SUBLANES), SUBLANES)
                 for a in range(per):
-                    fields[f, held, a * LANES : (a + 1) * LANES] = pieces[q * shards_of + d][
+                    fields[f, held, a * LANES : (a + 1) * LANES] = pieces[d][
                         pl.ds(f * field_rows + c * per + a, SUBLANES, stride=per), :
                     ]
 
-    for q in range(chunks):
-        rows = slice(q * chunk_rows, (q + 1) * chunk_rows)
-        gather(q, 2)
-        ship(q, 4, fields.at[2])
-        gather(q, 0)
-        conved = fields[0, rows, :]
-        output[rows, :] = (post[rows, :].astype(F32) * conved).astype(BF16)
-        ship(q, 0, output)
-        d_post[rows, :] = (cotangent[rows, :].astype(F32) * conved).astype(BF16)
-        ship(q, 1, d_post)
-        gather(q, 1)
-        d_gated = fields[1, rows, :]
-        d_pre[rows, :] = (signal[rows, :].astype(F32) * d_gated).astype(BF16)
-        ship(q, 2, d_pre)
-        d_signal[rows, :] = (pre[rows, :].astype(F32) * d_gated).astype(BF16)
-        ship(q, 3, d_signal)
+    if last:
+        ship(5, skip, outs[5])
+    gather(2)
+    ship(4, fields.at[2], part(4))
+    gather(0)
+    conved = fields[0]
+    output[...] = (post[rows, :].astype(F32) * conved).astype(BF16)
+    ship(0, output, part(0))
+    d_post[...] = (cotangent[rows, :].astype(F32) * conved).astype(BF16)
+    ship(1, d_post, part(1))
+    gather(1)
+    d_gated = fields[1]
+    d_pre[...] = (signal[rows, :].astype(F32) * d_gated).astype(BF16)
+    ship(2, d_pre, part(2))
+    d_signal[...] = (pre[rows, :].astype(F32) * d_gated).astype(BF16)
+    ship(3, d_signal, part(3))
     for copy in copies:
         copy.wait()
 
@@ -305,17 +313,32 @@
         )(*consts, *arrived[q])
         if last:
             d_skip = mixed[shards_of]
-        back += swap(mixed[:shards_of])
-    output, d_post, d_pre, d_signal, d_filter = pl.pallas_call(
-        functools.partial(gate_kernel, shards_of, chunks),
-        out_shape=[pltpu.HBM((channels, length), BF16)] * 4 + [pltpu.HBM((channels, length), F32)],
-        in_specs=[vmem] * (4 + chunks * shards_of),
-        out_specs=[hbm] * 5,
-        scratch_shapes=[pltpu.VMEM((3, channels, length), F32)]
-        + [pltpu.VMEM((channels, length), BF16)] * 4
-        + [pltpu.SemaphoreType.DMA((chunks, 5))],
-        compiler_params=params,
-    )(post_gate, pre_gate, signal, cotangent, *back)
+        back.append(swap(mixed[:shards_of]))
+    outs = []
+    for q in range(chunks):
+        last = q == chunks - 1
+        outs = pl.pallas_call(
+            functools.partial(gate_kernel, shards_of, chunks, q),
+            out_shape=[pltpu.HBM((channels, length), BF16)] * 4
+            + [pltpu.HBM((channels, length), F32)]
+            + [pltpu.HBM((1, channels), F32)] * last,
+            in_specs=[vmem] * (5 + shards_of) + [hbm] * len(outs),
+            out_specs=[hbm] * (5 + last),
+            scratch_shapes=[pltpu.VMEM((3, chunk_rows, length), F32)]
+            + [pltpu.VMEM((chunk_rows, length), BF16)] * 4
+            + [pltpu.SemaphoreType.DMA((6,))],
+            input_output_aliases={5 + shards_of + i: i for i in range(len(outs))},
+            compiler_params=params,
+        )(
+            post_gate,
+            pre_gate,
+            signal,
+            cotangent,
+            *back[q],
+            d_skip if last else back[q + 1][1],
+            *outs,
+        )
+    output, d_post, d_pre, d_signal, d_filter, d_skip = outs
     return (output, d_post, d_pre, d_signal, d_skip.reshape(channels), d_filter)
 
 

time: 27 us -> 26.6 us (0.985)
  waiting for transfers between devices: 4.72 us -> 3.89 us
  Pallas kernels: 5.23 us -> 5.59 us
    ppermute x12, waiting for transfers between devices: 4.72 us -> 3.89 us  [swap(): lax.ppermute(pieces[d], 'seq', [(i, i ^ d) for i in range(shards_of)])]
    pallas_call x1 -> x2, Pallas kernels: 0.98 us -> 1.64 us  [shards(): pl.pallas_call(functools.partial(gate_kernel, shards_of, chunks, q), out_...]
    pallas_call x2, Pallas kernels: 2.79 us -> 2.48 us  [shards(): pl.pallas_call(functools.partial(spectral_kernel, shards_of, chunks, last...]
  transfers between devices with their start and end apart: 12 -> 12, of which waited for: 4 -> 3; matrix products, arithmetic and copies ran while one was open for 0% -> 0% of each run, Pallas kernels for 11% -> 13%
where the time goes in v6:
time: 26.6 us; the launch traced here: 26.5 us
  starting transfers between devices  16.2 us (61%)
  Pallas kernels  5.59 us (21%)
  waiting for transfers between devices  3.89 us (15%)
  between operations  0.77 us (3%)
    ppermute x12, starting transfers between devices, swap(): lax.ppermute(pieces[d], 'seq', [(i, i ^ d) for i in range(shards_of)])  16.2 us
    ppermute x12, waiting for transfers between devices, swap(): lax.ppermute(pieces[d], 'seq', [(i, i ^ d) for i in range(shards_of)])  3.89 us
    pallas_call x2, Pallas kernels, shards(): pl.pallas_call(functools.partial(spectral_kernel, shards_of, chunks, last...  2.48 us
    pallas_call x2, Pallas kernels, shards(): pl.pallas_call(functools.partial(gate_kernel, shards_of, chunks, q), out_...  1.64 us
    pallas_call x2, Pallas kernels, shards(): pl.pallas_call(functools.partial(pack_kernel, shards_of, chunks, q), out_...  1.47 us
  transfers between devices with their start and end apart: 12, of which 3 were waited for; matrix products, arithmetic and copies ran while one was open for 0% of the time, Pallas kernels for 13%

profile of v6, /device:TPU:0, one launch (start us, length us, event | category | flops | bytes accessed | tf_op | source)
XLA Modules:
  0.0 26.5 jit_solution(272691296901214884)
XLA Ops:
  0.6 0.0 copy-start
  0.6 0.0 copy-start.1
  0.7 0.0 copy-start.2
  0.7 0.0 copy-start.3
  0.7 0.0 copy-start.5
  0.7 1.3 %shard_map.156 = (f32[192,128]{1,0:T(8,128)S(1)}, f32[192,128]{1,0:T(8,128)S(1)}, f32[192,128]{1,0:T(8,128)S(1)}, f32[192,128]{1,0:T(8,128)S(1)}) custom-call(bf16[64,1024]{1,0:T(8,128)(2,1)} %refs_0_.9, bf16[64,1024]{1,0:T(8,128)(2,1)} %refs_1_.9, bf16[64,1024]{1,0:T(8,128)(2,1)} %refs_2_.9, bf16[64,1024]{1,0:T(8,128)(2,1)} %refs_3_.9, f32[64,1024]{1,0:T(8,128)} %refs_4_.5, ...), custom_call_target="tpu_custom_call" | custom-call | tf_op jit(solution)/shard_map/pallas_call | solution.py:289
  2.0 3.0 %collective-permute-start.6 = (f32[192,128]{1,0:T(8,128)S(1)}, f32[192,128]{1,0:T(8,128)S(1)}, u32[]{:S(2)}, u32[]{:S(2)}) collective-permute-start(f32[192,128]{1,0:T(8,128)S(1)} %get-tuple-element.44), channel_id=1, source_target_pairs={{0,8},{8,0},{16,24},{24,16},{1,9},{9,1},{17,25},{25,17},{2,10},{10... | collective-permute-start | bytes 294920 | tf_op jit(solution)/shard_map/ppermute | solution.py:272
  5.0 0.0 copy-start.10
  5.0 1.5 %collective-permute-start.7 = (f32[192,128]{1,0:T(8,128)S(1)}, f32[192,128]{1,0:T(8,128)S(1)}, u32[]{:S(2)}, u32[]{:S(2)}) collective-permute-start(f32[192,128]{1,0:T(8,128)S(1)} %get-tuple-element.45), channel_id=1, source_target_pairs={{0,16},{8,24},{16,0},{24,8},{1,17},{9,25},{17,1},{25,9},{2,18},{10... | collective-permute-start | bytes 294920 | tf_op jit(solution)/shard_map/ppermute | solution.py:272
  6.5 0.0 copy-start.4
  6.5 0.0 copy-start.6
  6.5 0.0 copy-start.7
  6.5 0.0 copy-start.8
  6.5 0.0 copy-start.9
  6.5 0.1 collective-permute-start.8
  6.6 0.0 copy-done
  6.6 0.0 copy-done.1
  6.6 0.0 copy-done.2
  6.6 0.0 copy-done.3
  6.7 0.0 copy-done.5
  6.7 0.0 copy-done.10
  6.7 0.2 shard_map.154
  6.8 2.0 %collective-permute-start = (f32[200,128]{1,0:T(8,128)S(1)}, f32[200,128]{1,0:T(8,128)S(1)}, u32[]{:S(2)}, u32[]{:S(2)}) collective-permute-start(f32[200,128]{1,0:T(8,128)S(1)} %get-tuple-element.35), channel_id=1, source_target_pairs={{0,8},{8,0},{16,24},{24,16},{1,9},{9,1},{17,25},{25,17},{2,10},{10... | collective-permute-start | bytes 307208 | tf_op jit(solution)/shard_map/ppermute | solution.py:272
  8.8 1.5 %collective-permute-start.1 = (f32[200,128]{1,0:T(8,128)S(1)}, f32[200,128]{1,0:T(8,128)S(1)}, u32[]{:S(2)}, u32[]{:S(2)}) collective-permute-start(f32[200,128]{1,0:T(8,128)S(1)} %get-tuple-element.36), channel_id=1, source_target_pairs={{0,16},{8,24},{16,0},{24,8},{1,17},{9,25},{17,1},{25,9},{2,18},{10... | collective-permute-start | bytes 307208 | tf_op jit(solution)/shard_map/ppermute | solution.py:272
  10.4 0.0 collective-permute-done.6.refs_6_
  10.4 0.9 %collective-permute-start.2 = (f32[200,128]{1,0:T(8,128)S(1)}, f32[200,128]{1,0:T(8,128)S(1)}, u32[]{:S(2)}, u32[]{:S(2)}) collective-permute-start(f32[200,128]{1,0:T(8,128)S(1)} %get-tuple-element.37), channel_id=1, source_target_pairs={{0,24},{8,16},{16,8},{24,0},{1,25},{9,17},{17,9},{25,1},{2,26},{10... | collective-permute-start | bytes 307208 | tf_op jit(solution)/shard_map/ppermute | solution.py:272
  11.3 0.0 collective-permute-done.7.refs_7_
  11.3 1.7 %collective-permute-done.8.refs_8_ = f32[192,128]{1,0:T(8,128)S(1)} collective-permute-done((f32[192,128]{1,0:T(8,128)S(1)}, f32[192,128]{1,0:T(8,128)S(1)}, u32[]{:S(2)}, u32[]{:S(2)}) %collective-permute-start.8) | collective-permute-done | bytes 98336 | tf_op jit(solution)/shard_map/ppermute | solution.py:272
  13.0 0.0 copy-done.4
  13.0 0.0 copy-done.6
  13.0 0.0 copy-done.7
  13.0 0.0 copy-done.8
  13.0 0.0 copy-done.9
  13.0 1.2 %shard_map.157 = (f32[192,128]{1,0:T(8,128)S(1)}, f32[192,128]{1,0:T(8,128)S(1)}, f32[192,128]{1,0:T(8,128)S(1)}, f32[192,128]{1,0:T(8,128)S(1)}) custom-call(bf16[4,64,96]{2,1,0:T(8,128)(2,1)S(1)} %copy-done.8, bf16[4,32,192]{2,1,0:T(8,128)(2,1)S(1)} %copy-done.7, bf16[4,32,192]{2,1,0:T(8,128)(2,1)S(1)} %copy-done.6, f32[2,32,128]{2,1,0:T(8,128)S(1)} %copy-done.9, ...), custom_call_target="tpu_custom_call" | custom-call | tf_op jit(solution)/shard_map/pallas_call | solution.py:303
  14.3 0.8 %collective-permute-start.9 = (f32[192,128]{1,0:T(8,128)S(1)}, f32[192,128]{1,0:T(8,128)S(1)}, u32[]{:S(2)}, u32[]{:S(2)}) collective-permute-start(f32[192,128]{1,0:T(8,128)S(1)} %get-tuple-element.48), channel_id=1, source_target_pairs={{0,8},{8,0},{16,24},{24,16},{1,9},{9,1},{17,25},{25,17},{2,10},{10... | collective-permute-start | bytes 294920 | tf_op jit(solution)/shard_map/ppermute | solution.py:272
  15.1 0.2 collective-permute-start.10
  15.3 0.0 collective-permute-done.refs_6_
  15.3 2.5 %collective-permute-start.11 = (f32[192,128]{1,0:T(8,128)S(1)}, f32[192,128]{1,0:T(8,128)S(1)}, u32[]{:S(2)}, u32[]{:S(2)}) collective-permute-start(f32[192,128]{1,0:T(8,128)S(1)} %get-tuple-element.50), channel_id=1, source_target_pairs={{0,24},{8,16},{16,8},{24,0},{1,25},{9,17},{17,9},{25,1},{2,26},{10... | collective-permute-start | bytes 294920 | tf_op jit(solution)/shard_map/ppermute | solution.py:272
  17.8 0.0 collective-permute-done.1.refs_7_
  17.8 0.0 collective-permute-done.2.refs_8_
  17.8 1.2 %shard_map.155 = (f32[192,128]{1,0:T(8,128)S(1)}, f32[192,128]{1,0:T(8,128)S(1)}, f32[192,128]{1,0:T(8,128)S(1)}, f32[192,128]{1,0:T(8,128)S(1)}, f32[1,64]{1,0:T(1,128)S(1)}) custom-call(bf16[4,64,96]{2,1,0:T(8,128)(2,1)S(1)} %copy-done.8, bf16[4,32,192]{2,1,0:T(8,128)(2,1)S(1)} %copy-done.7, bf16[4,32,192]{2,1,0:T(8,128)(2,1)S(1)} %copy-done.6, ...), custom_call_target="tpu_custom_call" | custom-call | tf_op jit(solution)/shard_map/pallas_call | solution.py:303
  19.1 0.8 %collective-permute-start.3 = (f32[192,128]{1,0:T(8,128)S(1)}, f32[192,128]{1,0:T(8,128)S(1)}, u32[]{:S(2)}, u32[]{:S(2)}) collective-permute-start(f32[192,128]{1,0:T(8,128)S(1)} %get-tuple-element.39), channel_id=1, source_target_pairs={{0,8},{8,0},{16,24},{24,16},{1,9},{9,1},{17,25},{25,17},{2,10},{10... | collective-permute-start | bytes 294920 | tf_op jit(solution)/shard_map/ppermute | solution.py:272
  19.9 0.2 collective-permute-start.4
  20.1 0.0 collective-permute-done.9.refs_5_
  20.1 2.5 %collective-permute-start.5 = (f32[192,128]{1,0:T(8,128)S(1)}, f32[192,128]{1,0:T(8,128)S(1)}, u32[]{:S(2)}, u32[]{:S(2)}) collective-permute-start(f32[192,128]{1,0:T(8,128)S(1)} %get-tuple-element.41), channel_id=1, source_target_pairs={{0,24},{8,16},{16,8},{24,0},{1,25},{9,17},{17,9},{25,1},{2,26},{10... | collective-permute-start | bytes 294920 | tf_op jit(solution)/shard_map/ppermute | solution.py:272
  22.6 0.0 collective-permute-done.10.refs_6_
  22.7 0.0 collective-permute-done.11.refs_7_
  22.7 1.1 %collective-permute-done.3.refs_8_.refs_5_ = f32[192,128]{1,0:T(8,128)S(1)} collective-permute-done((f32[192,128]{1,0:T(8,128)S(1)}, f32[192,128]{1,0:T(8,128)S(1)}, u32[]{:S(2)}, u32[]{:S(2)}) %collective-permute-start.3) | collective-permute-done | bytes 98336 | tf_op jit(solution)/shard_map/ppermute | solution.py:272
  23.8 0.8 %shard_map.158 = (bf16[64,1024]{1,0:T(8,128)(2,1)}, bf16[64,1024]{1,0:T(8,128)(2,1)}, bf16[64,1024]{1,0:T(8,128)(2,1)}, bf16[64,1024]{1,0:T(8,128)(2,1)}, f32[64,1024]{1,0:T(8,128)}) custom-call(bf16[64,1024]{1,0:T(8,128)(2,1)S(1)} %copy-done, bf16[64,1024]{1,0:T(8,128)(2,1)S(1)} %copy-done.1, bf16[64,1024]{1,0:T(8,128)(2,1)S(1)} %copy-done.2, ...), custom_call_target="tpu_custom_call" | custom-call | tf_op jit(solution)/shard_map/pallas_call | solution.py:320
  24.6 0.0 collective-permute-done.4.refs_6_
  24.6 1.0 %collective-permute-done.5.refs_7_ = f32[192,128]{1,0:T(8,128)S(1)} collective-permute-done((f32[192,128]{1,0:T(8,128)S(1)}, f32[192,128]{1,0:T(8,128)S(1)}, u32[]{:S(2)}, u32[]{:S(2)}) %collective-permute-start.5) | collective-permute-done | bytes 98336 | tf_op jit(solution)/shard_map/ppermute | solution.py:272
  25.7 0.8 %shard_map.159 = (bf16[64,1024]{1,0:T(8,128)(2,1)}, bf16[64,1024]{1,0:T(8,128)(2,1)}, bf16[64,1024]{1,0:T(8,128)(2,1)}, bf16[64,1024]{1,0:T(8,128)(2,1)}, f32[64,1024]{1,0:T(8,128)}, /*index=5*/f32[1,64]{1,0:T(1,128)}) custom-call(bf16[64,1024]{1,0:T(8,128)(2,1)S(1)} %copy-done, ...), custom_call_target="tpu_custom_call", output_to_operand_aliasing={{0}: (9, {}), {1}: (10, {}), {2}: (11, {}), {3}: (12, {}), ... | custom-call | tf_op jit(solution)/shard_map/pallas_call | solution.py:320
Async XLA Ops:
  0.6 6.0 %copy-start = (bf16[64,1024]{1,0:T(8,128)(2,1)S(1)}, bf16[64,1024]{1,0:T(8,128)(2,1)}, u32[]{:S(2)}) copy-start(bf16[64,1024]{1,0:T(8,128)(2,1)} %refs_0_.9) | copy-start | bytes 393220
  0.6 6.0 %copy-start.1 = (bf16[64,1024]{1,0:T(8,128)(2,1)S(1)}, bf16[64,1024]{1,0:T(8,128)(2,1)}, u32[]{:S(2)}) copy-start(bf16[64,1024]{1,0:T(8,128)(2,1)} %refs_1_.9) | copy-start | bytes 393220
  0.7 6.0 %copy-start.2 = (bf16[64,1024]{1,0:T(8,128)(2,1)S(1)}, bf16[64,1024]{1,0:T(8,128)(2,1)}, u32[]{:S(2)}) copy-start(bf16[64,1024]{1,0:T(8,128)(2,1)} %refs_2_.9) | copy-start | bytes 393220
  0.7 6.0 %copy-start.3 = (bf16[64,1024]{1,0:T(8,128)(2,1)S(1)}, bf16[64,1024]{1,0:T(8,128)(2,1)}, u32[]{:S(2)}) copy-start(bf16[64,1024]{1,0:T(8,128)(2,1)} %refs_3_.9) | copy-start | bytes 393220
  0.7 6.0 %copy-start.5 = (f32[64,1024]{1,0:T(8,128)S(1)}, f32[64,1024]{1,0:T(8,128)}, u32[]{:S(2)}) copy-start(f32[64,1024]{1,0:T(8,128)} %refs_4_.5) | copy-start | bytes 786436
  2.0 8.4 %collective-permute-start.6 = (f32[192,128]{1,0:T(8,128)S(1)}, f32[192,128]{1,0:T(8,128)S(1)}, u32[]{:S(2)}, u32[]{:S(2)}) collective-permute-start(f32[192,128]{1,0:T(8,128)S(1)} %get-tuple-element.44), channel_id=1, source_target_pairs={{0,8},{8,0},{16,24},{24,16},{1,9},{9,1},{17,25},{25,17},{2,10},{10... | collective-permute-start | bytes 294920 | tf_op jit(solution)/shard_map/ppermute | solution.py:272
  5.0 1.7 %copy-start.10 = (f32[64]{0:T(128)S(1)}, f32[64]{0:T(128)}, u32[]{:S(2)}) copy-start(f32[64]{0:T(128)} %param.16) | copy-start | bytes 772
  5.0 6.3 %collective-permute-start.7 = (f32[192,128]{1,0:T(8,128)S(1)}, f32[192,128]{1,0:T(8,128)S(1)}, u32[]{:S(2)}, u32[]{:S(2)}) collective-permute-start(f32[192,128]{1,0:T(8,128)S(1)} %get-tuple-element.45), channel_id=1, source_target_pairs={{0,16},{8,24},{16,0},{24,8},{1,17},{9,25},{17,1},{25,9},{2,18},{10... | collective-permute-start | bytes 294920 | tf_op jit(solution)/shard_map/ppermute | solution.py:272
  6.5 6.5 %copy-start.4 = (bf16[768,256]{1,0:T(8,128)(2,1)S(1)}, bf16[768,256]{1,0:T(8,128)(2,1)}, u32[]{:S(2)}) copy-start(bf16[768,256]{1,0:T(8,128)(2,1)} %constant.14.clone.refs_4_) | copy-start | bytes 1179652
  6.5 6.5 %copy-start.6 = (bf16[4,32,192]{2,1,0:T(8,128)(2,1)S(1)}, bf16[4,32,192]{2,1,0:T(8,128)(2,1)}, u32[]{:S(2)}) copy-start(bf16[4,32,192]{2,1,0:T(8,128)(2,1)} %constant.12.clone.refs_2_) | copy-start | bytes 147460
  6.5 6.5 %copy-start.7 = (bf16[4,32,192]{2,1,0:T(8,128)(2,1)S(1)}, bf16[4,32,192]{2,1,0:T(8,128)(2,1)}, u32[]{:S(2)}) copy-start(bf16[4,32,192]{2,1,0:T(8,128)(2,1)} %constant.11.clone.refs_1_) | copy-start | bytes 147460
  6.5 6.5 %copy-start.8 = (bf16[4,64,96]{2,1,0:T(8,128)(2,1)S(1)}, bf16[4,64,96]{2,1,0:T(8,128)(2,1)}, u32[]{:S(2)}) copy-start(bf16[4,64,96]{2,1,0:T(8,128)(2,1)} %constant.10.clone.refs_0_) | copy-start | bytes 147460
  6.5 6.5 %copy-start.9 = (f32[2,32,128]{2,1,0:T(8,128)S(1)}, f32[2,32,128]{2,1,0:T(8,128)}, u32[]{:S(2)}) copy-start(f32[2,32,128]{2,1,0:T(8,128)} %constant.13.clone.refs_3_) | copy-start | bytes 98308
  6.5 6.5 %collective-permute-start.8 = (f32[192,128]{1,0:T(8,128)S(1)}, f32[192,128]{1,0:T(8,128)S(1)}, u32[]{:S(2)}, u32[]{:S(2)}) collective-permute-start(f32[192,128]{1,0:T(8,128)S(1)} %get-tuple-element.46), channel_id=1, source_target_pairs={{0,24},{8,16},{16,8},{24,0},{1,25},{9,17},{17,9},{25,1},{2,26},{10... | collective-permute-start | bytes 294920 | tf_op jit(solution)/shard_map/ppermute | solution.py:272
  6.8 8.5 %collective-permute-start = (f32[200,128]{1,0:T(8,128)S(1)}, f32[200,128]{1,0:T(8,128)S(1)}, u32[]{:S(2)}, u32[]{:S(2)}) collective-permute-start(f32[200,128]{1,0:T(8,128)S(1)} %get-tuple-element.35), channel_id=1, source_target_pairs={{0,8},{8,0},{16,24},{24,16},{1,9},{9,1},{17,25},{25,17},{2,10},{10... | collective-permute-start | bytes 307208 | tf_op jit(solution)/shard_map/ppermute | solution.py:272
  8.8 9.0 %collective-permute-start.1 = (f32[200,128]{1,0:T(8,128)S(1)}, f32[200,128]{1,0:T(8,128)S(1)}, u32[]{:S(2)}, u32[]{:S(2)}) collective-permute-start(f32[200,128]{1,0:T(8,128)S(1)} %get-tuple-element.36), channel_id=1, source_target_pairs={{0,16},{8,24},{16,0},{24,8},{1,17},{9,25},{17,1},{25,9},{2,18},{10... | collective-permute-start | bytes 307208 | tf_op jit(solution)/shard_map/ppermute | solution.py:272
  10.4 7.5 %collective-permute-start.2 = (f32[200,128]{1,0:T(8,128)S(1)}, f32[200,128]{1,0:T(8,128)S(1)}, u32[]{:S(2)}, u32[]{:S(2)}) collective-permute-start(f32[200,128]{1,0:T(8,128)S(1)} %get-tuple-element.37), channel_id=1, source_target_pairs={{0,24},{8,16},{16,8},{24,0},{1,25},{9,17},{17,9},{25,1},{2,26},{10... | collective-permute-start | bytes 307208 | tf_op jit(solution)/shard_map/ppermute | solution.py:272
  14.3 5.9 %collective-permute-start.9 = (f32[192,128]{1,0:T(8,128)S(1)}, f32[192,128]{1,0:T(8,128)S(1)}, u32[]{:S(2)}, u32[]{:S(2)}) collective-permute-start(f32[192,128]{1,0:T(8,128)S(1)} %get-tuple-element.48), channel_id=1, source_target_pairs={{0,8},{8,0},{16,24},{24,16},{1,9},{9,1},{17,25},{25,17},{2,10},{10... | collective-permute-start | bytes 294920 | tf_op jit(solution)/shard_map/ppermute | solution.py:272
  15.1 7.5 %collective-permute-start.10 = (f32[192,128]{1,0:T(8,128)S(1)}, f32[192,128]{1,0:T(8,128)S(1)}, u32[]{:S(2)}, u32[]{:S(2)}) collective-permute-start(f32[192,128]{1,0:T(8,128)S(1)} %get-tuple-element.49), channel_id=1, source_target_pairs={{0,16},{8,24},{16,0},{24,8},{1,17},{9,25},{17,1},{25,9},{2,18},{10... | collective-permute-start | bytes 294920 | tf_op jit(solution)/shard_map/ppermute | solution.py:272
  15.3 7.3 %collective-permute-start.11 = (f32[192,128]{1,0:T(8,128)S(1)}, f32[192,128]{1,0:T(8,128)S(1)}, u32[]{:S(2)}, u32[]{:S(2)}) collective-permute-start(f32[192,128]{1,0:T(8,128)S(1)} %get-tuple-element.50), channel_id=1, source_target_pairs={{0,24},{8,16},{16,8},{24,0},{1,25},{9,17},{17,9},{25,1},{2,26},{10... | collective-permute-start | bytes 294920 | tf_op jit(solution)/shard_map/ppermute | solution.py:272
  19.1 4.7 %collective-permute-start.3 = (f32[192,128]{1,0:T(8,128)S(1)}, f32[192,128]{1,0:T(8,128)S(1)}, u32[]{:S(2)}, u32[]{:S(2)}) collective-permute-start(f32[192,128]{1,0:T(8,128)S(1)} %get-tuple-element.39), channel_id=1, source_target_pairs={{0,8},{8,0},{16,24},{24,16},{1,9},{9,1},{17,25},{25,17},{2,10},{10... | collective-permute-start | bytes 294920 | tf_op jit(solution)/shard_map/ppermute | solution.py:272
  19.9 4.7 %collective-permute-start.4 = (f32[192,128]{1,0:T(8,128)S(1)}, f32[192,128]{1,0:T(8,128)S(1)}, u32[]{:S(2)}, u32[]{:S(2)}) collective-permute-start(f32[192,128]{1,0:T(8,128)S(1)} %get-tuple-element.40), channel_id=1, source_target_pairs={{0,16},{8,24},{16,0},{24,8},{1,17},{9,25},{17,1},{25,9},{2,18},{10... | collective-permute-start | bytes 294920 | tf_op jit(solution)/shard_map/ppermute | solution.py:272
  20.1 5.5 %collective-permute-start.5 = (f32[192,128]{1,0:T(8,128)S(1)}, f32[192,128]{1,0:T(8,128)S(1)}, u32[]{:S(2)}, u32[]{:S(2)}) collective-permute-start(f32[192,128]{1,0:T(8,128)S(1)} %get-tuple-element.41), channel_id=1, source_target_pairs={{0,24},{8,16},{16,8},{24,0},{1,25},{9,17},{17,9},{25,1},{2,26},{10... | collective-permute-start | bytes 294920 | tf_op jit(solution)/shard_map/ppermute | solution.py:272

commit v7 on v4

--- a/solution.py
+++ b/solution.py
@@ -53,13 +53,13 @@
     inner = 2 * np.pi * (q[:, None] * q[None, :] % LANES) / LANES
     dft = np.block([[np.cos(inner), -np.sin(inner)], [np.sin(inner), np.cos(inner)]])
     dft_high, dft_low = halves(dft)
-    return outer_w, inverse_w, filter_w, twiddle, np.concatenate([dft_high, dft_high, dft_low])
+    return outer_w, inverse_w, filter_w, twiddle, np.concatenate([dft_high, dft_low], axis=1)
 
 
 def triple(x, axis):
     high = x.astype(BF16)
     low = (x - high.astype(F32)).astype(BF16)
-    return jnp.concatenate([high, low, high], axis=axis)
+    return jnp.concatenate([high, low, high] if axis == 0 else [high, low], axis=axis)
 
 
 def matmul(a, b):
@@ -79,8 +79,8 @@
             pltpu.make_async_copy(source.at[rows, :] if i < 5 else source, copied, sems.at[i])
             for i, (source, copied) in enumerate(zip(sources, held))
         ]
-        for copy in copies:
-            copy.start()
+        for i, copy in enumerate(copies):
+            copy.start(priority=i % 2)
         for copy in copies:
             copy.wait()
         sources = held
@@ -155,7 +155,13 @@
 
     def inner(f):
         rows = slice(f * spectrum_rows, (f + 1) * spectrum_rows)
-        spectra[rows, :] = matmul(packed[rows, :], dft[...])
+        x = packed[rows, :]
+        wide = matmul(x[:, : 2 * LANES], dft[...])
+        spectra[rows, :] = (
+            wide[:, : 2 * LANES]
+            + wide[:, 2 * LANES :]
+            + matmul(x[:, 2 * LANES :], dft[:, : 2 * LANES])
+        )
 
     for f in range(3):
         for c in range(0, width, 2):
@@ -197,11 +203,16 @@
                     ]
 
 
-def gate_kernel(shards_of, chunks, *refs):
-    post, pre, signal, cotangent = refs[:4]
-    pieces = refs[4 : 4 + chunks * shards_of]
-    refs = refs[4 + chunks * shards_of :]
-    outs, (fields, output, d_post, d_pre, d_signal, sems) = refs[:5], refs[5:]
+def gate_kernel(shards_of, chunks, work, first, *refs):
+    post, pre, signal, cotangent, skip = refs[:5]
+    refs = refs[5:]
+    pieces = []
+    for _, distances in work:
+        pieces.append(refs[: len(distances)])
+        refs = refs[len(distances) :]
+    refs = refs[0 if first else 5 :]
+    outs, refs = refs[: 5 + first], refs[5 + first :]
+    *held, sems = refs
     me = lax.axis_index("seq")
     channels, length = post.shape
     chunk_rows = channels // chunks
@@ -209,39 +220,43 @@
     per = length // LANES
     field_rows = width * per
     copies = []
-
-    def ship(q, i, held):
-        rows = pl.ds(q * chunk_rows, chunk_rows)
-        copy = pltpu.make_async_copy(held.at[rows, :], outs[i].at[rows, :], sems.at[q, i])
-        copy.start()
-        copies.append(copy)
-
-    def gather(q, f):
-        for d in range(shards_of):
-            for c in range(0, width, SUBLANES):
-                top = q * chunk_rows + (me ^ d) * width + c
-                held = pl.ds(pl.multiple_of(top, SUBLANES), SUBLANES)
-                for a in range(per):
-                    fields[f, held, a * LANES : (a + 1) * LANES] = pieces[q * shards_of + d][
-                        pl.ds(f * field_rows + c * per + a, SUBLANES, stride=per), :
-                    ]
-
-    for q in range(chunks):
-        rows = slice(q * chunk_rows, (q + 1) * chunk_rows)
-        gather(q, 2)
-        ship(q, 4, fields.at[2])
-        gather(q, 0)
-        conved = fields[0, rows, :]
-        output[rows, :] = (post[rows, :].astype(F32) * conved).astype(BF16)
-        ship(q, 0, output)
-        d_post[rows, :] = (cotangent[rows, :].astype(F32) * conved).astype(BF16)
-        ship(q, 1, d_post)
-        gather(q, 1)
-        d_gated = fields[1, rows, :]
-        d_pre[rows, :] = (signal[rows, :].astype(F32) * d_gated).astype(BF16)
-        ship(q, 2, d_pre)
-        d_signal[rows, :] = (pre[rows, :].astype(F32) * d_gated).astype(BF16)
-        ship(q, 3, d_signal)
+    if first:
+        copies.append(pltpu.make_async_copy(skip, outs[5], sems.at[0, 5]))
+        copies[0].start()
+    for item, (q, distances) in enumerate(work):
+        fields, output, d_post, d_pre, d_signal = held[5 * item : 5 * item + 5]
+        count = len(distances)
+        tile = q * chunk_rows + (me ^ distances[0]) // count * (count * width)
+        rows = pl.ds(pl.multiple_of(tile, 16), count * width)
+
+        def ship(i, filled):
+            copies.append(pltpu.make_async_copy(filled, outs[i].at[rows, :], sems.at[item, i]))
+            copies[-1].start()
+
+        def gather(f):
+            for d, piece in zip(distances, pieces[item]):
+                for c in range(0, width, SUBLANES):
+                    top = (me ^ d) % count * width + c
+                    to = pl.ds(pl.multiple_of(top, SUBLANES), SUBLANES)
+                    for a in range(per):
+                        fields[f, to, a * LANES : (a + 1) * LANES] = piece[
+                            pl.ds(f * field_rows + c * per + a, SUBLANES, stride=per), :
+                        ]
+
+        gather(2)
+        ship(4, fields.at[2])
+        gather(0)
+        conved = fields[0]
+        output[...] = (post[rows, :].astype(F32) * conved).astype(BF16)
+        ship(0, output)
+        d_post[...] = (cotangent[rows, :].astype(F32) * conved).astype(BF16)
+        ship(1, d_post)
+        gather(1)
+        d_gated = fields[1]
+        d_pre[...] = (signal[rows, :].astype(F32) * d_gated).astype(BF16)
+        ship(2, d_pre)
+        d_signal[...] = (pre[rows, :].astype(F32) * d_gated).astype(BF16)
+        ship(3, d_signal)
     for copy in copies:
         copy.wait()
 
@@ -299,24 +314,45 @@
             out_specs=[vmem] * (shards_of + last),
             scratch_shapes=[
                 pltpu.VMEM((3 * spectrum_rows, 2 * LANES), F32),
-                pltpu.VMEM((3 * spectrum_rows, 6 * LANES), BF16),
+                pltpu.VMEM((3 * spectrum_rows, 4 * LANES), BF16),
             ],
             compiler_params=params,
         )(*consts, *arrived[q])
         if last:
             d_skip = mixed[shards_of]
-        back += swap(mixed[:shards_of])
-    output, d_post, d_pre, d_signal, d_filter = pl.pallas_call(
-        functools.partial(gate_kernel, shards_of, chunks),
-        out_shape=[pltpu.HBM((channels, length), BF16)] * 4 + [pltpu.HBM((channels, length), F32)],
-        in_specs=[vmem] * (4 + chunks * shards_of),
-        out_specs=[hbm] * 5,
-        scratch_shapes=[pltpu.VMEM((3, channels, length), F32)]
-        + [pltpu.VMEM((channels, length), BF16)] * 4
-        + [pltpu.SemaphoreType.DMA((chunks, 5))],
-        compiler_params=params,
-    )(post_gate, pre_gate, signal, cotangent, *back)
-    return (output, d_post, d_pre, d_signal, d_skip.reshape(channels), d_filter)
+        back.append(swap(mixed[:shards_of]))
+    whole = tuple(range(shards_of))
+    if shards_of == 4 and chunks > 1 and width == SUBLANES:
+        calls = [[(q, whole) for q in range(chunks - 1)] + [(chunks - 1, (0, 1))]]
+        calls.append([(chunks - 1, (2, 3))])
+    else:
+        calls = [[(q, whole) for q in range(chunks)]]
+    outs = []
+    for work in calls:
+        first = not outs
+        taken = [back[q][d] for q, distances in work for d in distances]
+        scratch = []
+        for _, distances in work:
+            count = len(distances) * width
+            scratch += [pltpu.VMEM((3, count, length), F32)]
+            scratch += [pltpu.VMEM((count, length), BF16)] * 4
+        filled = pl.pallas_call(
+            functools.partial(gate_kernel, shards_of, chunks, work, first),
+            out_shape=[pltpu.HBM((channels, length), BF16)] * 4
+            + [pltpu.HBM((channels, length), F32)]
+            + [pltpu.HBM((1, channels), F32)] * first,
+            in_specs=[vmem] * (5 + len(taken)) + [hbm] * len(outs),
+            out_specs=[hbm] * (5 + first),
+            scratch_shapes=scratch + [pltpu.SemaphoreType.DMA((len(work), 6))],
+            input_output_aliases={5 + len(taken) + i: i for i in range(len(outs))},
+            compiler_params=params,
+        )(post_gate, pre_gate, signal, cotangent, d_skip, *taken, *outs)
+        if first:
+            *outs, d_skip_out = filled
+        else:
+            outs = filled
+    output, d_post, d_pre, d_signal, d_filter = outs
+    return (output, d_post, d_pre, d_signal, d_skip_out.reshape(channels), d_filter)
 
 
 def solution(mesh):

time: 27 us -> 26.5 us (0.981)
  waiting for transfers between devices: 4.72 us -> 3.78 us
  Pallas kernels: 5.23 us -> 5.55 us
    ppermute x12, waiting for transfers between devices: 4.72 us -> 3.78 us  [swap(): lax.ppermute(pieces[d], 'seq', [(i, i ^ d) for i in range(shards_of)])]
    pallas_call x1 -> x2, Pallas kernels: 0.98 us -> 1.69 us  [shards(): pl.pallas_call(functools.partial(gate_kernel, shards_of, chunks, work, fi...]
    pallas_call x2, Pallas kernels: 2.79 us -> 2.43 us  [shards(): pl.pallas_call(functools.partial(spectral_kernel, shards_of, chunks, last...]
  transfers between devices with their start and end apart: 12 -> 12, of which waited for: 4 -> 3; matrix products, arithmetic and copies ran while one was open for 0% -> 0% of each run, Pallas kernels for 11% -> 13%
where the time goes in v7:
time: 26.5 us; the launch traced here: 26.3 us
  starting transfers between devices  16.2 us (61%)
  Pallas kernels  5.55 us (21%)
  waiting for transfers between devices  3.78 us (14%)
  between operations  0.77 us (3%)
    ppermute x12, starting transfers between devices, swap(): lax.ppermute(pieces[d], 'seq', [(i, i ^ d) for i in range(shards_of)])  16.2 us
    ppermute x12, waiting for transfers between devices, swap(): lax.ppermute(pieces[d], 'seq', [(i, i ^ d) for i in range(shards_of)])  3.78 us
    pallas_call x2, Pallas kernels, shards(): pl.pallas_call(functools.partial(spectral_kernel, shards_of, chunks, last...  2.43 us
    pallas_call x2, Pallas kernels, shards(): pl.pallas_call(functools.partial(gate_kernel, shards_of, chunks, work, fi...  1.69 us
    pallas_call x2, Pallas kernels, shards(): pl.pallas_call(functools.partial(pack_kernel, shards_of, chunks, q), out_...  1.43 us
  transfers between devices with their start and end apart: 12, of which 3 were waited for; matrix products, arithmetic and copies ran while one was open for 0% of the time, Pallas kernels for 13%

profile of v7, /device:TPU:0, one launch (start us, length us, event | category | flops | bytes accessed | tf_op | source)
XLA Modules:
  0.0 26.3 jit_solution(16161186377410195943)
XLA Ops:
  0.6 0.0 copy-start
  0.6 0.0 copy-start.1
  0.7 0.0 copy-start.2
  0.7 0.0 copy-start.3
  0.7 0.0 copy-start.5
  0.7 1.3 %shard_map.156 = (f32[192,128]{1,0:T(8,128)S(1)}, f32[192,128]{1,0:T(8,128)S(1)}, f32[192,128]{1,0:T(8,128)S(1)}, f32[192,128]{1,0:T(8,128)S(1)}) custom-call(bf16[64,1024]{1,0:T(8,128)(2,1)} %refs_0_.9, bf16[64,1024]{1,0:T(8,128)(2,1)} %refs_1_.9, bf16[64,1024]{1,0:T(8,128)(2,1)} %refs_2_.9, bf16[64,1024]{1,0:T(8,128)(2,1)} %refs_3_.9, f32[64,1024]{1,0:T(8,128)} %refs_4_.5, ...), custom_call_target="tpu_custom_call" | custom-call | tf_op jit(solution)/shard_map/pallas_call | solution.py:296
  1.9 3.0 %collective-permute-start.5 = (f32[192,128]{1,0:T(8,128)S(1)}, f32[192,128]{1,0:T(8,128)S(1)}, u32[]{:S(2)}, u32[]{:S(2)}) collective-permute-start(f32[192,128]{1,0:T(8,128)S(1)} %get-tuple-element.42), channel_id=1, source_target_pairs={{0,8},{8,0},{16,24},{24,16},{1,9},{9,1},{17,25},{25,17},{2,10},{10... | collective-permute-start | bytes 294920 | tf_op jit(solution)/shard_map/ppermute | solution.py:279
  5.0 0.0 copy-start.10
  5.0 1.5 %collective-permute-start.6 = (f32[192,128]{1,0:T(8,128)S(1)}, f32[192,128]{1,0:T(8,128)S(1)}, u32[]{:S(2)}, u32[]{:S(2)}) collective-permute-start(f32[192,128]{1,0:T(8,128)S(1)} %get-tuple-element.43), channel_id=1, source_target_pairs={{0,16},{8,24},{16,0},{24,8},{1,17},{9,25},{17,1},{25,9},{2,18},{10... | collective-permute-start | bytes 294920 | tf_op jit(solution)/shard_map/ppermute | solution.py:279
  6.5 0.0 copy-start.4
  6.5 0.0 copy-start.6
  6.5 0.0 copy-start.7
  6.5 0.0 copy-start.8
  6.5 0.0 copy-start.9
  6.5 0.1 collective-permute-start.7
  6.6 0.0 copy-done
  6.6 0.0 copy-done.1
  6.6 0.0 copy-done.2
  6.6 0.0 copy-done.3
  6.6 0.0 copy-done.5
  6.6 0.0 copy-done.10
  6.6 0.2 shard_map.154
  6.8 2.0 %collective-permute-start = (f32[200,128]{1,0:T(8,128)S(1)}, f32[200,128]{1,0:T(8,128)S(1)}, u32[]{:S(2)}, u32[]{:S(2)}) collective-permute-start(f32[200,128]{1,0:T(8,128)S(1)} %get-tuple-element.35), channel_id=1, source_target_pairs={{0,8},{8,0},{16,24},{24,16},{1,9},{9,1},{17,25},{25,17},{2,10},{10... | collective-permute-start | bytes 307208 | tf_op jit(solution)/shard_map/ppermute | solution.py:279
  8.8 1.5 %collective-permute-start.1 = (f32[200,128]{1,0:T(8,128)S(1)}, f32[200,128]{1,0:T(8,128)S(1)}, u32[]{:S(2)}, u32[]{:S(2)}) collective-permute-start(f32[200,128]{1,0:T(8,128)S(1)} %get-tuple-element.36), channel_id=1, source_target_pairs={{0,16},{8,24},{16,0},{24,8},{1,17},{9,25},{17,1},{25,9},{2,18},{10... | collective-permute-start | bytes 307208 | tf_op jit(solution)/shard_map/ppermute | solution.py:279
  10.3 0.0 collective-permute-done.5.refs_6_
  10.3 0.9 %collective-permute-start.2 = (f32[200,128]{1,0:T(8,128)S(1)}, f32[200,128]{1,0:T(8,128)S(1)}, u32[]{:S(2)}, u32[]{:S(2)}) collective-permute-start(f32[200,128]{1,0:T(8,128)S(1)} %get-tuple-element.37), channel_id=1, source_target_pairs={{0,24},{8,16},{16,8},{24,0},{1,25},{9,17},{17,9},{25,1},{2,26},{10... | collective-permute-start | bytes 307208 | tf_op jit(solution)/shard_map/ppermute | solution.py:279
  11.3 0.0 collective-permute-done.6.refs_7_
  11.3 1.7 %collective-permute-done.7.refs_8_ = f32[192,128]{1,0:T(8,128)S(1)} collective-permute-done((f32[192,128]{1,0:T(8,128)S(1)}, f32[192,128]{1,0:T(8,128)S(1)}, u32[]{:S(2)}, u32[]{:S(2)}) %collective-permute-start.7) | collective-permute-done | bytes 98336 | tf_op jit(solution)/shard_map/ppermute | solution.py:279
  13.0 0.0 copy-done.4
  13.0 0.0 copy-done.6
  13.0 0.0 copy-done.7
  13.0 0.0 copy-done.8
  13.0 0.0 copy-done.9
  13.0 1.2 %shard_map.157 = (f32[192,128]{1,0:T(8,128)S(1)}, f32[192,128]{1,0:T(8,128)S(1)}, f32[192,128]{1,0:T(8,128)S(1)}, f32[192,128]{1,0:T(8,128)S(1)}) custom-call(bf16[4,64,96]{2,1,0:T(8,128)(2,1)S(1)} %copy-done.8, bf16[4,32,192]{2,1,0:T(8,128)(2,1)S(1)} %copy-done.7, bf16[4,32,192]{2,1,0:T(8,128)(2,1)S(1)} %copy-done.6, f32[2,32,128]{2,1,0:T(8,128)S(1)} %copy-done.9, ...), custom_call_target="tpu_custom_call" | custom-call | tf_op jit(solution)/shard_map/pallas_call | solution.py:310
  14.2 0.8 %collective-permute-start.8 = (f32[192,128]{1,0:T(8,128)S(1)}, f32[192,128]{1,0:T(8,128)S(1)}, u32[]{:S(2)}, u32[]{:S(2)}) collective-permute-start(f32[192,128]{1,0:T(8,128)S(1)} %get-tuple-element.46), channel_id=1, source_target_pairs={{0,8},{8,0},{16,24},{24,16},{1,9},{9,1},{17,25},{25,17},{2,10},{10... | collective-permute-start | bytes 294920 | tf_op jit(solution)/shard_map/ppermute | solution.py:279
  15.1 0.2 collective-permute-start.9
  15.3 0.0 collective-permute-done.refs_6_
  15.3 2.5 %collective-permute-start.10 = (f32[192,128]{1,0:T(8,128)S(1)}, f32[192,128]{1,0:T(8,128)S(1)}, u32[]{:S(2)}, u32[]{:S(2)}) collective-permute-start(f32[192,128]{1,0:T(8,128)S(1)} %get-tuple-element.48), channel_id=1, source_target_pairs={{0,24},{8,16},{16,8},{24,0},{1,25},{9,17},{17,9},{25,1},{2,26},{10... | collective-permute-start | bytes 294920 | tf_op jit(solution)/shard_map/ppermute | solution.py:279
  17.8 0.0 collective-permute-done.1.refs_7_
  17.8 0.0 collective-permute-done.2.refs_8_
  17.8 1.2 %shard_map.155 = (f32[192,128]{1,0:T(8,128)S(1)}, f32[192,128]{1,0:T(8,128)S(1)}, f32[192,128]{1,0:T(8,128)S(1)}, f32[192,128]{1,0:T(8,128)S(1)}, f32[1,64]{1,0:T(1,128)S(1)}) custom-call(bf16[4,64,96]{2,1,0:T(8,128)(2,1)S(1)} %copy-done.8, bf16[4,32,192]{2,1,0:T(8,128)(2,1)S(1)} %copy-done.7, bf16[4,32,192]{2,1,0:T(8,128)(2,1)S(1)} %copy-done.6, ...), custom_call_target="tpu_custom_call" | custom-call | tf_op jit(solution)/shard_map/pallas_call | solution.py:310
  19.0 0.8 %collective-permute-start.11 = (f32[192,128]{1,0:T(8,128)S(1)}, f32[192,128]{1,0:T(8,128)S(1)}, u32[]{:S(2)}, u32[]{:S(2)}) collective-permute-start(f32[192,128]{1,0:T(8,128)S(1)} %get-tuple-element.50), channel_id=1, source_target_pairs={{0,8},{8,0},{16,24},{24,16},{1,9},{9,1},{17,25},{25,17},{2,10},{10... | collective-permute-start | bytes 294920 | tf_op jit(solution)/shard_map/ppermute | solution.py:279
  19.8 0.2 collective-permute-start.3
  20.1 0.0 collective-permute-done.8.refs_6_
  20.1 2.5 %collective-permute-start.4 = (f32[192,128]{1,0:T(8,128)S(1)}, f32[192,128]{1,0:T(8,128)S(1)}, u32[]{:S(2)}, u32[]{:S(2)}) collective-permute-start(f32[192,128]{1,0:T(8,128)S(1)} %get-tuple-element.40), channel_id=1, source_target_pairs={{0,24},{8,16},{16,8},{24,0},{1,25},{9,17},{17,9},{25,1},{2,26},{10... | collective-permute-start | bytes 294920 | tf_op jit(solution)/shard_map/ppermute | solution.py:279
  22.6 0.0 collective-permute-done.9.refs_7_
  22.6 0.0 collective-permute-done.10.refs_8_
  22.6 1.1 %collective-permute-done.11.refs_10_ = f32[192,128]{1,0:T(8,128)S(1)} collective-permute-done((f32[192,128]{1,0:T(8,128)S(1)}, f32[192,128]{1,0:T(8,128)S(1)}, u32[]{:S(2)}, u32[]{:S(2)}) %collective-permute-start.11) | collective-permute-done | bytes 98336 | tf_op jit(solution)/shard_map/ppermute | solution.py:279
  23.7 0.9 %shard_map.158 = (bf16[64,1024]{1,0:T(8,128)(2,1)}, bf16[64,1024]{1,0:T(8,128)(2,1)}, bf16[64,1024]{1,0:T(8,128)(2,1)}, bf16[64,1024]{1,0:T(8,128)(2,1)}, f32[64,1024]{1,0:T(8,128)}, /*index=5*/f32[1,64]{1,0:T(1,128)}) custom-call(bf16[64,1024]{1,0:T(8,128)(2,1)S(1)} %copy-done, bf16[64,1024]{1,0:T(8,128)(2,1)S(1)} %copy-done.1, ...), custom_call_target="tpu_custom_call" | custom-call | tf_op jit(solution)/shard_map/pallas_call | solution.py:339
  24.6 0.0 collective-permute-done.3.refs_5_
  24.6 0.9 %collective-permute-done.4.refs_6_ = f32[192,128]{1,0:T(8,128)S(1)} collective-permute-done((f32[192,128]{1,0:T(8,128)S(1)}, f32[192,128]{1,0:T(8,128)S(1)}, u32[]{:S(2)}, u32[]{:S(2)}) %collective-permute-start.4) | collective-permute-done | bytes 98336 | tf_op jit(solution)/shard_map/ppermute | solution.py:279
  25.6 0.7 %shard_map.159 = (bf16[64,1024]{1,0:T(8,128)(2,1)}, bf16[64,1024]{1,0:T(8,128)(2,1)}, bf16[64,1024]{1,0:T(8,128)(2,1)}, bf16[64,1024]{1,0:T(8,128)(2,1)}, f32[64,1024]{1,0:T(8,128)}) custom-call(bf16[64,1024]{1,0:T(8,128)(2,1)S(1)} %copy-done, ...), custom_call_target="tpu_custom_call", output_to_operand_aliasing={{0}: (7, {}), {1}: (8, {}), {2}: (9, {}), {3}: (10, {}), {4... | custom-call | tf_op jit(solution)/shard_map/pallas_call | solution.py:339
Async XLA Ops:
  0.6 6.0 %copy-start = (bf16[64,1024]{1,0:T(8,128)(2,1)S(1)}, bf16[64,1024]{1,0:T(8,128)(2,1)}, u32[]{:S(2)}) copy-start(bf16[64,1024]{1,0:T(8,128)(2,1)} %refs_0_.9) | copy-start | bytes 393220
  0.6 6.0 %copy-start.1 = (bf16[64,1024]{1,0:T(8,128)(2,1)S(1)}, bf16[64,1024]{1,0:T(8,128)(2,1)}, u32[]{:S(2)}) copy-start(bf16[64,1024]{1,0:T(8,128)(2,1)} %refs_1_.9) | copy-start | bytes 393220
  0.7 6.0 %copy-start.2 = (bf16[64,1024]{1,0:T(8,128)(2,1)S(1)}, bf16[64,1024]{1,0:T(8,128)(2,1)}, u32[]{:S(2)}) copy-start(bf16[64,1024]{1,0:T(8,128)(2,1)} %refs_2_.9) | copy-start | bytes 393220
  0.7 5.9 %copy-start.3 = (bf16[64,1024]{1,0:T(8,128)(2,1)S(1)}, bf16[64,1024]{1,0:T(8,128)(2,1)}, u32[]{:S(2)}) copy-start(bf16[64,1024]{1,0:T(8,128)(2,1)} %refs_3_.9) | copy-start | bytes 393220
  0.7 5.9 %copy-start.5 = (f32[64,1024]{1,0:T(8,128)S(1)}, f32[64,1024]{1,0:T(8,128)}, u32[]{:S(2)}) copy-start(f32[64,1024]{1,0:T(8,128)} %refs_4_.5) | copy-start | bytes 786436
  1.9 8.4 %collective-permute-start.5 = (f32[192,128]{1,0:T(8,128)S(1)}, f32[192,128]{1,0:T(8,128)S(1)}, u32[]{:S(2)}, u32[]{:S(2)}) collective-permute-start(f32[192,128]{1,0:T(8,128)S(1)} %get-tuple-element.42), channel_id=1, source_target_pairs={{0,8},{8,0},{16,24},{24,16},{1,9},{9,1},{17,25},{25,17},{2,10},{10... | collective-permute-start | bytes 294920 | tf_op jit(solution)/shard_map/ppermute | solution.py:279
  5.0 1.7 %copy-start.10 = (f32[64]{0:T(128)S(1)}, f32[64]{0:T(128)}, u32[]{:S(2)}) copy-start(f32[64]{0:T(128)} %param.16) | copy-start | bytes 772
  5.0 6.3 %collective-permute-start.6 = (f32[192,128]{1,0:T(8,128)S(1)}, f32[192,128]{1,0:T(8,128)S(1)}, u32[]{:S(2)}, u32[]{:S(2)}) collective-permute-start(f32[192,128]{1,0:T(8,128)S(1)} %get-tuple-element.43), channel_id=1, source_target_pairs={{0,16},{8,24},{16,0},{24,8},{1,17},{9,25},{17,1},{25,9},{2,18},{10... | collective-permute-start | bytes 294920 | tf_op jit(solution)/shard_map/ppermute | solution.py:279
  6.5 6.5 %copy-start.4 = (bf16[256,512]{1,0:T(8,128)(2,1)S(1)}, bf16[256,512]{1,0:T(8,128)(2,1)}, u32[]{:S(2)}) copy-start(bf16[256,512]{1,0:T(8,128)(2,1)} %constant.14.clone.refs_4_) | copy-start | bytes 786436
  6.5 6.5 %copy-start.6 = (bf16[4,32,192]{2,1,0:T(8,128)(2,1)S(1)}, bf16[4,32,192]{2,1,0:T(8,128)(2,1)}, u32[]{:S(2)}) copy-start(bf16[4,32,192]{2,1,0:T(8,128)(2,1)} %constant.12.clone.refs_2_) | copy-start | bytes 147460
  6.5 6.5 %copy-start.7 = (bf16[4,32,192]{2,1,0:T(8,128)(2,1)S(1)}, bf16[4,32,192]{2,1,0:T(8,128)(2,1)}, u32[]{:S(2)}) copy-start(bf16[4,32,192]{2,1,0:T(8,128)(2,1)} %constant.11.clone.refs_1_) | copy-start | bytes 147460
  6.5 6.5 %copy-start.8 = (bf16[4,64,96]{2,1,0:T(8,128)(2,1)S(1)}, bf16[4,64,96]{2,1,0:T(8,128)(2,1)}, u32[]{:S(2)}) copy-start(bf16[4,64,96]{2,1,0:T(8,128)(2,1)} %constant.10.clone.refs_0_) | copy-start | bytes 147460
  6.5 6.5 %copy-start.9 = (f32[2,32,128]{2,1,0:T(8,128)S(1)}, f32[2,32,128]{2,1,0:T(8,128)}, u32[]{:S(2)}) copy-start(f32[2,32,128]{2,1,0:T(8,128)} %constant.13.clone.refs_3_) | copy-start | bytes 98308
  6.5 6.5 %collective-permute-start.7 = (f32[192,128]{1,0:T(8,128)S(1)}, f32[192,128]{1,0:T(8,128)S(1)}, u32[]{:S(2)}, u32[]{:S(2)}) collective-permute-start(f32[192,128]{1,0:T(8,128)S(1)} %get-tuple-element.44), channel_id=1, source_target_pairs={{0,24},{8,16},{16,8},{24,0},{1,25},{9,17},{17,9},{25,1},{2,26},{10... | collective-permute-start | bytes 294920 | tf_op jit(solution)/shard_map/ppermute | solution.py:279
  6.8 8.5 %collective-permute-start = (f32[200,128]{1,0:T(8,128)S(1)}, f32[200,128]{1,0:T(8,128)S(1)}, u32[]{:S(2)}, u32[]{:S(2)}) collective-permute-start(f32[200,128]{1,0:T(8,128)S(1)} %get-tuple-element.35), channel_id=1, source_target_pairs={{0,8},{8,0},{16,24},{24,16},{1,9},{9,1},{17,25},{25,17},{2,10},{10... | collective-permute-start | bytes 307208 | tf_op jit(solution)/shard_map/ppermute | solution.py:279
  8.8 9.0 %collective-permute-start.1 = (f32[200,128]{1,0:T(8,128)S(1)}, f32[200,128]{1,0:T(8,128)S(1)}, u32[]{:S(2)}, u32[]{:S(2)}) collective-permute-start(f32[200,128]{1,0:T(8,128)S(1)} %get-tuple-element.36), channel_id=1, source_target_pairs={{0,16},{8,24},{16,0},{24,8},{1,17},{9,25},{17,1},{25,9},{2,18},{10... | collective-permute-start | bytes 307208 | tf_op jit(solution)/shard_map/ppermute | solution.py:279
  10.3 7.5 %collective-permute-start.2 = (f32[200,128]{1,0:T(8,128)S(1)}, f32[200,128]{1,0:T(8,128)S(1)}, u32[]{:S(2)}, u32[]{:S(2)}) collective-permute-start(f32[200,128]{1,0:T(8,128)S(1)} %get-tuple-element.37), channel_id=1, source_target_pairs={{0,24},{8,16},{16,8},{24,0},{1,25},{9,17},{17,9},{25,1},{2,26},{10... | collective-permute-start | bytes 307208 | tf_op jit(solution)/shard_map/ppermute | solution.py:279
  14.2 5.8 %collective-permute-start.8 = (f32[192,128]{1,0:T(8,128)S(1)}, f32[192,128]{1,0:T(8,128)S(1)}, u32[]{:S(2)}, u32[]{:S(2)}) collective-permute-start(f32[192,128]{1,0:T(8,128)S(1)} %get-tuple-element.46), channel_id=1, source_target_pairs={{0,8},{8,0},{16,24},{24,16},{1,9},{9,1},{17,25},{25,17},{2,10},{10... | collective-permute-start | bytes 294920 | tf_op jit(solution)/shard_map/ppermute | solution.py:279
  15.1 7.5 %collective-permute-start.9 = (f32[192,128]{1,0:T(8,128)S(1)}, f32[192,128]{1,0:T(8,128)S(1)}, u32[]{:S(2)}, u32[]{:S(2)}) collective-permute-start(f32[192,128]{1,0:T(8,128)S(1)} %get-tuple-element.47), channel_id=1, source_target_pairs={{0,16},{8,24},{16,0},{24,8},{1,17},{9,25},{17,1},{25,9},{2,18},{10... | collective-permute-start | bytes 294920 | tf_op jit(solution)/shard_map/ppermute | solution.py:279
  15.3 7.3 %collective-permute-start.10 = (f32[192,128]{1,0:T(8,128)S(1)}, f32[192,128]{1,0:T(8,128)S(1)}, u32[]{:S(2)}, u32[]{:S(2)}) collective-permute-start(f32[192,128]{1,0:T(8,128)S(1)} %get-tuple-element.48), channel_id=1, source_target_pairs={{0,24},{8,16},{16,8},{24,0},{1,25},{9,17},{17,9},{25,1},{2,26},{10... | collective-permute-start | bytes 294920 | tf_op jit(solution)/shard_map/ppermute | solution.py:279
  19.0 4.7 %collective-permute-start.11 = (f32[192,128]{1,0:T(8,128)S(1)}, f32[192,128]{1,0:T(8,128)S(1)}, u32[]{:S(2)}, u32[]{:S(2)}) collective-permute-start(f32[192,128]{1,0:T(8,128)S(1)} %get-tuple-element.50), channel_id=1, source_target_pairs={{0,8},{8,0},{16,24},{24,16},{1,9},{9,1},{17,25},{25,17},{2,10},{10... | collective-permute-start | bytes 294920 | tf_op jit(solution)/shard_map/ppermute | solution.py:279
  19.8 4.8 %collective-permute-start.3 = (f32[192,128]{1,0:T(8,128)S(1)}, f32[192,128]{1,0:T(8,128)S(1)}, u32[]{:S(2)}, u32[]{:S(2)}) collective-permute-start(f32[192,128]{1,0:T(8,128)S(1)} %get-tuple-element.39), channel_id=1, source_target_pairs={{0,16},{8,24},{16,0},{24,8},{1,17},{9,25},{17,1},{25,9},{2,18},{10... | collective-permute-start | bytes 294920 | tf_op jit(solution)/shard_map/ppermute | solution.py:279
  20.1 5.5 %collective-permute-start.4 = (f32[192,128]{1,0:T(8,128)S(1)}, f32[192,128]{1,0:T(8,128)S(1)}, u32[]{:S(2)}, u32[]{:S(2)}) collective-permute-start(f32[192,128]{1,0:T(8,128)S(1)} %get-tuple-element.40), channel_id=1, source_target_pairs={{0,24},{8,16},{16,8},{24,0},{1,25},{9,17},{17,9},{25,1},{2,26},{10... | collective-permute-start | bytes 294920 | tf_op jit(solution)/shard_map/ppermute | solution.py:279

commit v8 on v7

--- a/solution.py
+++ b/solution.py
@@ -81,7 +81,7 @@
         ]
         for i, copy in enumerate(copies):
             copy.start(priority=i % 2)
-        for copy in copies:
+        for copy in copies[:4]:
             copy.wait()
         sources = held
     post, pre, signal, cotangent, taps, skip_gain = sources
@@ -89,11 +89,6 @@
     width = chunk_rows // shards_of
     per = length // LANES
     field_rows = width * per
-    turn = lax.broadcasted_iota(jnp.int32, (channels, channels), 0)
-    lane = lax.broadcasted_iota(jnp.int32, (channels, channels), 1)
-    gains = jnp.broadcast_to(skip_gain[...], (channels, channels))
-    gain = jnp.sum(jnp.where(turn == lane, gains, 0.0), axis=1, keepdims=True)
-    first = (lax.broadcasted_iota(jnp.int32, (16, LANES), 1) == 0) & (me == 0)
     parts = []
     for c in range(0 if last else q * chunk_rows, (q + 1) * chunk_rows, 16):
         rows = slice(c, c + 16)
@@ -101,13 +96,24 @@
         dc = cotangent[rows, :].astype(F32) * post[rows, :].astype(F32)
         if c >= q * chunk_rows:
             to = slice(c - q * chunk_rows, c - q * chunk_rows + 16)
-            fields[0, to, :] = taps[rows, :]
-            fields[0, to, :LANES] = taps[rows, :LANES] + jnp.where(first, gain[rows], 0.0)
             fields[1, to, :] = g
             fields[2, to, :] = dc
         if last:
             prod = g * dc
             parts.append(sum(prod[:, a * LANES : (a + 1) * LANES] for a in range(per)))
+    if q == 0:
+        for copy in copies[4:]:
+            copy.wait()
+    turn = lax.broadcasted_iota(jnp.int32, (channels, channels), 0)
+    lane = lax.broadcasted_iota(jnp.int32, (channels, channels), 1)
+    gains = jnp.broadcast_to(skip_gain[...], (channels, channels))
+    gain = jnp.sum(jnp.where(turn == lane, gains, 0.0), axis=1, keepdims=True)
+    first = (lax.broadcasted_iota(jnp.int32, (16, LANES), 1) == 0) & (me == 0)
+    for c in range(q * chunk_rows, (q + 1) * chunk_rows, 16):
+        rows = slice(c, c + 16)
+        to = slice(c - q * chunk_rows, c - q * chunk_rows + 16)
+        fields[0, to, :] = taps[rows, :]
+        fields[0, to, :LANES] = taps[rows, :LANES] + jnp.where(first, gain[rows], 0.0)
     for d in range(shards_of):
         for f in range(3):
             for c in range(0, width, SUBLANES):

time: 26.5 us -> 26.5 us (level)
  no operation moved by 1% of the time
where the time goes in v8:
time: 26.5 us; the launch traced here: 26.4 us
  starting transfers between devices  16.2 us (61%)
  Pallas kernels  5.58 us (21%)
  waiting for transfers between devices  3.78 us (14%)
  between operations  0.77 us (3%)
    ppermute x12, starting transfers between devices, swap(): lax.ppermute(pieces[d], 'seq', [(i, i ^ d) for i in range(shards_of)])  16.2 us
    ppermute x12, waiting for transfers between devices, swap(): lax.ppermute(pieces[d], 'seq', [(i, i ^ d) for i in range(shards_of)])  3.78 us
    pallas_call x2, Pallas kernels, shards(): pl.pallas_call(functools.partial(spectral_kernel, shards_of, chunks, last...  2.43 us
    pallas_call x2, Pallas kernels, shards(): pl.pallas_call(functools.partial(gate_kernel, shards_of, chunks, work, fi...  1.69 us
    pallas_call x2, Pallas kernels, shards(): pl.pallas_call(functools.partial(pack_kernel, shards_of, chunks, q), out_...  1.46 us
  transfers between devices with their start and end apart: 12, of which 3 were waited for; matrix products, arithmetic and copies ran while one was open for 0% of the time, Pallas kernels for 13%

profile of v8, /device:TPU:0, one launch (start us, length us, event | category | flops | bytes accessed | tf_op | source)
XLA Modules:
  0.0 26.4 jit_solution(15234110481683051080)
XLA Ops:
  0.6 0.0 copy-start
  0.6 0.0 copy-start.1
  0.7 0.0 copy-start.2
  0.7 0.0 copy-start.3
  0.7 0.0 copy-start.5
  0.7 1.3 %shard_map.156 = (f32[192,128]{1,0:T(8,128)S(1)}, f32[192,128]{1,0:T(8,128)S(1)}, f32[192,128]{1,0:T(8,128)S(1)}, f32[192,128]{1,0:T(8,128)S(1)}) custom-call(bf16[64,1024]{1,0:T(8,128)(2,1)} %refs_0_.9, bf16[64,1024]{1,0:T(8,128)(2,1)} %refs_1_.9, bf16[64,1024]{1,0:T(8,128)(2,1)} %refs_2_.9, bf16[64,1024]{1,0:T(8,128)(2,1)} %refs_3_.9, f32[64,1024]{1,0:T(8,128)} %refs_4_.5, ...), custom_call_target="tpu_custom_call" | custom-call | tf_op jit(solution)/shard_map/pallas_call | solution.py:302
  2.0 3.0 %collective-permute-start.5 = (f32[192,128]{1,0:T(8,128)S(1)}, f32[192,128]{1,0:T(8,128)S(1)}, u32[]{:S(2)}, u32[]{:S(2)}) collective-permute-start(f32[192,128]{1,0:T(8,128)S(1)} %get-tuple-element.42), channel_id=1, source_target_pairs={{0,8},{8,0},{16,24},{24,16},{1,9},{9,1},{17,25},{25,17},{2,10},{10... | collective-permute-start | bytes 294920 | tf_op jit(solution)/shard_map/ppermute | solution.py:285
  5.0 0.0 copy-start.10
  5.0 1.5 %collective-permute-start.6 = (f32[192,128]{1,0:T(8,128)S(1)}, f32[192,128]{1,0:T(8,128)S(1)}, u32[]{:S(2)}, u32[]{:S(2)}) collective-permute-start(f32[192,128]{1,0:T(8,128)S(1)} %get-tuple-element.43), channel_id=1, source_target_pairs={{0,16},{8,24},{16,0},{24,8},{1,17},{9,25},{17,1},{25,9},{2,18},{10... | collective-permute-start | bytes 294920 | tf_op jit(solution)/shard_map/ppermute | solution.py:285
  6.5 0.0 copy-start.4
  6.5 0.0 copy-start.6
  6.5 0.0 copy-start.7
  6.5 0.0 copy-start.8
  6.5 0.0 copy-start.9
  6.5 0.1 collective-permute-start.7
  6.6 0.0 copy-done
  6.6 0.0 copy-done.1
  6.6 0.0 copy-done.2
  6.6 0.0 copy-done.3
  6.6 0.0 copy-done.5
  6.7 0.0 copy-done.10
  6.7 0.2 shard_map.154
  6.8 2.0 %collective-permute-start = (f32[200,128]{1,0:T(8,128)S(1)}, f32[200,128]{1,0:T(8,128)S(1)}, u32[]{:S(2)}, u32[]{:S(2)}) collective-permute-start(f32[200,128]{1,0:T(8,128)S(1)} %get-tuple-element.35), channel_id=1, source_target_pairs={{0,8},{8,0},{16,24},{24,16},{1,9},{9,1},{17,25},{25,17},{2,10},{10... | collective-permute-start | bytes 307208 | tf_op jit(solution)/shard_map/ppermute | solution.py:285
  8.8 1.5 %collective-permute-start.1 = (f32[200,128]{1,0:T(8,128)S(1)}, f32[200,128]{1,0:T(8,128)S(1)}, u32[]{:S(2)}, u32[]{:S(2)}) collective-permute-start(f32[200,128]{1,0:T(8,128)S(1)} %get-tuple-element.36), channel_id=1, source_target_pairs={{0,16},{8,24},{16,0},{24,8},{1,17},{9,25},{17,1},{25,9},{2,18},{10... | collective-permute-start | bytes 307208 | tf_op jit(solution)/shard_map/ppermute | solution.py:285
  10.4 0.0 collective-permute-done.5.refs_6_
  10.4 0.9 %collective-permute-start.2 = (f32[200,128]{1,0:T(8,128)S(1)}, f32[200,128]{1,0:T(8,128)S(1)}, u32[]{:S(2)}, u32[]{:S(2)}) collective-permute-start(f32[200,128]{1,0:T(8,128)S(1)} %get-tuple-element.37), channel_id=1, source_target_pairs={{0,24},{8,16},{16,8},{24,0},{1,25},{9,17},{17,9},{25,1},{2,26},{10... | collective-permute-start | bytes 307208 | tf_op jit(solution)/shard_map/ppermute | solution.py:285
  11.3 0.0 collective-permute-done.6.refs_7_
  11.3 1.7 %collective-permute-done.7.refs_8_ = f32[192,128]{1,0:T(8,128)S(1)} collective-permute-done((f32[192,128]{1,0:T(8,128)S(1)}, f32[192,128]{1,0:T(8,128)S(1)}, u32[]{:S(2)}, u32[]{:S(2)}) %collective-permute-start.7) | collective-permute-done | bytes 98336 | tf_op jit(solution)/shard_map/ppermute | solution.py:285
  13.0 0.0 copy-done.4
  13.0 0.0 copy-done.6
  13.0 0.0 copy-done.7
  13.0 0.0 copy-done.8
  13.0 0.0 copy-done.9
  13.0 1.2 %shard_map.157 = (f32[192,128]{1,0:T(8,128)S(1)}, f32[192,128]{1,0:T(8,128)S(1)}, f32[192,128]{1,0:T(8,128)S(1)}, f32[192,128]{1,0:T(8,128)S(1)}) custom-call(bf16[4,64,96]{2,1,0:T(8,128)(2,1)S(1)} %copy-done.8, bf16[4,32,192]{2,1,0:T(8,128)(2,1)S(1)} %copy-done.7, bf16[4,32,192]{2,1,0:T(8,128)(2,1)S(1)} %copy-done.6, f32[2,32,128]{2,1,0:T(8,128)S(1)} %copy-done.9, ...), custom_call_target="tpu_custom_call" | custom-call | tf_op jit(solution)/shard_map/pallas_call | solution.py:316
  14.3 0.8 %collective-permute-start.8 = (f32[192,128]{1,0:T(8,128)S(1)}, f32[192,128]{1,0:T(8,128)S(1)}, u32[]{:S(2)}, u32[]{:S(2)}) collective-permute-start(f32[192,128]{1,0:T(8,128)S(1)} %get-tuple-element.46), channel_id=1, source_target_pairs={{0,8},{8,0},{16,24},{24,16},{1,9},{9,1},{17,25},{25,17},{2,10},{10... | collective-permute-start | bytes 294920 | tf_op jit(solution)/shard_map/ppermute | solution.py:285
  15.1 0.2 collective-permute-start.9
  15.3 0.0 collective-permute-done.refs_6_
  15.3 2.5 %collective-permute-start.10 = (f32[192,128]{1,0:T(8,128)S(1)}, f32[192,128]{1,0:T(8,128)S(1)}, u32[]{:S(2)}, u32[]{:S(2)}) collective-permute-start(f32[192,128]{1,0:T(8,128)S(1)} %get-tuple-element.48), channel_id=1, source_target_pairs={{0,24},{8,16},{16,8},{24,0},{1,25},{9,17},{17,9},{25,1},{2,26},{10... | collective-permute-start | bytes 294920 | tf_op jit(solution)/shard_map/ppermute | solution.py:285
  17.8 0.0 collective-permute-done.1.refs_7_
  17.8 0.0 collective-permute-done.2.refs_8_
  17.8 1.2 %shard_map.155 = (f32[192,128]{1,0:T(8,128)S(1)}, f32[192,128]{1,0:T(8,128)S(1)}, f32[192,128]{1,0:T(8,128)S(1)}, f32[192,128]{1,0:T(8,128)S(1)}, f32[1,64]{1,0:T(1,128)S(1)}) custom-call(bf16[4,64,96]{2,1,0:T(8,128)(2,1)S(1)} %copy-done.8, bf16[4,32,192]{2,1,0:T(8,128)(2,1)S(1)} %copy-done.7, bf16[4,32,192]{2,1,0:T(8,128)(2,1)S(1)} %copy-done.6, ...), custom_call_target="tpu_custom_call" | custom-call | tf_op jit(solution)/shard_map/pallas_call | solution.py:316
  19.0 0.8 %collective-permute-start.11 = (f32[192,128]{1,0:T(8,128)S(1)}, f32[192,128]{1,0:T(8,128)S(1)}, u32[]{:S(2)}, u32[]{:S(2)}) collective-permute-start(f32[192,128]{1,0:T(8,128)S(1)} %get-tuple-element.50), channel_id=1, source_target_pairs={{0,8},{8,0},{16,24},{24,16},{1,9},{9,1},{17,25},{25,17},{2,10},{10... | collective-permute-start | bytes 294920 | tf_op jit(solution)/shard_map/ppermute | solution.py:285
  19.9 0.2 collective-permute-start.3
  20.1 0.0 collective-permute-done.8.refs_6_
  20.1 2.5 %collective-permute-start.4 = (f32[192,128]{1,0:T(8,128)S(1)}, f32[192,128]{1,0:T(8,128)S(1)}, u32[]{:S(2)}, u32[]{:S(2)}) collective-permute-start(f32[192,128]{1,0:T(8,128)S(1)} %get-tuple-element.40), channel_id=1, source_target_pairs={{0,24},{8,16},{16,8},{24,0},{1,25},{9,17},{17,9},{25,1},{2,26},{10... | collective-permute-start | bytes 294920 | tf_op jit(solution)/shard_map/ppermute | solution.py:285
  22.6 0.0 collective-permute-done.9.refs_7_
  22.6 0.0 collective-permute-done.10.refs_8_
  22.6 1.1 %collective-permute-done.11.refs_10_ = f32[192,128]{1,0:T(8,128)S(1)} collective-permute-done((f32[192,128]{1,0:T(8,128)S(1)}, f32[192,128]{1,0:T(8,128)S(1)}, u32[]{:S(2)}, u32[]{:S(2)}) %collective-permute-start.11) | collective-permute-done | bytes 98336 | tf_op jit(solution)/shard_map/ppermute | solution.py:285
  23.7 0.9 %shard_map.158 = (bf16[64,1024]{1,0:T(8,128)(2,1)}, bf16[64,1024]{1,0:T(8,128)(2,1)}, bf16[64,1024]{1,0:T(8,128)(2,1)}, bf16[64,1024]{1,0:T(8,128)(2,1)}, f32[64,1024]{1,0:T(8,128)}, /*index=5*/f32[1,64]{1,0:T(1,128)}) custom-call(bf16[64,1024]{1,0:T(8,128)(2,1)S(1)} %copy-done, bf16[64,1024]{1,0:T(8,128)(2,1)S(1)} %copy-done.1, ...), custom_call_target="tpu_custom_call" | custom-call | tf_op jit(solution)/shard_map/pallas_call | solution.py:345
  24.7 0.0 collective-permute-done.3.refs_5_
  24.7 0.9 %collective-permute-done.4.refs_6_ = f32[192,128]{1,0:T(8,128)S(1)} collective-permute-done((f32[192,128]{1,0:T(8,128)S(1)}, f32[192,128]{1,0:T(8,128)S(1)}, u32[]{:S(2)}, u32[]{:S(2)}) %collective-permute-start.4) | collective-permute-done | bytes 98336 | tf_op jit(solution)/shard_map/ppermute | solution.py:285
  25.6 0.7 %shard_map.159 = (bf16[64,1024]{1,0:T(8,128)(2,1)}, bf16[64,1024]{1,0:T(8,128)(2,1)}, bf16[64,1024]{1,0:T(8,128)(2,1)}, bf16[64,1024]{1,0:T(8,128)(2,1)}, f32[64,1024]{1,0:T(8,128)}) custom-call(bf16[64,1024]{1,0:T(8,128)(2,1)S(1)} %copy-done, ...), custom_call_target="tpu_custom_call", output_to_operand_aliasing={{0}: (7, {}), {1}: (8, {}), {2}: (9, {}), {3}: (10, {}), {4... | custom-call | tf_op jit(solution)/shard_map/pallas_call | solution.py:345
Async XLA Ops:
  0.6 6.0 %copy-start = (bf16[64,1024]{1,0:T(8,128)(2,1)S(1)}, bf16[64,1024]{1,0:T(8,128)(2,1)}, u32[]{:S(2)}) copy-start(bf16[64,1024]{1,0:T(8,128)(2,1)} %refs_0_.9) | copy-start | bytes 393220
  0.6 6.0 %copy-start.1 = (bf16[64,1024]{1,0:T(8,128)(2,1)S(1)}, bf16[64,1024]{1,0:T(8,128)(2,1)}, u32[]{:S(2)}) copy-start(bf16[64,1024]{1,0:T(8,128)(2,1)} %refs_1_.9) | copy-start | bytes 393220
  0.7 6.0 %copy-start.2 = (bf16[64,1024]{1,0:T(8,128)(2,1)S(1)}, bf16[64,1024]{1,0:T(8,128)(2,1)}, u32[]{:S(2)}) copy-start(bf16[64,1024]{1,0:T(8,128)(2,1)} %refs_2_.9) | copy-start | bytes 393220
  0.7 6.0 %copy-start.3 = (bf16[64,1024]{1,0:T(8,128)(2,1)S(1)}, bf16[64,1024]{1,0:T(8,128)(2,1)}, u32[]{:S(2)}) copy-start(bf16[64,1024]{1,0:T(8,128)(2,1)} %refs_3_.9) | copy-start | bytes 393220
  0.7 6.0 %copy-start.5 = (f32[64,1024]{1,0:T(8,128)S(1)}, f32[64,1024]{1,0:T(8,128)}, u32[]{:S(2)}) copy-start(f32[64,1024]{1,0:T(8,128)} %refs_4_.5) | copy-start | bytes 786436
  2.0 8.4 %collective-permute-start.5 = (f32[192,128]{1,0:T(8,128)S(1)}, f32[192,128]{1,0:T(8,128)S(1)}, u32[]{:S(2)}, u32[]{:S(2)}) collective-permute-start(f32[192,128]{1,0:T(8,128)S(1)} %get-tuple-element.42), channel_id=1, source_target_pairs={{0,8},{8,0},{16,24},{24,16},{1,9},{9,1},{17,25},{25,17},{2,10},{10... | collective-permute-start | bytes 294920 | tf_op jit(solution)/shard_map/ppermute | solution.py:285
  5.0 1.7 %copy-start.10 = (f32[64]{0:T(128)S(1)}, f32[64]{0:T(128)}, u32[]{:S(2)}) copy-start(f32[64]{0:T(128)} %param.16) | copy-start | bytes 772
  5.0 6.3 %collective-permute-start.6 = (f32[192,128]{1,0:T(8,128)S(1)}, f32[192,128]{1,0:T(8,128)S(1)}, u32[]{:S(2)}, u32[]{:S(2)}) collective-permute-start(f32[192,128]{1,0:T(8,128)S(1)} %get-tuple-element.43), channel_id=1, source_target_pairs={{0,16},{8,24},{16,0},{24,8},{1,17},{9,25},{17,1},{25,9},{2,18},{10... | collective-permute-start | bytes 294920 | tf_op jit(solution)/shard_map/ppermute | solution.py:285
  6.5 6.5 %copy-start.4 = (bf16[256,512]{1,0:T(8,128)(2,1)S(1)}, bf16[256,512]{1,0:T(8,128)(2,1)}, u32[]{:S(2)}) copy-start(bf16[256,512]{1,0:T(8,128)(2,1)} %constant.14.clone.refs_4_) | copy-start | bytes 786436
  6.5 6.5 %copy-start.6 = (bf16[4,32,192]{2,1,0:T(8,128)(2,1)S(1)}, bf16[4,32,192]{2,1,0:T(8,128)(2,1)}, u32[]{:S(2)}) copy-start(bf16[4,32,192]{2,1,0:T(8,128)(2,1)} %constant.12.clone.refs_2_) | copy-start | bytes 147460
  6.5 6.5 %copy-start.7 = (bf16[4,32,192]{2,1,0:T(8,128)(2,1)S(1)}, bf16[4,32,192]{2,1,0:T(8,128)(2,1)}, u32[]{:S(2)}) copy-start(bf16[4,32,192]{2,1,0:T(8,128)(2,1)} %constant.11.clone.refs_1_) | copy-start | bytes 147460
  6.5 6.5 %copy-start.8 = (bf16[4,64,96]{2,1,0:T(8,128)(2,1)S(1)}, bf16[4,64,96]{2,1,0:T(8,128)(2,1)}, u32[]{:S(2)}) copy-start(bf16[4,64,96]{2,1,0:T(8,128)(2,1)} %constant.10.clone.refs_0_) | copy-start | bytes 147460
  6.5 6.5 %copy-start.9 = (f32[2,32,128]{2,1,0:T(8,128)S(1)}, f32[2,32,128]{2,1,0:T(8,128)}, u32[]{:S(2)}) copy-start(f32[2,32,128]{2,1,0:T(8,128)} %constant.13.clone.refs_3_) | copy-start | bytes 98308
  6.5 6.5 %collective-permute-start.7 = (f32[192,128]{1,0:T(8,128)S(1)}, f32[192,128]{1,0:T(8,128)S(1)}, u32[]{:S(2)}, u32[]{:S(2)}) collective-permute-start(f32[192,128]{1,0:T(8,128)S(1)} %get-tuple-element.44), channel_id=1, source_target_pairs={{0,24},{8,16},{16,8},{24,0},{1,25},{9,17},{17,9},{25,1},{2,26},{10... | collective-permute-start | bytes 294920 | tf_op jit(solution)/shard_map/ppermute | solution.py:285
  6.8 8.5 %collective-permute-start = (f32[200,128]{1,0:T(8,128)S(1)}, f32[200,128]{1,0:T(8,128)S(1)}, u32[]{:S(2)}, u32[]{:S(2)}) collective-permute-start(f32[200,128]{1,0:T(8,128)S(1)} %get-tuple-element.35), channel_id=1, source_target_pairs={{0,8},{8,0},{16,24},{24,16},{1,9},{9,1},{17,25},{25,17},{2,10},{10... | collective-permute-start | bytes 307208 | tf_op jit(solution)/shard_map/ppermute | solution.py:285
  8.8 9.0 %collective-permute-start.1 = (f32[200,128]{1,0:T(8,128)S(1)}, f32[200,128]{1,0:T(8,128)S(1)}, u32[]{:S(2)}, u32[]{:S(2)}) collective-permute-start(f32[200,128]{1,0:T(8,128)S(1)} %get-tuple-element.36), channel_id=1, source_target_pairs={{0,16},{8,24},{16,0},{24,8},{1,17},{9,25},{17,1},{25,9},{2,18},{10... | collective-permute-start | bytes 307208 | tf_op jit(solution)/shard_map/ppermute | solution.py:285
  10.4 7.5 %collective-permute-start.2 = (f32[200,128]{1,0:T(8,128)S(1)}, f32[200,128]{1,0:T(8,128)S(1)}, u32[]{:S(2)}, u32[]{:S(2)}) collective-permute-start(f32[200,128]{1,0:T(8,128)S(1)} %get-tuple-element.37), channel_id=1, source_target_pairs={{0,24},{8,16},{16,8},{24,0},{1,25},{9,17},{17,9},{25,1},{2,26},{10... | collective-permute-start | bytes 307208 | tf_op jit(solution)/shard_map/ppermute | solution.py:285
  14.3 5.8 %collective-permute-start.8 = (f32[192,128]{1,0:T(8,128)S(1)}, f32[192,128]{1,0:T(8,128)S(1)}, u32[]{:S(2)}, u32[]{:S(2)}) collective-permute-start(f32[192,128]{1,0:T(8,128)S(1)} %get-tuple-element.46), channel_id=1, source_target_pairs={{0,8},{8,0},{16,24},{24,16},{1,9},{9,1},{17,25},{25,17},{2,10},{10... | collective-permute-start | bytes 294920 | tf_op jit(solution)/shard_map/ppermute | solution.py:285
  15.1 7.5 %collective-permute-start.9 = (f32[192,128]{1,0:T(8,128)S(1)}, f32[192,128]{1,0:T(8,128)S(1)}, u32[]{:S(2)}, u32[]{:S(2)}) collective-permute-start(f32[192,128]{1,0:T(8,128)S(1)} %get-tuple-element.47), channel_id=1, source_target_pairs={{0,16},{8,24},{16,0},{24,8},{1,17},{9,25},{17,1},{25,9},{2,18},{10... | collective-permute-start | bytes 294920 | tf_op jit(solution)/shard_map/ppermute | solution.py:285
  15.3 7.3 %collective-permute-start.10 = (f32[192,128]{1,0:T(8,128)S(1)}, f32[192,128]{1,0:T(8,128)S(1)}, u32[]{:S(2)}, u32[]{:S(2)}) collective-permute-start(f32[192,128]{1,0:T(8,128)S(1)} %get-tuple-element.48), channel_id=1, source_target_pairs={{0,24},{8,16},{16,8},{24,0},{1,25},{9,17},{17,9},{25,1},{2,26},{10... | collective-permute-start | bytes 294920 | tf_op jit(solution)/shard_map/ppermute | solution.py:285
  19.0 4.7 %collective-permute-start.11 = (f32[192,128]{1,0:T(8,128)S(1)}, f32[192,128]{1,0:T(8,128)S(1)}, u32[]{:S(2)}, u32[]{:S(2)}) collective-permute-start(f32[192,128]{1,0:T(8,128)S(1)} %get-tuple-element.50), channel_id=1, source_target_pairs={{0,8},{8,0},{16,24},{24,16},{1,9},{9,1},{17,25},{25,17},{2,10},{10... | collective-permute-start | bytes 294920 | tf_op jit(solution)/shard_map/ppermute | solution.py:285
  19.9 4.8 %collective-permute-start.3 = (f32[192,128]{1,0:T(8,128)S(1)}, f32[192,128]{1,0:T(8,128)S(1)}, u32[]{:S(2)}, u32[]{:S(2)}) collective-permute-start(f32[192,128]{1,0:T(8,128)S(1)} %get-tuple-element.39), channel_id=1, source_target_pairs={{0,16},{8,24},{16,0},{24,8},{1,17},{9,25},{17,1},{25,9},{2,18},{10... | collective-permute-start | bytes 294920 | tf_op jit(solution)/shard_map/ppermute | solution.py:285
  20.1 5.5 %collective-permute-start.4 = (f32[192,128]{1,0:T(8,128)S(1)}, f32[192,128]{1,0:T(8,128)S(1)}, u32[]{:S(2)}, u32[]{:S(2)}) collective-permute-start(f32[192,128]{1,0:T(8,128)S(1)} %get-tuple-element.40), channel_id=1, source_target_pairs={{0,24},{8,16},{16,8},{24,0},{1,25},{9,17},{17,9},{25,1},{2,26},{10... | collective-permute-start | bytes 294920 | tf_op jit(solution)/shard_map/ppermute | solution.py:285
